TPU v7x, 32 devices: a whole 2x2x4 slice. The times are simulated.
32 devices in a mesh: ty: 2 (over y), tx: 16 (over z, x, core).
Axes of the slice: x: 2, y: 2, z: 4, core: 2. Of those that a mesh axis runs over, the one named last changes fastest.
Arguments:
- tracer_start: float32 [48, 32, 2048], P(None, 'ty', 'tx'), may hold values from -6 to 6
- observed: bfloat16 [48, 32, 2048], P(None, 'ty', 'tx'), may hold values from -6 to 6
- east_speed: bfloat16 [48, 32, 2048], P(None, 'ty', 'tx'), may hold values from -4 to 4
- north_speed: bfloat16 [48, 32, 2048], P(None, 'ty', 'tx'), may hold values from -4 to 4
- mixing: bfloat16 [48, 32, 2048], P(None, 'ty', 'tx'), may hold values from 0.019897461 to 0.19921875
- vertical_mixing: bfloat16 [47, 32, 2048], P(None, 'ty', 'tx'), may hold values from 0.19921875 to 5
- relax_rate: bfloat16 [48, 32, 2048], P(None, 'ty', 'tx'), may hold values from 0.049804688 to 0.5
- level_count: int32 [32, 2048], P('ty', 'tx'), may hold values from 0 to 48, as said below
- face_east: int32 [32, 2048], P('ty', 'tx'), may hold values from 0 to 48, as said below
- face_north: int32 [32, 2048], P('ty', 'tx'), may hold values from 0 to 48, as said below
Outputs:
- adjoint_start: float32 [48, 32, 2048], P(None, 'ty', 'tx')
- mixing_gradient: float32 [48, 32, 2048], P(None, 'ty', 'tx')
Inputs may be any that keep to these rules, and one draw needn't show every extreme that they name: Levels 0 to level_count - 1 of a column are water; 0 marks land. `face_east`: the smaller of the level counts of a column and of the next column east, the last column's next being the first. `face_north`: the smaller of the level counts of a column and of the next row's column north, the last row's next being the first.
All inputs are finite; a program needn't handle non-finite values.
Results may differ from a plain program's by a relative error of at most 0.0006.
Values sent between devices are 32-bit elements; how exact they have to be, the bound alone decides.
No kernel may reach another device: no remote copies, remote signals or barrier semaphores. Data moves between devices by JAX's collectives and lax.ppermute only.
A program may use at most 64 MiB of HBM per device.

v0:
```python
import jax
import jax.numpy as jnp
from jax import lax
from jax.sharding import PartitionSpec as P


def shifted(block, axis, distance):
    devices = range(lax.axis_size(axis))
    route = [((i - distance) % len(devices), i) for i in devices]
    return lax.ppermute(block, axis, route)


def padded(block, sides, width):
    for axis, dim in sides:
        count = lax.axis_size(axis)
        forward = [(i, i + 1) for i in range(count - 1)]
        forward.append((count - 1, 0))
        backward = [(target, source) for source, target in forward]
        low = lax.ppermute(
            lax.slice_in_dim(block, block.shape[dim] - width, None, axis=dim), axis, forward
        )
        high = lax.ppermute(lax.slice_in_dim(block, 0, width, axis=dim), axis, backward)
        block = jnp.concatenate([low, block, high], axis=dim)
    return block


def solve_columns(rhs, level_links):
    levels = rhs.shape[0]
    nothing = jnp.zeros_like(rhs[0])
    ratios = []
    carries = []
    last_ratio = nothing
    last_carry = nothing
    for height in range(levels):
        upper_link = level_links[height - 1] if height > 0 else nothing
        lower_link = level_links[height] if height < levels - 1 else nothing
        divisor = 1.0 + upper_link + lower_link - upper_link * last_ratio
        last_carry = (rhs[height] + upper_link * last_carry) / divisor
        last_ratio = lower_link / divisor
        ratios.append(last_ratio)
        carries.append(last_carry)
    result = [carries[-1]]
    for height in range(levels - 2, -1, -1):
        result.append(carries[height] + ratios[height] * result[-1])
    return jnp.stack(result[::-1], axis=0)


def mask_levels(level_total, counts):
    heights = lax.broadcasted_iota(jnp.int32, (level_total,) + counts.shape, 0)
    return (heights < counts[None]).astype(jnp.float32)


def advance(extended, face_terms, level_links, sink_rate):
    east_minus, east_plus, north_minus, north_plus = face_terms
    flux_x = east_plus[:, :, :-1] * extended[:, :, :-1] + east_minus[:, :, :-1] * extended[:, :, 1:]
    flux_y = (
        north_plus[:, :-1, :] * extended[:, :-1, :] + north_minus[:, :-1, :] * extended[:, 1:, :]
    )
    centre = extended[:, 1:-1, 1:-1]
    spread = (
        flux_x[:, 1:-1, 1:] - flux_x[:, 1:-1, :-1] + (flux_y[:, 1:, 1:-1] - flux_y[:, :-1, 1:-1])
    )
    source = centre - spread - sink_rate * jnp.tanh(centre)
    return solve_columns(source, level_links)


def cycle_view(extended):
    return (extended[:, 1:-1, 1:-1], extended[:, 1:-1, 2:], extended[:, 2:, 1:-1])


def lower_rims(east_minus, east_plus, north_minus, north_plus):
    pair_east = jnp.stack([east_minus, east_plus])
    west_col = shifted(pair_east[:, :, :, -1:], "tx", 1)
    east_ext = jnp.pad(jnp.concatenate([west_col, pair_east], 3), ((0, 0), (0, 0), (1, 1), (0, 1)))
    pair_north = jnp.stack([north_minus, north_plus])
    south_row = shifted(pair_north[:, :, -1:, :], "ty", 1)
    north_ext = jnp.pad(
        jnp.concatenate([south_row, pair_north], 2), ((0, 0), (0, 0), (0, 1), (1, 1))
    )
    return (east_ext[0], east_ext[1], north_ext[0], north_ext[1])


def per_device(
    tracer_start,
    observed,
    east_speed,
    north_speed,
    mixing,
    vertical_mixing,
    relax_rate,
    level_count,
    face_east,
    face_north,
):
    levels = tracer_start.shape[0]
    water = mask_levels(levels, level_count)
    open_east = mask_levels(levels, face_east)
    open_north = mask_levels(levels, face_north)
    diffusion = mixing.astype(jnp.float32)
    speed_east = east_speed.astype(jnp.float32)
    speed_north = north_speed.astype(jnp.float32)
    east_minus = open_east * (0.5 * speed_east - diffusion)
    east_plus = open_east * (0.5 * speed_east + diffusion)
    north_minus = open_north * (0.5 * speed_north - diffusion)
    north_plus = open_north * (0.5 * speed_north + diffusion)
    level_links = vertical_mixing.astype(jnp.float32) * water[:-1] * water[1:]
    sink_rate = water * relax_rate.astype(jnp.float32)
    inner_terms = None
    states = []
    current = tracer_start
    inner_terms = lower_rims(east_minus, east_plus, north_minus, north_plus)
    for position in range(2):
        extended = padded(current, (("ty", 1), ("tx", 2)), 1)
        states.append(cycle_view(extended))
        current = advance(extended, inner_terms, level_links, sink_rate)
    adjoint = water * (current - observed.astype(jnp.float32))
    gradient = jnp.zeros_like(adjoint)
    for position in (1, 0):
        centre, right_state, above_state = states[position]
        solved = solve_columns(adjoint, level_links)
        squeeze = jnp.tanh(centre)
        solved_ext = padded(solved, (("ty", 1), ("tx", 2)), 1)
        east_m, east_p, north_m, north_p = inner_terms
        full_x = solved_ext[:, :, 1:] - solved_ext[:, :, :-1]
        full_y = solved_ext[:, 1:, :] - solved_ext[:, :-1, :]
        grad_x = full_x[:, 1:-1, 1:]
        grad_y = full_y[:, 1:, 1:-1]
        from_x = east_p[:, 1:-1, 1:-1] * grad_x + east_m[:, 1:-1, :-2] * full_x[:, 1:-1, :-1]
        from_y = north_p[:, 1:-1, 1:-1] * grad_y + north_m[:, :-2, 1:-1] * full_y[:, :-1, 1:-1]
        adjoint = solved * (1.0 - sink_rate * (1.0 - squeeze * squeeze)) + from_x + from_y
        kappa_part = -(
            open_east * grad_x * (right_state - centre)
            + open_north * grad_y * (above_state - centre)
        )
        gradient = gradient + kappa_part
    return (adjoint, gradient)


def solution(mesh):
    placed = (
        P(None, "ty", "tx"),
        P(None, "ty", "tx"),
        P(None, "ty", "tx"),
        P(None, "ty", "tx"),
        P(None, "ty", "tx"),
        P(None, "ty", "tx"),
        P(None, "ty", "tx"),
        P("ty", "tx"),
        P("ty", "tx"),
        P("ty", "tx"),
    )
    return jax.shard_map(
        per_device,
        mesh=mesh,
        in_specs=placed,
        out_specs=(P(None, "ty", "tx"), P(None, "ty", "tx")),
        check_vma=False,
    )
```

profile of v0, /device:TPU:0, one launch (start us, length us, event | category | flops | bytes accessed | tf_op | source)
XLA Modules:
  0.0 135.9 jit_solution(16668520410638977114)
XLA Ops:
  0.6 1.1 fusion.609
  1.7 3.0 %collective-permute-start.1 = (f32[48,1,128]{2,1,0:T(1,128)S(1)}, f32[48,1,128]{2,1,0:T(1,128)S(1)}, u32[]{:S(2)}, u32[]{:S(2)}) collective-permute-start(f32[48,1,128]{2,1,0:T(1,128)S(1)} %get-tuple-element.424), channel_id=1, source_target_pairs={{0,16},{16,0},{1,17},{17,1},{2,18},{18,2},{3,19},{19,3},{4,20},{20... | collective-permute-start | bytes 73736 | tf_op jit(solution)/shard_map/ppermute | solution.py:19
  4.8 1.3 fusion.18
  6.1 0.7 pad_maximum_fusion.23
  6.9 1.9 %collective-permute-start.5 = (f32[2,48,1,128]{3,2,1,0:T(1,128)}, f32[2,48,1,128]{3,2,1,0:T(1,128)}, u32[]{:S(2)}, u32[]{:S(2)}) collective-permute-start(f32[2,48,1,128]{3,2,1,0:T(1,128)} %pad_maximum_fusion.23), channel_id=1, source_target_pairs={{16,0},{0,16},{17,1},{1,17},{18,2},{2,18},{19,3},{3,19},{20,4},{4,... | collective-permute-start | bytes 147464 | tf_op jit(solution)/shard_map/ppermute | solution.py:10
  10.5 4.8 %collective-permute-done = f32[2,48,16,1]{1,2,3,0:T(8,128)S(1)} collective-permute-done((f32[2,48,16,1]{1,2,3,0:T(8,128)S(1)}, f32[2,48,16,1]{1,2,3,0:T(8,128)S(1)}, u32[]{:S(2)}, u32[]{:S(2)}) %collective-permute-start) | collective-permute-done | bytes 6176 | tf_op jit(solution)/shard_map/ppermute | solution.py:10
  15.8 2.3 %select_maximum_fusion = f32[2,48,18,130]{3,2,1,0:T(8,128)} fusion(f32[2,48,16,1]{3,2,1,0:T(8,128)S(1)} %copy.190, f32[1,48,16,128]{3,2,1,0:T(8,128)S(1)} %get-tuple-element.415, f32[1,48,16,128]{3,2,1,0:T(8,128)S(1)} %get-tuple-element.414), kind=kLoop, calls=%fused_computation.13 | loop fusion | flops 2920320 | bytes 1691136 | tf_op jit(solution)/shard_map/concatenate | solution.py:74
  19.6 0.8 copy.191
  20.4 0.8 copy.193
  21.7 1.8 %slice_bitcast_fusion.3 = (f32[48,18,130]{2,1,0:T(8,128)S(1)}, f32[48,18,130]{2,1,0:T(8,128)S(1)}) fusion(f32[2,48,18,130]{3,2,1,0:T(8,128)} %select_maximum_fusion), kind=kLoop, calls=%fused_computation.30 | loop fusion | bytes 1797120 | tf_op jit(solution)/shard_map/squeeze | solution.py:80
  23.5 3.8 %collective-permute-done.3 = f32[48,18,1]{0,2,1:T(1,128)} collective-permute-done((f32[48,18,1]{0,2,1:T(1,128)}, f32[48,18,1]{0,2,1:T(1,128)}, u32[]{:S(2)}, u32[]{:S(2)}) %collective-permute-start.3) | collective-permute-done | bytes 3488 | tf_op jit(solution)/shard_map/ppermute | solution.py:19
  27.3 1.8 %copy.192 = f32[48,18,1]{2,1,0:T(8,128)} copy(f32[48,18,1]{0,2,1:T(1,128)} %collective-permute-done.3) | data formatting | bytes 6912 | tf_op jit(solution)/shard_map/ppermute | solution.py:19
  29.1 1.8 %copy.194 = f32[48,18,1]{2,1,0:T(8,128)} copy(f32[48,18,1]{0,2,1:T(1,128)} %collective-permute-done.4) | data formatting | bytes 6912 | tf_op jit(solution)/shard_map/ppermute | solution.py:22
  30.9 3.0 %pad_maximum_fusion = (f32[48,18,129]{2,1,0:T(8,128)}, f32[48,18,129]{2,1,0:T(8,128)S(1)}) fusion(f32[48,18,1]{2,1,0:T(8,128)} %copy.194, f32[48,1,128]{2,1,0:T(1,128)} %copy-done.87, f32[48,16,128]{2,1,0:T(8,128)S(1)} %copy-done.4, f32[48,1,128]{2,1,0:T(1,128)} %copy-done.106, f32[48,18,130]{2,1,0:T(8,128)S(1)} %get-tuple-element.399, ...), kind=kLoop, calls=%fused_computation.33 | loop fusion | flops 1003104 | bytes 2232576 | tf_op jit(solution)/shard_map/concatenate | solution.py:23
  34.9 1.7 %fusion.6 = f32[2,48,18,130]{3,2,1,0:T(8,128)S(1)} fusion(f32[2,48,1,128]{3,2,1,0:T(1,128)} %collective-permute-done.5, f32[1,48,16,128]{3,2,1,0:T(8,128)S(1)} %get-tuple-element.426, f32[1,48,16,128]{3,2,1,0:T(8,128)S(1)} %copy-done.22), kind=kLoop, calls=%fused_computation.8 | loop fusion | flops 2920320 | bytes 1734144 | tf_op jit(solution)/shard_map/concatenate | solution.py:78
  37.1 0.7 copy-done
  38.8 1.1 fusion.425
  40.0 1.0 add_divide_fusion.133
  41.4 0.9 constant_dynamic-update-slice_fusion.47
  44.0 1.9 %collective-permute-start.7 = (f32[48,1,128]{2,1,0:T(1,128)S(1)}, f32[48,1,128]{2,1,0:T(1,128)S(1)}, u32[]{:S(2)}, u32[]{:S(2)}) collective-permute-start(f32[48,1,128]{2,1,0:T(1,128)S(1)} %get-tuple-element.423), channel_id=1, source_target_pairs={{16,0},{0,16},{17,1},{1,17},{18,2},{2,18},{19,3},{3,19},{20,4},{4,... | collective-permute-start | bytes 73736 | tf_op jit(solution)/shard_map/ppermute | solution.py:22
  45.9 1.8 %collective-permute-done.6 = f32[48,1,128]{2,1,0:T(1,128)S(1)} collective-permute-done((f32[48,1,128]{2,1,0:T(1,128)S(1)}, f32[48,1,128]{2,1,0:T(1,128)S(1)}, u32[]{:S(2)}, u32[]{:S(2)}) %collective-permute-start.6) | collective-permute-done | bytes 24608 | tf_op jit(solution)/shard_map/ppermute | solution.py:19
  49.0 1.3 fusion.604
  50.3 1.9 %copy.197 = f32[48,18,1]{0,2,1:T(1,128)} copy(f32[48,18,1]{2,1,0:T(8,128)} %get-tuple-element.410) | data formatting | bytes 6912 | tf_op jit(solution)/shard_map/slice | solution.py:20
  52.1 1.9 %copy.199 = f32[48,18,1]{0,2,1:T(1,128)} copy(f32[48,18,1]{2,1,0:T(8,128)} %get-tuple-element.411) | data formatting | bytes 6912 | tf_op jit(solution)/shard_map/slice | solution.py:22
  54.0 4.4 %collective-permute-start.9 = (f32[48,18,1]{0,2,1:T(1,128)}, f32[48,18,1]{0,2,1:T(1,128)}, u32[]{:S(2)}, u32[]{:S(2)}) collective-permute-start(f32[48,18,1]{0,2,1:T(1,128)} %copy.199), channel_id=1, source_target_pairs={{1,0},{2,1},{3,2},{4,3},{5,4},{6,5},{7,6},{8,7},{9,8},{10,9},{11,1... | collective-permute-start | bytes 10376 | tf_op jit(solution)/shard_map/ppermute | solution.py:22
  58.4 1.8 %copy.198 = f32[48,18,1]{2,1,0:T(8,128)} copy(f32[48,18,1]{0,2,1:T(1,128)} %collective-permute-done.8) | data formatting | bytes 6912 | tf_op jit(solution)/shard_map/ppermute | solution.py:19
  60.3 1.8 %copy.200 = f32[48,18,1]{2,1,0:T(8,128)} copy(f32[48,18,1]{0,2,1:T(1,128)} %collective-permute-done.9) | data formatting | bytes 6912 | tf_op jit(solution)/shard_map/ppermute | solution.py:22
  62.1 2.2 %pad_maximum_fusion.3 = f32[48,18,130]{2,1,0:T(8,128)S(1)} fusion(f32[48,18,1]{2,1,0:T(8,128)} %copy.200, f32[48,1,128]{2,1,0:T(1,128)} %copy-done.90, f32[48,16,128]{2,1,0:T(8,128)S(1)} %constant_dynamic-update-slice_fusion, f32[48,1,128]{2,1,0:T(1,128)} %copy-done.108, f32[48,18,1]{2,1,0:T(8,128)} %copy.198), kind=kLoop, calls=%fused_computation.38 | loop fusion | flops 449280 | bytes 898560 | tf_op jit(solution)/shard_map/concatenate | solution.py:23
  64.6 0.8 copy-done.16
  65.6 1.7 %pad_maximum_fusion.2 = (f32[48,18,129]{2,1,0:T(8,128)}, f32[48,18,129]{2,1,0:T(8,128)S(1)}) fusion(f32[48,18,1]{2,1,0:T(8,128)S(1)} %copy-done.18, f32[48,1,128]{2,1,0:T(1,128)S(1)} %copy-done.91, f32[48,16,128]{2,1,0:T(8,128)S(1)} %constant_dynamic-update-slice_fusion, f32[48,1,128]{2,1,0:T(1,128)S(1)} %copy-done.109, ...), kind=kLoop, calls=%fused_computation.37 | loop fusion | flops 1003104 | bytes 2232576 | tf_op jit(solution)/shard_map/concatenate | solution.py:23
  68.1 1.4 %add_divide_fusion.92 = (f32[1,16,128]{2,1,0:T(8,128)S(1)}, f32[1,16,128]{2,1,0:T(8,128)S(1)}, f32[1,16,128]{2,1,0:T(8,128)S(1)}, f32[1,16,128]{2,1,0:T(8,128)S(...) fusion(f32[1,16,128]{2,1,0:T(8,128)S(1)} %copy-done.153, ...), kind=kLoop, calls=%fused_computation.1269 | loop fusion | flops 249856 | bytes 1318912 | tf_op jit(solution)/shard_map/div | solution.py:38
  69.9 1.0 constant_dynamic-update-slice_fusion.95
  71.5 1.2 fusion.323
  73.0 0.8 constant_dynamic-update-slice_fusion.52
  74.0 1.2 fusion.224
  76.2 0.9 constant_dynamic-update-slice_fusion.143
  77.8 1.5 %collective-permute-start.10 = (f32[48,1,128]{2,1,0:T(1,128)S(1)}, f32[48,1,128]{2,1,0:T(1,128)S(1)}, u32[]{:S(2)}, u32[]{:S(2)}) collective-permute-start(f32[48,1,128]{2,1,0:T(1,128)S(1)} %get-tuple-element.420), channel_id=1, source_target_pairs={{0,16},{16,0},{1,17},{17,1},{2,18},{18,2},{3,19},{19,3},{4,20},{20... | collective-permute-start | bytes 73736 | tf_op jit(solution)/shard_map/ppermute | solution.py:19
  79.8 1.8 %collective-permute-done.10 = f32[48,1,128]{2,1,0:T(1,128)S(1)} collective-permute-done((f32[48,1,128]{2,1,0:T(1,128)S(1)}, f32[48,1,128]{2,1,0:T(1,128)S(1)}, u32[]{:S(2)}, u32[]{:S(2)}) %collective-permute-start.10) | collective-permute-done | bytes 24608 | tf_op jit(solution)/shard_map/ppermute | solution.py:19
  81.7 1.4 %collective-permute-done.11 = f32[48,1,128]{2,1,0:T(1,128)S(1)} collective-permute-done((f32[48,1,128]{2,1,0:T(1,128)S(1)}, f32[48,1,128]{2,1,0:T(1,128)S(1)}, u32[]{:S(2)}, u32[]{:S(2)}) %collective-permute-start.11) | collective-permute-done | bytes 24608 | tf_op jit(solution)/shard_map/ppermute | solution.py:22
  83.8 1.2 fusion.603
  84.9 1.9 %copy.205 = f32[48,18,1]{0,2,1:T(1,128)} copy(f32[48,18,1]{2,1,0:T(8,128)} %get-tuple-element.408) | data formatting | bytes 6912 | tf_op jit(solution)/shard_map/slice | solution.py:20
  86.8 1.9 %copy.203 = f32[48,18,1]{0,2,1:T(1,128)} copy(f32[48,18,1]{2,1,0:T(8,128)} %get-tuple-element.409) | data formatting | bytes 6912 | tf_op jit(solution)/shard_map/slice | solution.py:22
  88.7 4.4 %collective-permute-start.12 = (f32[48,18,1]{0,2,1:T(1,128)}, f32[48,18,1]{0,2,1:T(1,128)}, u32[]{:S(2)}, u32[]{:S(2)}) collective-permute-start(f32[48,18,1]{0,2,1:T(1,128)} %copy.203), channel_id=1, source_target_pairs={{1,0},{2,1},{3,2},{4,3},{5,4},{6,5},{7,6},{8,7},{9,8},{10,9},{11,1... | collective-permute-start | bytes 10376 | tf_op jit(solution)/shard_map/ppermute | solution.py:22
  93.1 1.8 %copy.206 = f32[48,18,1]{2,1,0:T(8,128)} copy(f32[48,18,1]{0,2,1:T(1,128)} %collective-permute-done.13) | data formatting | bytes 6912 | tf_op jit(solution)/shard_map/ppermute | solution.py:19
  94.9 1.8 %copy.204 = f32[48,18,1]{2,1,0:T(8,128)} copy(f32[48,18,1]{0,2,1:T(1,128)} %collective-permute-done.12) | data formatting | bytes 6912 | tf_op jit(solution)/shard_map/ppermute | solution.py:22
  96.7 2.1 %pad_maximum_fusion.4 = f32[48,18,130]{2,1,0:T(8,128)S(1)} fusion(f32[48,18,1]{2,1,0:T(8,128)} %copy.204, f32[48,1,128]{2,1,0:T(1,128)} %copy-done.96, f32[48,16,128]{2,1,0:T(8,128)} %copy-done.13, f32[48,1,128]{2,1,0:T(1,128)} %copy-done.93, f32[48,18,1]{2,1,0:T(8,128)} %copy.206), kind=kLoop, calls=%fused_computation.39 | loop fusion | flops 449280 | bytes 898560 | tf_op jit(solution)/shard_map/concatenate | solution.py:23
  99.0 0.9 copy-done.5
  100.3 3.1 %fusion.43 = f32[48,16,128]{2,1,0:T(8,128)S(1)} fusion(f32[48,17,130]{2,1,0:T(8,128)S(1)} %slice_subtract_fusion.1, f32[48,18,1]{2,1,0:T(8,128)S(1)} %copy-done.7, f32[48,18,1]{2,1,0:T(8,128)S(1)} %copy-done.5, f32[48,1,128]{2,1,0:T(1,128)S(1)} %copy-done.97, f32[48,16,128]{2,1,0:T(8,128)S(1)} %copy-done.14, f32[48,1,128]{2,1,0:T(1,128)S(1)} %copy-done.94, ...), kind=kLoop, calls=%fused_computation.280 | loop fusion | flops 2752512 | bytes 3799808 | tf_op jit(solution)/shard_map/add | solution.py:130
  103.7 1.2 fusion.125
  105.0 1.4 %add_divide_fusion.10 = (f32[1,16,128]{2,1,0:T(8,128)S(1)}, f32[1,16,128]{2,1,0:T(8,128)S(1)}, f32[1,16,128]{2,1,0:T(8,128)S(1)}, f32[1,16,128]{2,1,0:T(8,128)S(...) fusion(f32[1,16,128]{2,1,0:T(8,128)} %copy-done.152, ...), kind=kLoop, calls=%fused_computation.1097 | loop fusion | flops 249856 | bytes 1318912 | tf_op jit(solution)/shard_map/div | solution.py:38
  106.7 1.0 constant_dynamic-update-slice_fusion.191
  108.3 0.7 constant_dynamic-update-slice_fusion.148
  109.8 1.4 %collective-permute-start.15 = (f32[48,1,128]{2,1,0:T(1,128)S(1)}, f32[48,1,128]{2,1,0:T(1,128)S(1)}, u32[]{:S(2)}, u32[]{:S(2)}) collective-permute-start(f32[48,1,128]{2,1,0:T(1,128)S(1)} %get-tuple-element.419), channel_id=1, source_target_pairs={{16,0},{0,16},{17,1},{1,17},{18,2},{2,18},{19,3},{3,19},{20,4},{4,... | collective-permute-start | bytes 73736 | tf_op jit(solution)/shard_map/ppermute | solution.py:22
  111.3 1.8 %collective-permute-done.14 = f32[48,1,128]{2,1,0:T(1,128)S(1)} collective-permute-done((f32[48,1,128]{2,1,0:T(1,128)S(1)}, f32[48,1,128]{2,1,0:T(1,128)S(1)}, u32[]{:S(2)}, u32[]{:S(2)}) %collective-permute-start.14) | collective-permute-done | bytes 24608 | tf_op jit(solution)/shard_map/ppermute | solution.py:19
  113.8 1.2 fusion.602
  114.9 1.3 copy.211
  116.3 1.3 copy.209
  117.5 4.7 %collective-permute-start.16 = (f32[48,18,1]{0,2,1:T(1,128)S(1)}, f32[48,18,1]{0,2,1:T(1,128)S(1)}, u32[]{:S(2)}, u32[]{:S(2)}) collective-permute-start(f32[48,18,1]{0,2,1:T(1,128)S(1)} %copy.209), channel_id=1, source_target_pairs={{1,0},{2,1},{3,2},{4,3},{5,4},{6,5},{7,6},{8,7},{9,8},{10,9},{11,1... | collective-permute-start | bytes 10376 | tf_op jit(solution)/shard_map/ppermute | solution.py:22
  122.2 1.1 copy.212
  123.6 1.1 copy.210
  124.7 2.1 %pad_maximum_fusion.5 = f32[48,18,130]{2,1,0:T(8,128)S(1)} fusion(f32[48,18,1]{2,1,0:T(8,128)} %copy.210, f32[48,1,128]{2,1,0:T(1,128)S(1)} %collective-permute-done.15, f32[48,16,128]{2,1,0:T(8,128)} %copy-done.11, f32[48,1,128]{2,1,0:T(1,128)S(1)} %collective-permute-done.14, f32[48,18,1]{2,1,0:T(8,128)} %copy.212), kind=kLoop, calls=%fused_computation.40 | loop fusion | flops 449280 | bytes 898560 | tf_op jit(solution)/shard_map/concatenate | solution.py:23
  127.0 0.9 copy-done.9
  128.3 3.5 %fusion.37 = f32[48,16,128]{2,1,0:T(8,128)} fusion(f32[48,17,130]{2,1,0:T(8,128)S(1)} %slice_subtract_fusion, f32[48,18,1]{2,1,0:T(8,128)S(1)} %copy-done.10, f32[48,18,1]{2,1,0:T(8,128)S(1)} %copy-done.9, f32[48,1,128]{2,1,0:T(1,128)S(1)} %collective-permute-done.15, f32[48,16,128]{2,1,0:T(8,128)S(1)} %copy-done.12, ...), kind=kLoop, calls=%fused_computation.267 | loop fusion | flops 2752512 | bytes 3799808 | tf_op jit(solution)/shard_map/add | solution.py:130
  131.9 4.1 %fusion.29 = f32[48,16,128]{2,1,0:T(8,128)} fusion(f32[48,16,128]{2,1,0:T(8,128)S(1)} %copy-done.4, f32[48,1,128]{2,1,0:T(1,128)S(1)} %copy-done.89, f32[48,18,129]{2,1,0:T(8,128)} %get-tuple-element.404, f32[48,16,128]{2,1,0:T(8,128)S(1)} %constant_dynamic-update-slice_fusion, f32[48,1,128]{2,1,0:T(1,128)S(1)} %copy-done.92, ...), kind=kLoop, calls=%fused_computation.255 | loop fusion | flops 3440640 | bytes 3716608 | tf_op jit(solution)/shard_map/add | solution.py:135
  (685 shorter events, 16.0 us)
Async XLA Ops:
  1.7 16.4 %collective-permute-start.1 = (f32[48,1,128]{2,1,0:T(1,128)S(1)}, f32[48,1,128]{2,1,0:T(1,128)S(1)}, u32[]{:S(2)}, u32[]{:S(2)}) collective-permute-start(f32[48,1,128]{2,1,0:T(1,128)S(1)} %get-tuple-element.424), channel_id=1, source_target_pairs={{0,16},{16,0},{1,17},{17,1},{2,18},{18,2},{3,19},{19,3},{4,20},{20... | collective-permute-start | bytes 73736 | tf_op jit(solution)/shard_map/ppermute | solution.py:19
  4.7 13.3 %collective-permute-start.2 = (f32[48,1,128]{2,1,0:T(1,128)S(1)}, f32[48,1,128]{2,1,0:T(1,128)S(1)}, u32[]{:S(2)}, u32[]{:S(2)}) collective-permute-start(f32[48,1,128]{2,1,0:T(1,128)S(1)} %get-tuple-element.425), channel_id=1, source_target_pairs={{16,0},{0,16},{17,1},{1,17},{18,2},{2,18},{19,3},{3,19},{20,4},{4,... | collective-permute-start | bytes 73736 | tf_op jit(solution)/shard_map/ppermute | solution.py:22
  6.1 3.0 %copy-start.21 = (f32[1,48,16,128]{3,2,1,0:T(8,128)}, f32[1,48,16,128]{3,2,1,0:T(8,128)S(1)}, u32[]{:S(2)}) copy-start(f32[1,48,16,128]{3,2,1,0:T(8,128)S(1)} %get-tuple-element.427) | copy-start | bytes 1179652
  6.9 27.8 %collective-permute-start.5 = (f32[2,48,1,128]{3,2,1,0:T(1,128)}, f32[2,48,1,128]{3,2,1,0:T(1,128)}, u32[]{:S(2)}, u32[]{:S(2)}) collective-permute-start(f32[2,48,1,128]{3,2,1,0:T(1,128)} %pad_maximum_fusion.23), channel_id=1, source_target_pairs={{16,0},{0,16},{17,1},{1,17},{18,2},{2,18},{19,3},{3,19},{20,4},{4,... | collective-permute-start | bytes 147464 | tf_op jit(solution)/shard_map/ppermute | solution.py:10
  9.5 5.9 %collective-permute-start = (f32[2,48,16,1]{1,2,3,0:T(8,128)S(1)}, f32[2,48,16,1]{1,2,3,0:T(8,128)S(1)}, u32[]{:S(2)}, u32[]{:S(2)}) collective-permute-start(f32[2,48,16,1]{1,2,3,0:T(8,128)S(1)} %copy.189), channel_id=1, source_target_pairs={{15,0},{0,1},{1,2},{2,3},{3,4},{4,5},{5,6},{6,7},{7,8},{8,9},{9,10... | collective-permute-start | bytes 18440 | tf_op jit(solution)/shard_map/ppermute | solution.py:10
  10.5 29.4 %copy-start.169 = (f32[1,16,128]{2,1,0:T(8,128)}, f32[1,16,128]{2,1,0:T(8,128)S(1)}, u32[]{:S(2)}) copy-start(f32[1,16,128]{2,1,0:T(8,128)S(1)} %get-tuple-element.369) | copy-start | bytes 24580
  10.5 31.9 %copy-start.66 = (f32[1,16,128]{2,1,0:T(8,128)}, f32[1,16,128]{2,1,0:T(8,128)S(1)}, u32[]{:S(2)}) copy-start(f32[1,16,128]{2,1,0:T(8,128)S(1)} %get-tuple-element.370) | copy-start | bytes 24580
  15.8 3.5 %copy-start.4 = (f32[48,16,128]{2,1,0:T(8,128)S(1)}, f32[48,16,128]{2,1,0:T(8,128)}, u32[]{:S(2)}) copy-start(f32[48,16,128]{2,1,0:T(8,128)} %param.10) | copy-start | bytes 1179652
  21.2 7.9 %collective-permute-start.4 = (f32[48,18,1]{0,2,1:T(1,128)}, f32[48,18,1]{0,2,1:T(1,128)}, u32[]{:S(2)}, u32[]{:S(2)}) collective-permute-start(f32[48,18,1]{0,2,1:T(1,128)} %copy.193), channel_id=1, source_target_pairs={{1,0},{2,1},{3,2},{4,3},{5,4},{6,5},{7,6},{8,7},{9,8},{10,9},{11,1... | collective-permute-start | bytes 10376 | tf_op jit(solution)/shard_map/ppermute | solution.py:22
  21.2 6.1 %collective-permute-start.3 = (f32[48,18,1]{0,2,1:T(1,128)}, f32[48,18,1]{0,2,1:T(1,128)}, u32[]{:S(2)}, u32[]{:S(2)}) collective-permute-start(f32[48,18,1]{0,2,1:T(1,128)} %copy.191), channel_id=1, source_target_pairs={{0,1},{1,2},{2,3},{3,4},{4,5},{5,6},{6,7},{7,8},{8,9},{9,10},{10,1... | collective-permute-start | bytes 10376 | tf_op jit(solution)/shard_map/ppermute | solution.py:19
  30.9 3.0 %copy-start.17 = (f32[48,18,1]{2,1,0:T(8,128)S(1)}, f32[48,18,1]{2,1,0:T(8,128)}, u32[]{:S(2)}) copy-start(f32[48,18,1]{2,1,0:T(8,128)} %copy.192) | copy-start | bytes 10372
  30.9 3.0 %copy-start.19 = (f32[48,18,1]{2,1,0:T(8,128)S(1)}, f32[48,18,1]{2,1,0:T(8,128)}, u32[]{:S(2)}) copy-start(f32[48,18,1]{2,1,0:T(8,128)} %copy.194) | copy-start | bytes 10372
  30.9 3.0 %copy-start.88 = (f32[48,1,128]{2,1,0:T(1,128)S(1)}, f32[48,1,128]{2,1,0:T(1,128)}, u32[]{:S(2)}) copy-start(f32[48,1,128]{2,1,0:T(1,128)} %copy-done.87) | copy-start | bytes 73732
  30.9 3.0 %copy-start.107 = (f32[48,1,128]{2,1,0:T(1,128)S(1)}, f32[48,1,128]{2,1,0:T(1,128)}, u32[]{:S(2)}) copy-start(f32[48,1,128]{2,1,0:T(1,128)} %copy-done.106) | copy-start | bytes 73732
  39.9 3.0 %copy-start.166 = (f32[16,128]{1,0:T(8,128)}, f32[16,128]{1,0:T(8,128)S(1)}, u32[]{:S(2)}) copy-start(f32[16,128]{1,0:T(8,128)S(1)} %get-tuple-element.218) | copy-start | bytes 24580
  39.9 3.0 %copy-start.189 = (f32[16,128]{1,0:T(8,128)}, f32[16,128]{1,0:T(8,128)S(1)}, u32[]{:S(2)}) copy-start(f32[16,128]{1,0:T(8,128)S(1)} %get-tuple-element.222) | copy-start | bytes 24580
  39.9 3.8 %copy-start.81 = (f32[16,128]{1,0:T(8,128)}, f32[16,128]{1,0:T(8,128)S(1)}, u32[]{:S(2)}) copy-start(f32[16,128]{1,0:T(8,128)S(1)} %get-tuple-element.219) | copy-start | bytes 24580
  42.3 5.4 %copy-start.84 = (f32[1,16,128]{2,1,0:T(8,128)}, f32[1,16,128]{2,1,0:T(8,128)S(1)}, u32[]{:S(2)}) copy-start(f32[1,16,128]{2,1,0:T(8,128)S(1)} %get-tuple-element.275) | copy-start | bytes 24580
  43.8 3.9 %collective-permute-start.6 = (f32[48,1,128]{2,1,0:T(1,128)S(1)}, f32[48,1,128]{2,1,0:T(1,128)S(1)}, u32[]{:S(2)}, u32[]{:S(2)}) collective-permute-start(f32[48,1,128]{2,1,0:T(1,128)S(1)} %get-tuple-element.422), channel_id=1, source_target_pairs={{0,16},{16,0},{1,17},{17,1},{2,18},{18,2},{3,19},{19,3},{4,20},{20... | collective-permute-start | bytes 73736 | tf_op jit(solution)/shard_map/ppermute | solution.py:19
  44.0 4.0 %collective-permute-start.7 = (f32[48,1,128]{2,1,0:T(1,128)S(1)}, f32[48,1,128]{2,1,0:T(1,128)S(1)}, u32[]{:S(2)}, u32[]{:S(2)}) collective-permute-start(f32[48,1,128]{2,1,0:T(1,128)S(1)} %get-tuple-element.423), channel_id=1, source_target_pairs={{16,0},{0,16},{17,1},{1,17},{18,2},{2,18},{19,3},{3,19},{20,4},{4,... | collective-permute-start | bytes 73736 | tf_op jit(solution)/shard_map/ppermute | solution.py:22
  52.1 6.3 %collective-permute-start.8 = (f32[48,18,1]{0,2,1:T(1,128)}, f32[48,18,1]{0,2,1:T(1,128)}, u32[]{:S(2)}, u32[]{:S(2)}) collective-permute-start(f32[48,18,1]{0,2,1:T(1,128)} %copy.197), channel_id=1, source_target_pairs={{0,1},{1,2},{2,3},{3,4},{4,5},{5,6},{6,7},{7,8},{8,9},{9,10},{10,1... | collective-permute-start | bytes 10376 | tf_op jit(solution)/shard_map/ppermute | solution.py:19
  54.0 6.3 %collective-permute-start.9 = (f32[48,18,1]{0,2,1:T(1,128)}, f32[48,18,1]{0,2,1:T(1,128)}, u32[]{:S(2)}, u32[]{:S(2)}) collective-permute-start(f32[48,18,1]{0,2,1:T(1,128)} %copy.199), channel_id=1, source_target_pairs={{1,0},{2,1},{3,2},{4,3},{5,4},{6,5},{7,6},{8,7},{9,8},{10,9},{11,1... | collective-permute-start | bytes 10376 | tf_op jit(solution)/shard_map/ppermute | solution.py:22
  77.7 5.4 %copy-start.13 = (f32[48,16,128]{2,1,0:T(8,128)}, f32[48,16,128]{2,1,0:T(8,128)S(1)}, u32[]{:S(2)}) copy-start(f32[48,16,128]{2,1,0:T(8,128)S(1)} %constant_dynamic-update-slice_fusion.96) | copy-start | bytes 1179652
  77.8 3.9 %collective-permute-start.10 = (f32[48,1,128]{2,1,0:T(1,128)S(1)}, f32[48,1,128]{2,1,0:T(1,128)S(1)}, u32[]{:S(2)}, u32[]{:S(2)}) collective-permute-start(f32[48,1,128]{2,1,0:T(1,128)S(1)} %get-tuple-element.420), channel_id=1, source_target_pairs={{0,16},{16,0},{1,17},{17,1},{2,18},{18,2},{3,19},{19,3},{4,20},{20... | collective-permute-start | bytes 73736 | tf_op jit(solution)/shard_map/ppermute | solution.py:19
  79.2 3.8 %collective-permute-start.11 = (f32[48,1,128]{2,1,0:T(1,128)S(1)}, f32[48,1,128]{2,1,0:T(1,128)S(1)}, u32[]{:S(2)}, u32[]{:S(2)}) collective-permute-start(f32[48,1,128]{2,1,0:T(1,128)S(1)} %get-tuple-element.421), channel_id=1, source_target_pairs={{16,0},{0,16},{17,1},{1,17},{18,2},{2,18},{19,3},{3,19},{20,4},{4,... | collective-permute-start | bytes 73736 | tf_op jit(solution)/shard_map/ppermute | solution.py:22
  86.8 6.3 %collective-permute-start.13 = (f32[48,18,1]{0,2,1:T(1,128)}, f32[48,18,1]{0,2,1:T(1,128)}, u32[]{:S(2)}, u32[]{:S(2)}) collective-permute-start(f32[48,18,1]{0,2,1:T(1,128)} %copy.205), channel_id=1, source_target_pairs={{0,1},{1,2},{2,3},{3,4},{4,5},{5,6},{6,7},{7,8},{8,9},{9,10},{10,1... | collective-permute-start | bytes 10376 | tf_op jit(solution)/shard_map/ppermute | solution.py:19
  88.7 6.3 %collective-permute-start.12 = (f32[48,18,1]{0,2,1:T(1,128)}, f32[48,18,1]{0,2,1:T(1,128)}, u32[]{:S(2)}, u32[]{:S(2)}) collective-permute-start(f32[48,18,1]{0,2,1:T(1,128)} %copy.203), channel_id=1, source_target_pairs={{1,0},{2,1},{3,2},{4,3},{5,4},{6,5},{7,6},{8,7},{9,8},{10,9},{11,1... | collective-permute-start | bytes 10376 | tf_op jit(solution)/shard_map/ppermute | solution.py:22
  100.3 3.1 %copy-start.20 = (f32[48,17,130]{2,1,0:T(8,128)}, f32[48,17,130]{2,1,0:T(8,128)S(1)}, u32[]{:S(2)}) copy-start(f32[48,17,130]{2,1,0:T(8,128)S(1)} %slice_subtract_fusion.1) | copy-start | bytes 1272964
  100.3 3.1 %copy-start.168 = (f32[16,128]{1,0:T(8,128)S(1)}, f32[16,128]{1,0:T(8,128)}, u32[]{:S(2)}) copy-start(f32[16,128]{1,0:T(8,128)} %copy-done.166) | copy-start | bytes 24580
  103.4 2.9 %copy-start.29 = (f32[1,16,128]{2,1,0:T(8,128)S(1)}, f32[1,16,128]{2,1,0:T(8,128)}, u32[]{:S(2)}) copy-start(f32[1,16,128]{2,1,0:T(8,128)} %copy-done.27) | copy-start | bytes 24580
  103.4 2.9 %copy-start.32 = (f32[1,16,128]{2,1,0:T(8,128)S(1)}, f32[1,16,128]{2,1,0:T(8,128)}, u32[]{:S(2)}) copy-start(f32[1,16,128]{2,1,0:T(8,128)} %copy-done.30) | copy-start | bytes 24580
  103.4 2.9 %copy-start.35 = (f32[1,16,128]{2,1,0:T(8,128)S(1)}, f32[1,16,128]{2,1,0:T(8,128)}, u32[]{:S(2)}) copy-start(f32[1,16,128]{2,1,0:T(8,128)} %copy-done.33) | copy-start | bytes 24580
  103.4 2.9 %copy-start.38 = (f32[1,16,128]{2,1,0:T(8,128)S(1)}, f32[1,16,128]{2,1,0:T(8,128)}, u32[]{:S(2)}) copy-start(f32[1,16,128]{2,1,0:T(8,128)} %copy-done.36) | copy-start | bytes 24580
  103.4 2.9 %copy-start.41 = (f32[1,16,128]{2,1,0:T(8,128)S(1)}, f32[1,16,128]{2,1,0:T(8,128)}, u32[]{:S(2)}) copy-start(f32[1,16,128]{2,1,0:T(8,128)} %copy-done.39) | copy-start | bytes 24580
  103.5 2.9 %copy-start.44 = (f32[1,16,128]{2,1,0:T(8,128)S(1)}, f32[1,16,128]{2,1,0:T(8,128)}, u32[]{:S(2)}) copy-start(f32[1,16,128]{2,1,0:T(8,128)} %copy-done.42) | copy-start | bytes 24580
  103.5 2.9 %copy-start.47 = (f32[1,16,128]{2,1,0:T(8,128)S(1)}, f32[1,16,128]{2,1,0:T(8,128)}, u32[]{:S(2)}) copy-start(f32[1,16,128]{2,1,0:T(8,128)} %copy-done.45) | copy-start | bytes 24580
  103.5 2.9 %copy-start.50 = (f32[1,16,128]{2,1,0:T(8,128)S(1)}, f32[1,16,128]{2,1,0:T(8,128)}, u32[]{:S(2)}) copy-start(f32[1,16,128]{2,1,0:T(8,128)} %copy-done.48) | copy-start | bytes 24580
  103.5 2.9 %copy-start.53 = (f32[1,16,128]{2,1,0:T(8,128)S(1)}, f32[1,16,128]{2,1,0:T(8,128)}, u32[]{:S(2)}) copy-start(f32[1,16,128]{2,1,0:T(8,128)} %copy-done.51) | copy-start | bytes 24580
  103.5 2.9 %copy-start.56 = (f32[1,16,128]{2,1,0:T(8,128)S(1)}, f32[1,16,128]{2,1,0:T(8,128)}, u32[]{:S(2)}) copy-start(f32[1,16,128]{2,1,0:T(8,128)} %copy-done.54) | copy-start | bytes 24580
  103.5 2.9 %copy-start.59 = (f32[1,16,128]{2,1,0:T(8,128)S(1)}, f32[1,16,128]{2,1,0:T(8,128)}, u32[]{:S(2)}) copy-start(f32[1,16,128]{2,1,0:T(8,128)} %copy-done.57) | copy-start | bytes 24580
  103.5 2.9 %copy-start.62 = (f32[1,16,128]{2,1,0:T(8,128)S(1)}, f32[1,16,128]{2,1,0:T(8,128)}, u32[]{:S(2)}) copy-start(f32[1,16,128]{2,1,0:T(8,128)} %copy-done.60) | copy-start | bytes 24580
  103.5 2.9 %copy-start.65 = (f32[1,16,128]{2,1,0:T(8,128)S(1)}, f32[1,16,128]{2,1,0:T(8,128)}, u32[]{:S(2)}) copy-start(f32[1,16,128]{2,1,0:T(8,128)} %copy-done.63) | copy-start | bytes 24580
  103.5 2.9 %copy-start.68 = (f32[1,16,128]{2,1,0:T(8,128)S(1)}, f32[1,16,128]{2,1,0:T(8,128)}, u32[]{:S(2)}) copy-start(f32[1,16,128]{2,1,0:T(8,128)} %copy-done.66) | copy-start | bytes 24580
  103.5 2.9 %copy-start.71 = (f32[1,16,128]{2,1,0:T(8,128)S(1)}, f32[1,16,128]{2,1,0:T(8,128)}, u32[]{:S(2)}) copy-start(f32[1,16,128]{2,1,0:T(8,128)} %get-tuple-element.374) | copy-start | bytes 24580
  103.6 2.9 %copy-start.74 = (f32[1,16,128]{2,1,0:T(8,128)S(1)}, f32[1,16,128]{2,1,0:T(8,128)}, u32[]{:S(2)}) copy-start(f32[1,16,128]{2,1,0:T(8,128)} %get-tuple-element.378) | copy-start | bytes 24580
  103.6 2.9 %copy-start.77 = (f32[1,16,128]{2,1,0:T(8,128)S(1)}, f32[1,16,128]{2,1,0:T(8,128)}, u32[]{:S(2)}) copy-start(f32[1,16,128]{2,1,0:T(8,128)} %get-tuple-element.382) | copy-start | bytes 24580
  103.6 2.9 %copy-start.80 = (f32[1,16,128]{2,1,0:T(8,128)S(1)}, f32[1,16,128]{2,1,0:T(8,128)}, u32[]{:S(2)}) copy-start(f32[1,16,128]{2,1,0:T(8,128)} %get-tuple-element.386) | copy-start | bytes 24580
  103.6 2.9 %copy-start.86 = (f32[1,16,128]{2,1,0:T(8,128)S(1)}, f32[1,16,128]{2,1,0:T(8,128)}, u32[]{:S(2)}) copy-start(f32[1,16,128]{2,1,0:T(8,128)} %copy-done.84) | copy-start | bytes 24580
  103.6 2.9 %copy-start.105 = (f32[1,16,128]{2,1,0:T(8,128)S(1)}, f32[1,16,128]{2,1,0:T(8,128)}, u32[]{:S(2)}) copy-start(f32[1,16,128]{2,1,0:T(8,128)} %get-tuple-element.368) | copy-start | bytes 24580
  103.6 2.9 %copy-start.112 = (f32[1,16,128]{2,1,0:T(8,128)S(1)}, f32[1,16,128]{2,1,0:T(8,128)}, u32[]{:S(2)}) copy-start(f32[1,16,128]{2,1,0:T(8,128)} %copy-done.110) | copy-start | bytes 24580
  109.1 4.6 %copy-start.11 = (f32[48,16,128]{2,1,0:T(8,128)}, f32[48,16,128]{2,1,0:T(8,128)S(1)}, u32[]{:S(2)}) copy-start(f32[48,16,128]{2,1,0:T(8,128)S(1)} %constant_dynamic-update-slice_fusion.144) | copy-start | bytes 1179652
  109.2 3.9 %collective-permute-start.14 = (f32[48,1,128]{2,1,0:T(1,128)S(1)}, f32[48,1,128]{2,1,0:T(1,128)S(1)}, u32[]{:S(2)}, u32[]{:S(2)}) collective-permute-start(f32[48,1,128]{2,1,0:T(1,128)S(1)} %get-tuple-element.418), channel_id=1, source_target_pairs={{0,16},{16,0},{1,17},{17,1},{2,18},{18,2},{3,19},{19,3},{4,20},{20... | collective-permute-start | bytes 73736 | tf_op jit(solution)/shard_map/ppermute | solution.py:19
  109.8 3.8 %collective-permute-start.15 = (f32[48,1,128]{2,1,0:T(1,128)S(1)}, f32[48,1,128]{2,1,0:T(1,128)S(1)}, u32[]{:S(2)}, u32[]{:S(2)}) collective-permute-start(f32[48,1,128]{2,1,0:T(1,128)S(1)} %get-tuple-element.419), channel_id=1, source_target_pairs={{16,0},{0,16},{17,1},{1,17},{18,2},{2,18},{19,3},{3,19},{20,4},{4,... | collective-permute-start | bytes 73736 | tf_op jit(solution)/shard_map/ppermute | solution.py:22
  116.2 6.0 %collective-permute-start.17 = (f32[48,18,1]{0,2,1:T(1,128)S(1)}, f32[48,18,1]{0,2,1:T(1,128)S(1)}, u32[]{:S(2)}, u32[]{:S(2)}) collective-permute-start(f32[48,18,1]{0,2,1:T(1,128)S(1)} %copy.211), channel_id=1, source_target_pairs={{0,1},{1,2},{2,3},{3,4},{4,5},{5,6},{6,7},{7,8},{8,9},{9,10},{10,1... | collective-permute-start | bytes 10376 | tf_op jit(solution)/shard_map/ppermute | solution.py:19
  117.5 6.1 %collective-permute-start.16 = (f32[48,18,1]{0,2,1:T(1,128)S(1)}, f32[48,18,1]{0,2,1:T(1,128)S(1)}, u32[]{:S(2)}, u32[]{:S(2)}) collective-permute-start(f32[48,18,1]{0,2,1:T(1,128)S(1)} %copy.209), channel_id=1, source_target_pairs={{1,0},{2,1},{3,2},{4,3},{5,4},{6,5},{7,6},{8,7},{9,8},{10,9},{11,1... | collective-permute-start | bytes 10376 | tf_op jit(solution)/shard_map/ppermute | solution.py:22
  128.2 3.6 %copy-start.6 = (f32[48,18,1]{2,1,0:T(8,128)S(1)}, f32[48,18,1]{2,1,0:T(8,128)}, u32[]{:S(2)}) copy-start(f32[48,18,1]{2,1,0:T(8,128)} %copy.206) | copy-start | bytes 10372
  128.2 3.6 %copy-start.8 = (f32[48,18,1]{2,1,0:T(8,128)S(1)}, f32[48,18,1]{2,1,0:T(8,128)}, u32[]{:S(2)}) copy-start(f32[48,18,1]{2,1,0:T(8,128)} %copy.204) | copy-start | bytes 10372
  128.2 3.6 %copy-start.15 = (f32[48,16,128]{2,1,0:T(8,128)S(1)}, f32[48,16,128]{2,1,0:T(8,128)}, u32[]{:S(2)}) copy-start(f32[48,16,128]{2,1,0:T(8,128)} %copy-done.13) | copy-start | bytes 1179652
  128.2 3.6 %copy-start.89 = (f32[48,1,128]{2,1,0:T(1,128)S(1)}, f32[48,1,128]{2,1,0:T(1,128)}, u32[]{:S(2)}) copy-start(f32[48,1,128]{2,1,0:T(1,128)} %copy-done.87) | copy-start | bytes 73732
  128.2 3.6 %copy-start.92 = (f32[48,1,128]{2,1,0:T(1,128)S(1)}, f32[48,1,128]{2,1,0:T(1,128)}, u32[]{:S(2)}) copy-start(f32[48,1,128]{2,1,0:T(1,128)} %copy-done.90) | copy-start | bytes 73732
  128.2 3.6 %copy-start.95 = (f32[48,1,128]{2,1,0:T(1,128)S(1)}, f32[48,1,128]{2,1,0:T(1,128)}, u32[]{:S(2)}) copy-start(f32[48,1,128]{2,1,0:T(1,128)} %copy-done.93) | copy-start | bytes 73732
  128.2 3.6 %copy-start.98 = (f32[48,1,128]{2,1,0:T(1,128)S(1)}, f32[48,1,128]{2,1,0:T(1,128)}, u32[]{:S(2)}) copy-start(f32[48,1,128]{2,1,0:T(1,128)} %copy-done.96) | copy-start | bytes 73732
  128.2 3.6 %copy-start.226 = (s32[16,128]{1,0:T(8,128)S(1)}, s32[16,128]{1,0:T(8,128)}, u32[]{:S(2)}) copy-start(s32[16,128]{1,0:T(8,128)} %param.18) | copy-start | bytes 24580
  128.2 3.6 %copy-start.227 = (s32[16,128]{1,0:T(8,128)S(1)}, s32[16,128]{1,0:T(8,128)}, u32[]{:S(2)}) copy-start(s32[16,128]{1,0:T(8,128)} %param.19) | copy-start | bytes 24580
  (182 other events, 366.6 us)
where the time goes:
time: 138 us; the launch traced here: 136 us
  other arithmetic  46.8 us (34%)
  local copies, waits for them, and re-layouts  41.7 us (30%)
  starting transfers between devices  25.5 us (18%)
  waiting for transfers between devices  16.6 us (12%)
  between operations  5.34 us (4%)
    ppermute x8, starting transfers between devices, padded(): lax.ppermute(lax.slice_in_dim(block, 0, width, axis=dim), axis, backward)  17.6 us
    concatenate x10, other arithmetic, padded(): block = jnp.concatenate([low, block, high], axis=dim)  12.2 us
    slice x12, local copies, waits for them, and re-layouts, padded(): lax.slice_in_dim(block, block.shape[dim] - width, None, axis=dim)  10.8 us
    unnamed x544, local copies, waits for them, and re-layouts  9.37 us
    ppermute x8, waiting for transfers between devices, padded(): lax.ppermute(lax.slice_in_dim(block, block.shape[dim] - width, None, axis...  9.22 us
    div x9, other arithmetic, solve_columns(): last_carry = (rhs[height] + upper_link * last_carry) / divisor  8.53 us
    add x2, other arithmetic, per_device(): solved * (1.0 - sink_rate * (1.0 - squeeze * squeeze)) + from_x + from_y  6.65 us
    unnamed x100, other arithmetic  6.57 us
  transfers between devices with their start and end apart: 18, of which 9 were waited for; matrix products, arithmetic and copies ran while one was open for 20% of the time, Pallas kernels for 0%

commit v1 on v0

v1 whole, which is shorter than its diff:
```python
import functools

import jax
import jax.numpy as jnp
from jax import lax
from jax.experimental import pallas as pl
from jax.experimental.pallas import tpu as pltpu
from jax.sharding import PartitionSpec as P

F32 = jnp.float32
VMEM = pl.BlockSpec(memory_space=pltpu.VMEM)
GROUP = 8
NAMES = ("s", "es", "ns", "mix", "relax", "vm", "obs")


def call(kernel, outs, scratch, *args):
    return pl.pallas_call(
        kernel,
        out_shape=[jax.ShapeDtypeStruct(shape, F32) for shape in outs],
        in_specs=[VMEM] * len(args),
        out_specs=[VMEM] * len(outs),
        scratch_shapes=[pltpu.VMEM(shape, F32) for shape in scratch],
        compiler_params=pltpu.CompilerParams(vmem_limit_bytes=16 << 20),
    )(*args)


def iota(shape, dim):
    return lax.broadcasted_iota(jnp.int32, shape, dim)


def roll(x, shift, axis):
    if isinstance(shift, int):
        shift = shift % x.shape[axis]
        if shift == 0:
            return x
    return pltpu.roll(x, shift, axis)


def odd_column():
    return lax.rem(lax.axis_index("tx"), 2) == 1


def level_of(ref, name, level):
    if name == "vm":
        level = jnp.minimum(level, ref.shape[0] - 1)
    return ref[level].astype(F32)


def edge_rows(block):
    return jnp.where(iota((8, block.shape[1]), 0) < 4, block[:8], block[-8:])


def near(shape):
    sub = iota(shape, 0)
    return (sub < 2) | (sub >= 6)


def pack_rows(get):
    tile = {name: edge_rows(get(name)) for name in NAMES[:6]}
    shape = tile["s"].shape
    sub = iota(shape, 0)
    first = jnp.where(near(shape), tile["s"], roll(tile["ns"], 4, 0))
    first = jnp.where(sub == 5, roll(tile["vm"], 5, 0), first)
    second = jnp.where((sub == 3) | (sub == 4), roll(tile["es"], 4, 0), tile["mix"])
    second = jnp.where((sub == 1) | (sub == 2), roll(tile["relax"], 2, 0), second)
    second = jnp.where(sub == 5, roll(tile["vm"], 6, 0), second)
    return first, second


def unpack_rows(first, second):
    sub = iota(first.shape, 0)
    return {
        "s": first,
        "ns": roll(first, 4, 0),
        "mix": second,
        "es": roll(second, 4, 0),
        "relax": roll(second, 6, 0),
        "vm": jnp.where(sub == 0, roll(first, 3, 0), roll(second, 2, 0)),
    }


def pack_kernel(s, es, ns, mix, relax, vm, obs, count, rows, corners, one, two, planes):
    refs = dict(zip(NAMES, (s, es, ns, mix, relax, vm, obs)))
    levels = s.shape[0]
    per_plane = 128 // GROUP
    plane_count = levels // per_plane
    shape = s.shape[1:]
    group = iota(shape, 1) // GROUP

    for a, name in enumerate(NAMES):
        def columns(p, carry, a=a, name=name):
            acc = jnp.zeros(shape, F32)
            for g in range(per_plane):
                x = level_of(refs[name], name, p * per_plane + g)
                acc = jnp.where(group == g, roll(x, GROUP * g + 4, 1), acc)
            planes[a * plane_count + p] = acc
            return carry

        lax.fori_loop(0, plane_count, columns, 0)
    total = len(NAMES) * plane_count
    count_plane = count[...].astype(F32)
    planes[total] = roll(count_plane, 4, 1)
    if (total + 1) % 2:
        planes[total + 1] = jnp.zeros(shape, F32)

    odd = odd_column()
    low = iota(shape, 1) % GROUP < 4
    for h in range(one.shape[0]):
        x, y = planes[2 * h], planes[2 * h + 1]
        to_east = jnp.where(low, x, roll(y, 4, 1))
        to_west = jnp.where(low, roll(x, -4, 1), y)
        one[h] = jnp.where(odd, to_west, to_east)
        two[h] = jnp.where(odd, to_east, to_west)

    small = (8, shape[1])
    small_group = iota(small, 1) // GROUP
    half = per_plane // 2

    def rims(p, carry):
        acc = jnp.zeros(small, F32)
        for m in range(half):
            level = p * half + m
            pair = pack_rows(lambda name: level_of(refs[name], name, level))
            for q in range(2):
                rows[2 * level + q] = pair[q]
                g = 2 * m + q
                acc = jnp.where(small_group == g, roll(pair[q], GROUP * g + 4, 1), acc)
        corners[p] = acc
        return carry

    lax.fori_loop(0, levels // half, rims, 0)
    count_rows = edge_rows(count_plane)
    rows[2 * levels] = count_rows
    corners[levels // half] = roll(count_rows, 4, 1)


def shift_up(x, axis):
    return roll(x, -1, axis)


def shift_down(x, axis):
    return roll(x, 1, axis)


def extend(main, side, rows=None, corners=None):
    top = jnp.concatenate([main, side], axis=1)
    if rows is None:
        return top
    return jnp.concatenate([top, jnp.concatenate([rows, corners], axis=1)], axis=0)


def solve_inward(levels, get, inv_q, carries):
    half = levels // 2
    inv, q = inv_q

    def step(t, carry):
        new = []
        for k, last in ((t, carry[0]), (levels - 1 - t, carry[1])):
            c = get(k) * inv(k) + q(k) * last
            carries[k] = c
            new.append(c)
        return tuple(new)

    zero = jnp.zeros(carries.shape[1:], F32)
    return lax.fori_loop(0, half, step, (zero, zero), unroll=2)


def solve_outward(levels, ends, ratio, join, carries, use):
    half = levels // 2
    high, low = ends
    upper = (high + ratio(half - 1) * low) * join
    lower = (low + ratio(half) * high) * join

    def step(t, carry):
        t = half - 1 - t
        new = []
        for k, last in ((t, carry[0]), (levels - 1 - t, carry[1])):
            x = carries[k] + ratio(k) * last
            use(k, x)
            new.append(x)
        return tuple(new)

    lax.fori_loop(0, half, step, (lower, upper), unroll=2)


def merge_halos(odd, from_one, from_two, planes):
    low = iota(from_one.shape[1:], 1) % GROUP < 4
    for h in range(from_one.shape[0]):
        a, b = from_one[h], from_two[h]
        west = jnp.where(odd, a, b)
        east = jnp.where(odd, b, a)
        planes[2 * h] = jnp.where(low, west, roll(east, 4, 1))
        planes[2 * h + 1] = jnp.where(low, roll(west, -4, 1), east)


def forward_kernel(
    s, es, ns, mix, relax, vm, obs, count, from_one, from_two, rows_n, rows_s, corner_one_n,
    corner_one_s, corner_two_n, corner_two_s,
    ep_out, em_out, np_out, nm_out, sink_out, inv_out, q_out, r_out, middle_out, solved_out,
    counts_out, join_out, start_out, send,
    planes, corners, rhs, links, carries,
):
    refs = dict(zip(NAMES, (s, es, ns, mix, relax, vm, obs)))
    levels = s.shape[0]
    half = levels // 2
    per_plane = 128 // GROUP
    plane_count = levels // per_plane
    odd = odd_column()
    merge_halos(odd, from_one, from_two, planes)
    small = (8, s.shape[2])
    low = iota(small, 1) % GROUP < 4
    north = iota(small, 0) < 4

    def rows_at(index):
        return rows_n[index], rows_s[index]

    def merge_first(n, s_):
        sub = iota(n.shape, 0)
        return jnp.where((sub < 2) | (sub == 4) | (sub == 5), n, s_)

    def merge_second(n, s_):
        sub = iota(n.shape, 0)
        return jnp.where((sub == 0) | (sub == 4) | (sub == 2), n, s_)

    def corner_plane(p):
        out = []
        for one_ref, two_ref in ((corner_one_n, corner_two_n), (corner_one_s, corner_two_s)):
            a, b = one_ref[p], two_ref[p]
            west = jnp.where(odd, a, b)
            east = jnp.where(odd, b, a)
            out.append(jnp.where(low, west, east))
        return out

    total = levels * 2 // per_plane
    first_group = (iota(small, 1) // GROUP) % 2 == 0
    for p in range(total):
        n, s_ = corner_plane(p)
        corners[p] = jnp.where(first_group, merge_first(n, s_), merge_second(n, s_))
    n, s_ = corner_plane(total)
    corners[total] = jnp.where(north, n, s_)

    last = len(NAMES) * plane_count
    count_ext = extend(
        count[...].astype(F32),
        roll(planes[last], 124, 1),
        jnp.where(north, rows_n[2 * levels], rows_s[2 * levels]),
        roll(corners[total], 124, 1),
    )
    east_count = jnp.minimum(count_ext, shift_up(count_ext, 1))
    north_count = jnp.minimum(count_ext, shift_up(count_ext, 0))
    counts_out[0] = count_ext
    counts_out[1] = east_count
    counts_out[2] = north_count

    def side_of(name, k):
        p = NAMES.index(name) * plane_count + k // per_plane
        return roll(planes[p], 124 - GROUP * (k % per_plane), 1)

    def load(k):
        pair = []
        for j, merge in enumerate((merge_first, merge_second)):
            index = 2 * k + j
            line = merge(rows_n[index], rows_s[index])
            corner = roll(corners[index // per_plane], 124 - GROUP * (index % per_plane), 1)
            pair.append(jnp.concatenate([line, corner], axis=1))
        rim = unpack_rows(*pair)
        return {
            name: jnp.concatenate(
                [extend(level_of(refs[name], name, k), side_of(name, k)), rim[name]], axis=0
            )
            for name in NAMES[:6]
        }

    def prepare(k, carry):
        x = load(k)
        level = k.astype(F32)
        state = x["s"]
        open_east = level < east_count
        open_north = level < north_count
        ep = jnp.where(open_east, 0.5 * x["es"] + x["mix"], 0.0)
        em = jnp.where(open_east, 0.5 * x["es"] - x["mix"], 0.0)
        np_ = jnp.where(open_north, 0.5 * x["ns"] + x["mix"], 0.0)
        nm = jnp.where(open_north, 0.5 * x["ns"] - x["mix"], 0.0)
        sink = jnp.where(level < count_ext, x["relax"], 0.0)
        link = jnp.where(level + 1.0 < count_ext, x["vm"], 0.0)
        ep_out[k] = ep
        em_out[k] = em
        np_out[k] = np_
        nm_out[k] = nm
        sink_out[k] = sink
        links[k] = link
        start_out[k] = state
        rhs[k] = advance(state, ep, em, np_, nm, sink)
        return carry

    def advance(state, ep, em, np_, nm, sink):
        fe = ep * state + em * shift_up(state, 1)
        fn = np_ * state + nm * shift_up(state, 0)
        spread = (fe - shift_down(fe, 1)) + (fn - shift_down(fn, 0))
        return state - spread - sink * jnp.tanh(state)

    lax.fori_loop(0, levels, prepare, 0)

    def factor(t, carry):
        (r_top, c_top), (r_low, c_low) = carry
        k = t
        above = jnp.where(k > 0, links[jnp.maximum(k - 1, 0)], 0.0)
        below = links[k]
        inv = 1.0 / (1.0 + above + below - above * r_top)
        q = above * inv
        r_top = below * inv
        c_top = rhs[k] * inv + q * c_top
        inv_out[k] = inv
        q_out[k] = q
        r_out[k] = r_top
        carries[k] = c_top
        k = levels - 1 - t
        above = links[k - 1]
        below = links[k]
        inv = 1.0 / (1.0 + above + below - below * r_low)
        q = below * inv
        r_low = above * inv
        c_low = rhs[k] * inv + q * c_low
        inv_out[k] = inv
        q_out[k] = q
        r_out[k] = r_low
        carries[k] = c_low
        return (r_top, c_top), (r_low, c_low)

    zero = jnp.zeros(rhs.shape[1:], F32)
    (r_top, c_top), (r_low, c_low) = lax.fori_loop(
        0, half, factor, ((zero, zero), (zero, zero)), unroll=2
    )
    join = 1.0 / (1.0 - r_top * r_low)
    join_out[...] = join

    def to_second(k, x):
        middle_out[k] = x
        value = advance(x, ep_out[k], em_out[k], np_out[k], nm_out[k], sink_out[k])
        rhs[k, :16] = value[:16]

    solve_outward(levels, (c_top, c_low), lambda k: r_out[k], join, carries, to_second)

    main = carries.at[:, :16]
    inv_q = (lambda k: inv_out[k, :16], lambda k: q_out[k, :16])
    ratio = lambda k: r_out[k, :16]
    ends = solve_inward(levels, lambda k: rhs[k, :16], inv_q, main)

    def to_adjoint(k, x):
        seen = extend(level_of(refs["obs"], "obs", k), side_of("obs", k))
        rhs[k, :16] = jnp.where(k.astype(F32) < count_ext[:16], x - seen, 0.0)

    solve_outward(levels, ends, ratio, join[:16], main, to_adjoint)
    ends = solve_inward(levels, lambda k: rhs[k, :16], inv_q, main)

    def to_solved(k, x):
        solved_out[k] = x

    solve_outward(levels, ends, ratio, join[:16], main, to_solved)

    group = iota(small, 1) // GROUP
    for p in range(send.shape[0] - half):
        acc = jnp.zeros(small, F32)
        for g in range(min(per_plane, half - p * per_plane)):
            t = p * per_plane + g
            x = edge_rows(solved_out[t])
            y = edge_rows(solved_out[levels - 1 - t])
            both = jnp.where(near(x.shape), x, roll(y, 4, 0))
            send[t] = both[:, :128]
            acc = jnp.where(
                group == g, roll(both[:, 128:], GROUP * g + 4, 1), acc
            )
        send[half + p] = acc


def backward_kernel(
    ep, em, np_, nm, sink, inv, q, r, middle, solved, counts, join, start, rows_n, rows_s,
    adjoint_out, gradient_out, carries,
):
    levels = solved.shape[0]
    half = levels // 2
    per_plane = 128 // GROUP
    small = (8, 128)
    sub = iota(small, 0)
    from_north = (sub < 2) | (sub == 4) | (sub == 5)

    def rims(t):
        line = jnp.where(from_north, rows_n[t], rows_s[t])
        p = half + t // per_plane
        corner = jnp.where(from_north, rows_n[p], rows_s[p])
        corner = roll(corner, 124 - GROUP * (t % per_plane), 1)
        both = jnp.concatenate([line, corner], axis=1)
        return both, roll(both, 4, 0)

    def pull(k, x, state):
        ge = shift_up(x, 1) - x
        gn = shift_up(x, 0) - x
        squeeze = jnp.tanh(state)
        result = x * (1.0 - sink[k] * (1.0 - squeeze * squeeze))
        result = result + ep[k] * ge + shift_down(em[k] * ge, 1)
        result = result + np_[k] * gn + shift_down(nm[k] * gn, 0)
        level = k.astype(F32)
        part = jnp.where(level < counts[1], ge * (shift_up(state, 1) - state), 0.0)
        part = part + jnp.where(level < counts[2], gn * (shift_up(state, 0) - state), 0.0)
        return result, part

    def late(t, carry):
        new = []
        for k, rim, last in zip((t, levels - 1 - t), rims(t), carry):
            x = jnp.concatenate([solved[k], rim], axis=0)
            result, part = pull(k, x, middle[k])
            gradient_out[k] = -part[:16, :128]
            c = result * inv[k] + q[k] * last
            carries[k] = c
            new.append(c)
        return tuple(new)

    zero = jnp.zeros(carries.shape[1:], F32)
    ends = lax.fori_loop(0, half, late, (zero, zero))

    def early(k, x):
        result, part = pull(k, x, start[k])
        adjoint_out[k] = result[:16, :128]
        gradient_out[k] = gradient_out[k] - part[:16, :128]

    solve_outward(levels, ends, lambda k: r[k], join[...], carries, early)


def ring(axis, distance):
    count = lax.axis_size(axis)
    return [(i, (i + distance) % count) for i in range(count)]


def both_ways(x):
    from_north = lax.ppermute(x, "ty", ring("ty", -1))
    if lax.axis_size("ty") == 2:
        return from_north, from_north
    return from_north, lax.ppermute(x, "ty", ring("ty", 1))


def swap(x, phase, rise):
    ny, nx = lax.axis_size("ty"), lax.axis_size("tx")
    route = []
    for j in range(ny):
        for i in range(nx):
            partner = (i + 1) % nx if i % 2 == phase else (i - 1) % nx
            route.append((j * nx + i, ((j + rise) % ny) * nx + partner))
    return lax.ppermute(x, ("ty", "tx"), route)


def diagonal(x, phase):
    from_north = swap(x, phase, -1)
    if lax.axis_size("ty") == 2:
        return from_north, from_north
    return from_north, swap(x, phase, 1)


def per_device(
    tracer_start,
    observed,
    east_speed,
    north_speed,
    mixing,
    vertical_mixing,
    relax_rate,
    level_count,
    face_east,
    face_north,
):
    levels, ny, nx = tracer_start.shape
    per_plane = 128 // GROUP
    plane_count = levels // per_plane
    pairs = (len(NAMES) * plane_count + 2) // 2
    fields = (
        tracer_start, east_speed, north_speed, mixing, relax_rate, vertical_mixing, observed,
        level_count,
    )
    corner_planes = 2 * levels // per_plane + 1
    rows, corners, one, two = call(
        pack_kernel,
        [
            (2 * levels + 1, 8, nx),
            (corner_planes, 8, nx),
            (pairs, ny, nx),
            (pairs, ny, nx),
        ],
        [(2 * pairs, ny, nx)],
        *fields,
    )
    rows_n, rows_s = both_ways(rows)
    from_two = swap(two, 1, 0)
    corner_two_n, corner_two_s = diagonal(corners, 1)
    from_one = swap(one, 0, 0)
    corner_one_n, corner_one_s = diagonal(corners, 0)
    ext = (levels, ny + 8, 2 * nx)
    half = levels // 2
    outs = call(
        forward_kernel,
        [ext] * 9 + [(levels, ny, 2 * nx), (3,) + ext[1:], ext[1:], ext]
        + [(half + -(-half // per_plane), 8, nx)],
        [(2 * pairs, ny, nx), (corner_planes, 8, nx), ext, ext, ext],
        *fields, from_one, from_two, rows_n, rows_s,
        corner_one_n, corner_one_s, corner_two_n, corner_two_s,
    )
    ep, em, np_, nm, sink, inv, q, r, middle, solved, counts, join, start, send = outs
    sent_n, sent_s = both_ways(send)
    adjoint, gradient = call(
        backward_kernel,
        [(levels, ny, nx)] * 2,
        [ext],
        ep, em, np_, nm, sink, inv, q, r, middle, solved, counts, join, start, sent_n, sent_s,
    )
    return adjoint, gradient


def solution(mesh):
    block = P(None, "ty", "tx")
    plane = P("ty", "tx")
    return jax.shard_map(
        per_device,
        mesh=mesh,
        in_specs=(block,) * 7 + (plane,) * 3,
        out_specs=(block, block),
        check_vma=False,
    )
```

time: 138 us -> 54.1 us (0.39); the launches traced: 136 us -> 53.8 us
  other arithmetic: 46.8 us -> 0 us
  local copies, waits for them, and re-layouts: 41.7 us -> 7.24 us
  Pallas kernels: 0 us -> 26.5 us
  starting transfers between devices: 25.5 us -> 8.36 us
  waiting for transfers between devices: 16.6 us -> 11 us
  between operations: 5.34 us -> 0.68 us
    pallas_call x0 -> x3, Pallas kernels: none -> 26.5 us  [call(): pl.pallas_call(kernel, out_shape=[jax.ShapeDtypeStruct(shape, F32) for sh...]
    ppermute x18 -> x6, starting transfers between devices: 25.5 us -> 8.36 us  [the longest x4 4.65 us: swap(): return lax.ppermute(x, ('ty', 'tx'), route)]
    slice x17 -> x0, local copies, waits for them, and re-layouts: 16.9 us -> none  [the longest x12 10.8 us: padded(): lax.slice_in_dim(block, block.shape[dim] - width, None, axis=dim)]
    concatenate x12 -> x0, other arithmetic: 16.1 us -> none  [the longest x10 12.2 us: padded(): block = jnp.concatenate([low, block, high], axis=dim)]
    ppermute x9 -> x0, local copies, waits for them, and re-layouts: 13.5 us -> none  [the longest x4 6.56 us: padded(): lax.ppermute(lax.slice_in_dim(block, block.shape[dim] - width, None, axis...]
    add x5 -> x0, other arithmetic: 11.2 us -> none  [the longest x2 6.65 us: per_device(): solved * (1.0 - sink_rate * (1.0 - squeeze * squeeze)) + from_x + from_y]
    div x10 -> x0, other arithmetic: 9.25 us -> none  [the longest x9 8.53 us: solve_columns(): last_carry = (rhs[height] + upper_link * last_carry) / divisor]
    unnamed x100 -> x0, other arithmetic: 6.57 us -> none
  transfers between devices with their start and end apart: 18 -> 6, of which waited for: 9 -> 2; matrix products, arithmetic and copies ran while one was open for 20% -> 0% of each run, Pallas kernels for 0% -> 0%
where the time goes in v1:
time: 54.1 us; the launch traced here: 53.8 us
  Pallas kernels  26.5 us (49%)
  waiting for transfers between devices  11 us (20%)
  starting transfers between devices  8.36 us (15%)
  local copies, waits for them, and re-layouts  7.24 us (13%)
  between operations  0.68 us (1%)
    pallas_call x3, Pallas kernels, call(): pl.pallas_call(kernel, out_shape=[jax.ShapeDtypeStruct(shape, F32) for sh...  26.5 us
    unnamed x16, local copies, waits for them, and re-layouts  7.24 us
    ppermute x4, waiting for transfers between devices, swap(): return lax.ppermute(x, ('ty', 'tx'), route)  6.89 us
    ppermute x4, starting transfers between devices, swap(): return lax.ppermute(x, ('ty', 'tx'), route)  4.65 us
    ppermute x2, waiting for transfers between devices, both_ways(): from_north = lax.ppermute(x, 'ty', ring('ty', -1))  4.09 us
    ppermute x2, starting transfers between devices, both_ways(): from_north = lax.ppermute(x, 'ty', ring('ty', -1))  3.71 us
  transfers between devices with their start and end apart: 6, of which 2 were waited for; matrix products, arithmetic and copies ran while one was open for 0% of the time, Pallas kernels for 0%

profile of v1, /device:TPU:0, one launch (start us, length us, event | category | flops | bytes accessed | tf_op | source)
XLA Modules:
  0.0 53.8 jit_solution(14306276667034113730)
XLA Ops:
  0.6 0.0 copy-start
  0.6 1.0 %copy-done = f32[48,16,128]{2,1,0:T(8,128)S(1)} copy-done((f32[48,16,128]{2,1,0:T(8,128)S(1)}, f32[48,16,128]{2,1,0:T(8,128)}, u32[]{:S(2)}) %copy-start) | copy-done | bytes 393240
  1.6 0.0 copy-start.1
  1.6 0.9 %copy-done.1 = bf16[48,16,128]{2,1,0:T(8,128)(2,1)S(1)} copy-done((bf16[48,16,128]{2,1,0:T(8,128)(2,1)S(1)}, bf16[48,16,128]{2,1,0:T(8,128)(2,1)}, u32[]{:S(2)}) %copy-start.1) | copy-done | bytes 196632
  2.6 0.0 copy-start.2
  2.6 0.9 %copy-done.2 = bf16[48,16,128]{2,1,0:T(8,128)(2,1)S(1)} copy-done((bf16[48,16,128]{2,1,0:T(8,128)(2,1)S(1)}, bf16[48,16,128]{2,1,0:T(8,128)(2,1)}, u32[]{:S(2)}) %copy-start.2) | copy-done | bytes 196632
  3.5 0.0 copy-start.3
  3.5 0.9 %copy-done.3 = bf16[48,16,128]{2,1,0:T(8,128)(2,1)S(1)} copy-done((bf16[48,16,128]{2,1,0:T(8,128)(2,1)S(1)}, bf16[48,16,128]{2,1,0:T(8,128)(2,1)}, u32[]{:S(2)}) %copy-start.3) | copy-done | bytes 196632
  4.4 0.0 copy-start.4
  4.4 0.9 %copy-done.4 = bf16[48,16,128]{2,1,0:T(8,128)(2,1)S(1)} copy-done((bf16[48,16,128]{2,1,0:T(8,128)(2,1)S(1)}, bf16[48,16,128]{2,1,0:T(8,128)(2,1)}, u32[]{:S(2)}) %copy-start.4) | copy-done | bytes 196632
  5.3 0.0 copy-start.5
  5.3 0.9 %copy-done.5 = bf16[48,16,128]{2,1,0:T(8,128)(2,1)S(1)} copy-done((bf16[48,16,128]{2,1,0:T(8,128)(2,1)S(1)}, bf16[48,16,128]{2,1,0:T(8,128)(2,1)}, u32[]{:S(2)}) %copy-start.5) | copy-done | bytes 196632
  6.3 0.0 copy-start.6
  6.3 0.9 %copy-done.6 = bf16[47,16,128]{2,1,0:T(8,128)(2,1)S(1)} copy-done((bf16[47,16,128]{2,1,0:T(8,128)(2,1)S(1)}, bf16[47,16,128]{2,1,0:T(8,128)(2,1)}, u32[]{:S(2)}) %copy-start.6) | copy-done | bytes 192536
  7.2 0.0 copy-start.7
  7.2 0.7 %copy-done.7 = s32[16,128]{1,0:T(8,128)S(1)} copy-done((s32[16,128]{1,0:T(8,128)S(1)}, s32[16,128]{1,0:T(8,128)}, u32[]{:S(2)}) %copy-start.7) | copy-done | bytes 8216
  7.9 2.6 %shard_map.95 = (f32[97,8,128]{2,1,0:T(8,128)S(1)}, f32[7,8,128]{2,1,0:T(8,128)S(1)}, f32[11,16,128]{2,1,0:T(8,128)S(1)}, f32[11,16,128]{2,1,0:T(8,128)S(1)}) custom-call(f32[48,16,128]{2,1,0:T(8,128)S(1)} %copy-done, bf16[48,16,128]{2,1,0:T(8,128)(2,1)S(1)} %copy-done.1, bf16[48,16,128]{2,1,0:T(8,128)(2,1)S(1)} %copy-done.2, ...), custom_call_target="tpu_custom_call" | custom-call | tf_op jit(solution)/shard_map/pallas_call | solution.py:17
  10.5 3.0 %collective-permute-start.2 = (f32[97,8,128]{2,1,0:T(8,128)S(1)}, f32[97,8,128]{2,1,0:T(8,128)S(1)}, u32[]{:S(2)}, u32[]{:S(2)}) collective-permute-start(f32[97,8,128]{2,1,0:T(8,128)S(1)} %get-tuple-element.22), channel_id=1, source_target_pairs={{0,16},{16,0},{1,17},{17,1},{2,18},{18,2},{3,19},{19,3},{4,20},{20... | collective-permute-start | bytes 1191944 | tf_op jit(solution)/shard_map/ppermute | solution.py:435
  13.6 0.0 collective-permute-start
  13.6 4.6 %collective-permute-start.1 = (f32[11,16,128]{2,1,0:T(8,128)S(1)}, f32[11,16,128]{2,1,0:T(8,128)S(1)}, u32[]{:S(2)}, u32[]{:S(2)}) collective-permute-start(f32[11,16,128]{2,1,0:T(8,128)S(1)} %get-tuple-element.21), channel_id=1, source_target_pairs={{0,15},{1,2},{2,1},{3,4},{4,3},{5,6},{6,5},{7,8},{8,7},{9,10},{10,... | collective-permute-start | bytes 270344 | tf_op jit(solution)/shard_map/ppermute | solution.py:448
  18.2 0.0 collective-permute-start.4
  18.2 0.0 collective-permute-start.3
  18.2 6.9 %collective-permute-done.4.corner_two_n.corner_two_s = f32[7,8,128]{2,1,0:T(8,128)S(1)} collective-permute-done((f32[7,8,128]{2,1,0:T(8,128)S(1)}, f32[7,8,128]{2,1,0:T(8,128)S(1)}, u32[]{:S(2)}, u32[]{:S(2)}) %collective-permute-start.4) | collective-permute-done | bytes 28704 | tf_op jit(solution)/shard_map/ppermute | solution.py:448
  25.1 0.0 collective-permute-done.3.corner_one_n.corner_one_s
  25.1 0.0 collective-permute-done.from_one
  25.1 0.0 collective-permute-done.1.from_two
  25.1 0.0 collective-permute-done.2.rows_n.rows_s
  25.1 15.6 %shard_map.96 = (f32[48,24,256]{2,1,0:T(8,128)S(1)}, f32[48,24,256]{2,1,0:T(8,128)S(1)}, f32[48,24,256]{2,1,0:T(8,128)S(1)}, f32[48,24,256]{2,1,0:T(8,128)S(1)},...) custom-call(f32[48,16,128]{2,1,0:T(8,128)S(1)} %copy-done, ...), custom_call_target="tpu_custom_call" | custom-call | tf_op jit(solution)/shard_map/pallas_call | solution.py:17
  40.8 0.7 %collective-permute-start.5 = (f32[26,8,128]{2,1,0:T(8,128)S(1)}, f32[26,8,128]{2,1,0:T(8,128)S(1)}, u32[]{:S(2)}, u32[]{:S(2)}) collective-permute-start(f32[26,8,128]{2,1,0:T(8,128)S(1)} %get-tuple-element.37), channel_id=1, source_target_pairs={{0,16},{16,0},{1,17},{17,1},{2,18},{18,2},{3,19},{19,3},{4,20},{20... | collective-permute-start | bytes 319496 | tf_op jit(solution)/shard_map/ppermute | solution.py:435
  41.4 4.1 %collective-permute-done.5.rows_n.rows_s = f32[26,8,128]{2,1,0:T(8,128)S(1)} collective-permute-done((f32[26,8,128]{2,1,0:T(8,128)S(1)}, f32[26,8,128]{2,1,0:T(8,128)S(1)}, u32[]{:S(2)}, u32[]{:S(2)}) %collective-permute-start.5) | collective-permute-done | bytes 106528 | tf_op jit(solution)/shard_map/ppermute | solution.py:435
  45.5 8.2 %shard_map.97 = (f32[48,16,128]{2,1,0:T(8,128)}, f32[48,16,128]{2,1,0:T(8,128)}) custom-call(f32[48,24,256]{2,1,0:T(8,128)S(1)} %get-tuple-element.24.ep, f32[48,24,256]{2,1,0:T(8,128)S(1)} %get-tuple-element.25.em, f32[48,24,256]{2,1,0:T(8,128)S(1)} %get-tuple-element.26.np_, f32[48,24,256]{2,1,0:T(8,128)S(1)} %get-tuple-element.27.nm, ...), custom_call_target="tpu_custom_call" | custom-call | tf_op jit(solution)/shard_map/pallas_call | solution.py:17
Async XLA Ops:
  0.6 1.0 %copy-start = (f32[48,16,128]{2,1,0:T(8,128)S(1)}, f32[48,16,128]{2,1,0:T(8,128)}, u32[]{:S(2)}) copy-start(f32[48,16,128]{2,1,0:T(8,128)} %s.3) | copy-start | bytes 1179652
  1.6 0.9 %copy-start.1 = (bf16[48,16,128]{2,1,0:T(8,128)(2,1)S(1)}, bf16[48,16,128]{2,1,0:T(8,128)(2,1)}, u32[]{:S(2)}) copy-start(bf16[48,16,128]{2,1,0:T(8,128)(2,1)} %es.3) | copy-start | bytes 589828
  2.6 0.9 %copy-start.2 = (bf16[48,16,128]{2,1,0:T(8,128)(2,1)S(1)}, bf16[48,16,128]{2,1,0:T(8,128)(2,1)}, u32[]{:S(2)}) copy-start(bf16[48,16,128]{2,1,0:T(8,128)(2,1)} %ns.3) | copy-start | bytes 589828
  3.5 0.9 %copy-start.3 = (bf16[48,16,128]{2,1,0:T(8,128)(2,1)S(1)}, bf16[48,16,128]{2,1,0:T(8,128)(2,1)}, u32[]{:S(2)}) copy-start(bf16[48,16,128]{2,1,0:T(8,128)(2,1)} %mix.3) | copy-start | bytes 589828
  4.4 0.9 %copy-start.4 = (bf16[48,16,128]{2,1,0:T(8,128)(2,1)S(1)}, bf16[48,16,128]{2,1,0:T(8,128)(2,1)}, u32[]{:S(2)}) copy-start(bf16[48,16,128]{2,1,0:T(8,128)(2,1)} %relax.3) | copy-start | bytes 589828
  5.3 0.9 %copy-start.5 = (bf16[48,16,128]{2,1,0:T(8,128)(2,1)S(1)}, bf16[48,16,128]{2,1,0:T(8,128)(2,1)}, u32[]{:S(2)}) copy-start(bf16[48,16,128]{2,1,0:T(8,128)(2,1)} %obs.3) | copy-start | bytes 589828
  6.3 0.9 %copy-start.6 = (bf16[47,16,128]{2,1,0:T(8,128)(2,1)S(1)}, bf16[47,16,128]{2,1,0:T(8,128)(2,1)}, u32[]{:S(2)}) copy-start(bf16[47,16,128]{2,1,0:T(8,128)(2,1)} %vm.3) | copy-start | bytes 577540
  7.2 0.7 %copy-start.7 = (s32[16,128]{1,0:T(8,128)S(1)}, s32[16,128]{1,0:T(8,128)}, u32[]{:S(2)}) copy-start(s32[16,128]{1,0:T(8,128)} %count.3) | copy-start | bytes 24580
  10.5 14.6 %collective-permute-start.2 = (f32[97,8,128]{2,1,0:T(8,128)S(1)}, f32[97,8,128]{2,1,0:T(8,128)S(1)}, u32[]{:S(2)}, u32[]{:S(2)}) collective-permute-start(f32[97,8,128]{2,1,0:T(8,128)S(1)} %get-tuple-element.22), channel_id=1, source_target_pairs={{0,16},{16,0},{1,17},{17,1},{2,18},{18,2},{3,19},{19,3},{4,20},{20... | collective-permute-start | bytes 1191944 | tf_op jit(solution)/shard_map/ppermute | solution.py:435
  13.6 11.5 %collective-permute-start = (f32[11,16,128]{2,1,0:T(8,128)S(1)}, f32[11,16,128]{2,1,0:T(8,128)S(1)}, u32[]{:S(2)}, u32[]{:S(2)}) collective-permute-start(f32[11,16,128]{2,1,0:T(8,128)S(1)} %get-tuple-element.20), channel_id=1, source_target_pairs={{0,1},{1,0},{2,3},{3,2},{4,5},{5,4},{6,7},{7,6},{8,9},{9,8},{10,11... | collective-permute-start | bytes 270344 | tf_op jit(solution)/shard_map/ppermute | solution.py:448
  13.6 11.5 %collective-permute-start.1 = (f32[11,16,128]{2,1,0:T(8,128)S(1)}, f32[11,16,128]{2,1,0:T(8,128)S(1)}, u32[]{:S(2)}, u32[]{:S(2)}) collective-permute-start(f32[11,16,128]{2,1,0:T(8,128)S(1)} %get-tuple-element.21), channel_id=1, source_target_pairs={{0,15},{1,2},{2,1},{3,4},{4,3},{5,6},{6,5},{7,8},{8,7},{9,10},{10,... | collective-permute-start | bytes 270344 | tf_op jit(solution)/shard_map/ppermute | solution.py:448
  18.2 6.9 %collective-permute-start.4 = (f32[7,8,128]{2,1,0:T(8,128)S(1)}, f32[7,8,128]{2,1,0:T(8,128)S(1)}, u32[]{:S(2)}, u32[]{:S(2)}) collective-permute-start(f32[7,8,128]{2,1,0:T(8,128)S(1)} %get-tuple-element.23), channel_id=1, source_target_pairs={{0,31},{1,18},{2,17},{3,20},{4,19},{5,22},{6,21},{7,24},{8,23},{9,... | collective-permute-start | bytes 86024 | tf_op jit(solution)/shard_map/ppermute | solution.py:448
  18.2 6.9 %collective-permute-start.3 = (f32[7,8,128]{2,1,0:T(8,128)S(1)}, f32[7,8,128]{2,1,0:T(8,128)S(1)}, u32[]{:S(2)}, u32[]{:S(2)}) collective-permute-start(f32[7,8,128]{2,1,0:T(8,128)S(1)} %get-tuple-element.23), channel_id=1, source_target_pairs={{0,17},{1,16},{2,19},{3,18},{4,21},{5,20},{6,23},{7,22},{8,25},{9,... | collective-permute-start | bytes 86024 | tf_op jit(solution)/shard_map/ppermute | solution.py:448
  40.8 4.8 %collective-permute-start.5 = (f32[26,8,128]{2,1,0:T(8,128)S(1)}, f32[26,8,128]{2,1,0:T(8,128)S(1)}, u32[]{:S(2)}, u32[]{:S(2)}) collective-permute-start(f32[26,8,128]{2,1,0:T(8,128)S(1)} %get-tuple-element.37), channel_id=1, source_target_pairs={{0,16},{16,0},{1,17},{17,1},{2,18},{18,2},{3,19},{19,3},{4,20},{20... | collective-permute-start | bytes 319496 | tf_op jit(solution)/shard_map/ppermute | solution.py:435

commit v2 on v1

--- a/solution.py
+++ b/solution.py
@@ -9,17 +9,22 @@
 
 F32 = jnp.float32
 VMEM = pl.BlockSpec(memory_space=pltpu.VMEM)
+HBM = pl.BlockSpec(memory_space=pltpu.HBM)
+UNROLL = 8
 GROUP = 8
 NAMES = ("s", "es", "ns", "mix", "relax", "vm", "obs")
 
 
-def call(kernel, outs, scratch, *args):
+def call(kernel, outs, scratch, *args, space=VMEM):
+    def typed(x):
+        return x if isinstance(x, jax.ShapeDtypeStruct) else jax.ShapeDtypeStruct(x, F32)
+
     return pl.pallas_call(
         kernel,
-        out_shape=[jax.ShapeDtypeStruct(shape, F32) for shape in outs],
-        in_specs=[VMEM] * len(args),
+        out_shape=[typed(x) for x in outs],
+        in_specs=[space] * len(args),
         out_specs=[VMEM] * len(outs),
-        scratch_shapes=[pltpu.VMEM(shape, F32) for shape in scratch],
+        scratch_shapes=[pltpu.VMEM(x, F32) if isinstance(x, tuple) else x for x in scratch],
         compiler_params=pltpu.CompilerParams(vmem_limit_bytes=16 << 20),
     )(*args)
 
@@ -79,7 +84,13 @@
     }
 
 
-def pack_kernel(s, es, ns, mix, relax, vm, obs, count, rows, corners, one, two, planes):
+def pack_kernel(*args):
+    fields = args[:8]
+    s, es, ns, mix, relax, vm, obs, count = kept = args[8:16]
+    rows, corners, one, two, planes, arrived = args[16:]
+    copies = [pltpu.make_async_copy(fields[i], kept[i], arrived.at[i]) for i in range(8)]
+    for copy in copies:
+        copy.start()
     refs = dict(zip(NAMES, (s, es, ns, mix, relax, vm, obs)))
     levels = s.shape[0]
     per_plane = 128 // GROUP
@@ -88,6 +99,8 @@
     group = iota(shape, 1) // GROUP
 
     for a, name in enumerate(NAMES):
+        copies[a].wait()
+
         def columns(p, carry, a=a, name=name):
             acc = jnp.zeros(shape, F32)
             for g in range(per_plane):
@@ -98,6 +111,7 @@
 
         lax.fori_loop(0, plane_count, columns, 0)
     total = len(NAMES) * plane_count
+    copies[7].wait()
     count_plane = count[...].astype(F32)
     planes[total] = roll(count_plane, 4, 1)
     if (total + 1) % 2:
@@ -162,7 +176,7 @@
         return tuple(new)
 
     zero = jnp.zeros(carries.shape[1:], F32)
-    return lax.fori_loop(0, half, step, (zero, zero), unroll=2)
+    return lax.fori_loop(0, half, step, (zero, zero), unroll=UNROLL)
 
 
 def solve_outward(levels, ends, ratio, join, carries, use):
@@ -180,7 +194,7 @@
             new.append(x)
         return tuple(new)
 
-    lax.fori_loop(0, half, step, (lower, upper), unroll=2)
+    lax.fori_loop(0, half, step, (lower, upper), unroll=UNROLL)
 
 
 def merge_halos(odd, from_one, from_two, planes):
@@ -299,7 +313,7 @@
         spread = (fe - shift_down(fe, 1)) + (fn - shift_down(fn, 0))
         return state - spread - sink * jnp.tanh(state)
 
-    lax.fori_loop(0, levels, prepare, 0)
+    lax.fori_loop(0, levels, prepare, 0, unroll=UNROLL)
 
     def factor(t, carry):
         (r_top, c_top), (r_low, c_low) = carry
@@ -329,7 +343,7 @@
 
     zero = jnp.zeros(rhs.shape[1:], F32)
     (r_top, c_top), (r_low, c_low) = lax.fori_loop(
-        0, half, factor, ((zero, zero), (zero, zero)), unroll=2
+        0, half, factor, ((zero, zero), (zero, zero)), unroll=UNROLL
     )
     join = 1.0 / (1.0 - r_top * r_low)
     join_out[...] = join
@@ -416,7 +430,7 @@
         return tuple(new)
 
     zero = jnp.zeros(carries.shape[1:], F32)
-    ends = lax.fori_loop(0, half, late, (zero, zero))
+    ends = lax.fori_loop(0, half, late, (zero, zero), unroll=UNROLL // 2)
 
     def early(k, x):
         result, part = pull(k, x, start[k])
@@ -476,16 +490,18 @@
         level_count,
     )
     corner_planes = 2 * levels // per_plane + 1
-    rows, corners, one, two = call(
+    *fields, rows, corners, one, two = call(
         pack_kernel,
-        [
+        [jax.ShapeDtypeStruct(x.shape, x.dtype) for x in fields]
+        + [
             (2 * levels + 1, 8, nx),
             (corner_planes, 8, nx),
             (pairs, ny, nx),
             (pairs, ny, nx),
         ],
-        [(2 * pairs, ny, nx)],
-        *fields,
+        [(2 * pairs, ny, nx), pltpu.SemaphoreType.DMA((8,))],
+        *[pltpu.with_memory_space_constraint(x, pltpu.HBM) for x in fields],
+        space=HBM,
     )
     rows_n, rows_s = both_ways(rows)
     from_two = swap(two, 1, 0)

time: 54.1 us -> 34.3 us (0.63)
  Pallas kernels: 26.5 us -> 14.1 us
  local copies, waits for them, and re-layouts: 7.24 us -> 0 us
    pallas_call x3, Pallas kernels: 26.5 us -> 14.1 us  [call(): pl.pallas_call(kernel, out_shape=[typed(x) for x in outs], in_specs=[spac...]
    unnamed x16 -> x0, local copies, waits for them, and re-layouts: 7.24 us -> none
where the time goes in v2:
time: 34.3 us; the launch traced here: 34.1 us
  Pallas kernels  14.1 us (41%)
  waiting for transfers between devices  11 us (32%)
  starting transfers between devices  8.36 us (24%)
  between operations  0.67 us (2%)
    pallas_call x3, Pallas kernels, call(): pl.pallas_call(kernel, out_shape=[typed(x) for x in outs], in_specs=[spac...  14.1 us
    ppermute x4, waiting for transfers between devices, swap(): return lax.ppermute(x, ('ty', 'tx'), route)  6.89 us
    ppermute x4, starting transfers between devices, swap(): return lax.ppermute(x, ('ty', 'tx'), route)  4.65 us
    ppermute x2, waiting for transfers between devices, both_ways(): from_north = lax.ppermute(x, 'ty', ring('ty', -1))  4.09 us
    ppermute x2, starting transfers between devices, both_ways(): from_north = lax.ppermute(x, 'ty', ring('ty', -1))  3.71 us
  transfers between devices with their start and end apart: 6, of which 2 were waited for; matrix products, arithmetic and copies ran while one was open for 0% of the time, Pallas kernels for 0%

profile of v2, /device:TPU:0, one launch (start us, length us, event | category | flops | bytes accessed | tf_op | source)
XLA Modules:
  0.0 34.1 jit_solution(14732490810035467646)
XLA Ops:
  0.6 3.7 %shard_map.95 = (f32[48,16,128]{2,1,0:T(8,128)S(1)}, bf16[48,16,128]{2,1,0:T(8,128)(2,1)S(1)}, bf16[48,16,128]{2,1,0:T(8,128)(2,1)S(1)}, bf16[48,16,128]{2,1,0:T...) custom-call(f32[48,16,128]{2,1,0:T(8,128)} %args_0_.4, ...), custom_call_target="tpu_custom_call" | custom-call | tf_op jit(solution)/shard_map/pallas_call | solution.py:22
  4.4 3.0 %collective-permute-start.2 = (f32[97,8,128]{2,1,0:T(8,128)S(1)}, f32[97,8,128]{2,1,0:T(8,128)S(1)}, u32[]{:S(2)}, u32[]{:S(2)}) collective-permute-start(f32[97,8,128]{2,1,0:T(8,128)S(1)} %get-tuple-element.38), channel_id=1, source_target_pairs={{0,16},{16,0},{1,17},{17,1},{2,18},{18,2},{3,19},{19,3},{4,20},{20... | collective-permute-start | bytes 1191944 | tf_op jit(solution)/shard_map/ppermute | solution.py:449
  7.4 0.0 collective-permute-start
  7.4 4.6 %collective-permute-start.1 = (f32[11,16,128]{2,1,0:T(8,128)S(1)}, f32[11,16,128]{2,1,0:T(8,128)S(1)}, u32[]{:S(2)}, u32[]{:S(2)}) collective-permute-start(f32[11,16,128]{2,1,0:T(8,128)S(1)} %get-tuple-element.37), channel_id=1, source_target_pairs={{0,15},{1,2},{2,1},{3,4},{4,3},{5,6},{6,5},{7,8},{8,7},{9,10},{10,... | collective-permute-start | bytes 270344 | tf_op jit(solution)/shard_map/ppermute | solution.py:462
  12.1 0.0 collective-permute-start.4
  12.1 0.0 collective-permute-start.3
  12.1 6.9 %collective-permute-done.4.corner_two_n.corner_two_s = f32[7,8,128]{2,1,0:T(8,128)S(1)} collective-permute-done((f32[7,8,128]{2,1,0:T(8,128)S(1)}, f32[7,8,128]{2,1,0:T(8,128)S(1)}, u32[]{:S(2)}, u32[]{:S(2)}) %collective-permute-start.4) | collective-permute-done | bytes 28704 | tf_op jit(solution)/shard_map/ppermute | solution.py:462
  18.9 0.0 collective-permute-done.3.corner_one_n.corner_one_s
  18.9 0.0 collective-permute-done.from_one
  19.0 0.0 collective-permute-done.1.from_two
  19.0 0.0 collective-permute-done.2.rows_n.rows_s
  19.0 5.7 %shard_map.96 = (f32[48,24,256]{2,1,0:T(8,128)S(1)}, f32[48,24,256]{2,1,0:T(8,128)S(1)}, f32[48,24,256]{2,1,0:T(8,128)S(1)}, f32[48,24,256]{2,1,0:T(8,128)S(1)},...) custom-call(f32[48,16,128]{2,1,0:T(8,128)S(1)} %get-tuple-element.28, ...), custom_call_target="tpu_custom_call" | custom-call | tf_op jit(solution)/shard_map/pallas_call | solution.py:22
  24.7 0.7 %collective-permute-start.5 = (f32[26,8,128]{2,1,0:T(8,128)S(1)}, f32[26,8,128]{2,1,0:T(8,128)S(1)}, u32[]{:S(2)}, u32[]{:S(2)}) collective-permute-start(f32[26,8,128]{2,1,0:T(8,128)S(1)} %get-tuple-element.53), channel_id=1, source_target_pairs={{0,16},{16,0},{1,17},{17,1},{2,18},{18,2},{3,19},{19,3},{4,20},{20... | collective-permute-start | bytes 319496 | tf_op jit(solution)/shard_map/ppermute | solution.py:449
  25.4 4.1 %collective-permute-done.5.rows_n.rows_s = f32[26,8,128]{2,1,0:T(8,128)S(1)} collective-permute-done((f32[26,8,128]{2,1,0:T(8,128)S(1)}, f32[26,8,128]{2,1,0:T(8,128)S(1)}, u32[]{:S(2)}, u32[]{:S(2)}) %collective-permute-start.5) | collective-permute-done | bytes 106528 | tf_op jit(solution)/shard_map/ppermute | solution.py:449
  29.5 4.6 %shard_map.97 = (f32[48,16,128]{2,1,0:T(8,128)}, f32[48,16,128]{2,1,0:T(8,128)}) custom-call(f32[48,24,256]{2,1,0:T(8,128)S(1)} %get-tuple-element.40.ep, f32[48,24,256]{2,1,0:T(8,128)S(1)} %get-tuple-element.41.em, f32[48,24,256]{2,1,0:T(8,128)S(1)} %get-tuple-element.42.np_, f32[48,24,256]{2,1,0:T(8,128)S(1)} %get-tuple-element.43.nm, ...), custom_call_target="tpu_custom_call" | custom-call | tf_op jit(solution)/shard_map/pallas_call | solution.py:22
Async XLA Ops:
  4.4 14.6 %collective-permute-start.2 = (f32[97,8,128]{2,1,0:T(8,128)S(1)}, f32[97,8,128]{2,1,0:T(8,128)S(1)}, u32[]{:S(2)}, u32[]{:S(2)}) collective-permute-start(f32[97,8,128]{2,1,0:T(8,128)S(1)} %get-tuple-element.38), channel_id=1, source_target_pairs={{0,16},{16,0},{1,17},{17,1},{2,18},{18,2},{3,19},{19,3},{4,20},{20... | collective-permute-start | bytes 1191944 | tf_op jit(solution)/shard_map/ppermute | solution.py:449
  7.4 11.5 %collective-permute-start = (f32[11,16,128]{2,1,0:T(8,128)S(1)}, f32[11,16,128]{2,1,0:T(8,128)S(1)}, u32[]{:S(2)}, u32[]{:S(2)}) collective-permute-start(f32[11,16,128]{2,1,0:T(8,128)S(1)} %get-tuple-element.36), channel_id=1, source_target_pairs={{0,1},{1,0},{2,3},{3,2},{4,5},{5,4},{6,7},{7,6},{8,9},{9,8},{10,11... | collective-permute-start | bytes 270344 | tf_op jit(solution)/shard_map/ppermute | solution.py:462
  7.4 11.5 %collective-permute-start.1 = (f32[11,16,128]{2,1,0:T(8,128)S(1)}, f32[11,16,128]{2,1,0:T(8,128)S(1)}, u32[]{:S(2)}, u32[]{:S(2)}) collective-permute-start(f32[11,16,128]{2,1,0:T(8,128)S(1)} %get-tuple-element.37), channel_id=1, source_target_pairs={{0,15},{1,2},{2,1},{3,4},{4,3},{5,6},{6,5},{7,8},{8,7},{9,10},{10,... | collective-permute-start | bytes 270344 | tf_op jit(solution)/shard_map/ppermute | solution.py:462
  12.1 6.9 %collective-permute-start.4 = (f32[7,8,128]{2,1,0:T(8,128)S(1)}, f32[7,8,128]{2,1,0:T(8,128)S(1)}, u32[]{:S(2)}, u32[]{:S(2)}) collective-permute-start(f32[7,8,128]{2,1,0:T(8,128)S(1)} %get-tuple-element.39), channel_id=1, source_target_pairs={{0,31},{1,18},{2,17},{3,20},{4,19},{5,22},{6,21},{7,24},{8,23},{9,... | collective-permute-start | bytes 86024 | tf_op jit(solution)/shard_map/ppermute | solution.py:462
  12.1 6.9 %collective-permute-start.3 = (f32[7,8,128]{2,1,0:T(8,128)S(1)}, f32[7,8,128]{2,1,0:T(8,128)S(1)}, u32[]{:S(2)}, u32[]{:S(2)}) collective-permute-start(f32[7,8,128]{2,1,0:T(8,128)S(1)} %get-tuple-element.39), channel_id=1, source_target_pairs={{0,17},{1,16},{2,19},{3,18},{4,21},{5,20},{6,23},{7,22},{8,25},{9,... | collective-permute-start | bytes 86024 | tf_op jit(solution)/shard_map/ppermute | solution.py:462
  24.7 4.8 %collective-permute-start.5 = (f32[26,8,128]{2,1,0:T(8,128)S(1)}, f32[26,8,128]{2,1,0:T(8,128)S(1)}, u32[]{:S(2)}, u32[]{:S(2)}) collective-permute-start(f32[26,8,128]{2,1,0:T(8,128)S(1)} %get-tuple-element.53), channel_id=1, source_target_pairs={{0,16},{16,0},{1,17},{17,1},{2,18},{18,2},{3,19},{19,3},{4,20},{20... | collective-permute-start | bytes 319496 | tf_op jit(solution)/shard_map/ppermute | solution.py:449

commit v3 on v2

v3 whole, which is shorter than its diff:
```python
import functools

import jax
import jax.numpy as jnp
from jax import lax
from jax.experimental import pallas as pl
from jax.experimental.pallas import tpu as pltpu
from jax.sharding import PartitionSpec as P

F32 = jnp.float32
VMEM = pl.BlockSpec(memory_space=pltpu.VMEM)
HBM = pl.BlockSpec(memory_space=pltpu.HBM)
UNROLL = 8
GROUP = 8
NAMES = ("s", "es", "ns", "mix", "relax", "vm", "obs")


def call(kernel, outs, scratch, *args, space=VMEM, cost=None):
    def typed(x):
        return x if isinstance(x, jax.ShapeDtypeStruct) else jax.ShapeDtypeStruct(x, F32)

    return pl.pallas_call(
        kernel,
        out_shape=[typed(x) for x in outs],
        in_specs=[space] * len(args),
        out_specs=[VMEM] * len(outs),
        scratch_shapes=[pltpu.VMEM(x, F32) if isinstance(x, tuple) else x for x in scratch],
        compiler_params=pltpu.CompilerParams(vmem_limit_bytes=16 << 20),
        cost_estimate=cost,
    )(*args)


def iota(shape, dim):
    return lax.broadcasted_iota(jnp.int32, shape, dim)


def roll(x, shift, axis):
    if isinstance(shift, int):
        shift = shift % x.shape[axis]
        if shift == 0:
            return x
    return pltpu.roll(x, shift, axis)


def odd_column():
    return lax.rem(lax.axis_index("tx"), 2) == 1


def level_of(ref, name, level):
    if name == "vm":
        level = jnp.minimum(level, ref.shape[0] - 1)
    return ref[level].astype(F32)


def edge_rows(block):
    return jnp.where(iota((8, block.shape[1]), 0) < 4, block[:8], block[-8:])


def sublane(shape):
    return iota(shape, 0)


def step_count(counts, axis):
    return jnp.minimum(counts, shift_up(counts, axis))


def pair_rows(first, second):
    sub = sublane(first.shape)
    return jnp.where((sub == 1) | (sub == 2), roll(second, 2, 0), first)


def pack_rows(get, counts, level):
    tile = {name: edge_rows(get(name)) for name in NAMES[:6]}
    s = tile["s"]
    sub = sublane(s.shape)
    open_north = level < step_count(counts, 0)
    fn = jnp.where(
        open_north,
        (0.5 * tile["ns"] + tile["mix"]) * s + (0.5 * tile["ns"] - tile["mix"]) * shift_up(s, 0),
        0.0,
    )
    sink = jnp.where(level < counts, tile["relax"], 0.0)
    inner = jnp.where(sub == 0, -fn, jnp.where(sub == 7, shift_down(fn, 0), 0.0))
    base = s - sink * jnp.tanh(s) + inner
    first = pair_rows(s, base)
    first = jnp.where((sub == 3) | (sub == 4), roll(tile["es"], 4, 0), first)
    first = jnp.where((sub == 5) | (sub == 6), roll(tile["mix"], 6, 0), first)
    return first, pair_rows(tile["vm"], tile["ns"])


def unpack_rows(first, second):
    return {
        "s": first,
        "base": roll(first, 6, 0),
        "es": roll(first, 4, 0),
        "mix": roll(first, 2, 0),
        "vm": second,
        "ns": roll(second, 6, 0),
    }


def two_levels(x, y):
    sub = sublane(x.shape)
    return jnp.where((sub >= 3) & (sub <= 6), roll(y, 4, 0), x)


def shift_up(x, axis):
    return roll(x, -1, axis)


def shift_down(x, axis):
    return roll(x, 1, axis)


def rim_kernel(*args):
    fields = args[:8]
    s, es, ns, mix, relax, vm, obs, count = kept = args[8:16]
    rows, corners, arrived = args[16:]
    copies = [pltpu.make_async_copy(fields[i], kept[i], arrived.at[i]) for i in range(8)]
    for copy in copies:
        copy.start()
    for copy in copies:
        copy.wait()
    refs = dict(zip(NAMES, (s, es, ns, mix, relax, vm, obs)))
    levels = s.shape[0]
    per_plane = 128 // GROUP
    small = (8, s.shape[2])
    group = iota(small, 1) // GROUP
    half = per_plane // 2
    count_planes = levels // per_plane
    counts = edge_rows(count[...].astype(F32))

    def rims(p, carry):
        acc = jnp.zeros(small, F32)
        late = jnp.zeros(small, F32)
        for g in range(0, per_plane, 2):
            tiles = []
            for level in (p * per_plane + g, p * per_plane + g + 1):
                tiles.append(
                    pack_rows(
                        lambda name: level_of(refs[name], name, level), counts, level.astype(F32)
                    )
                )
            half_tile = two_levels(tiles[0][1], tiles[1][1])
            h = g // 2
            rows[levels + p * half + h] = half_tile
            late = jnp.where(group == h, roll(half_tile, GROUP * h + 4, 1), late)
            for q in range(2):
                rows[p * per_plane + g + q] = tiles[q][0]
                acc = jnp.where(
                    group == g + q, roll(tiles[q][0], GROUP * (g + q) + 4, 1), acc
                )
        corners[p] = acc
        corners[count_planes + p] = late
        return carry

    lax.fori_loop(0, count_planes, rims, 0)
    rows[levels + levels // 2] = counts
    corners[2 * count_planes] = roll(counts, 4, 1)
    for p in range(2 * count_planes + 1, corners.shape[0]):
        corners[p] = jnp.zeros(small, F32)


def column_kernel(s, es, ns, mix, relax, vm, obs, count, planes):
    refs = dict(zip(NAMES, (s, es, ns, mix, relax, vm, obs)))
    levels = s.shape[0]
    per_plane = 128 // GROUP
    plane_count = levels // per_plane
    shape = s.shape[1:]
    group = iota(shape, 1) // GROUP

    def columns(p, carry):
        for a, name in enumerate(NAMES):
            acc = jnp.zeros(shape, F32)
            for g in range(per_plane):
                x = level_of(refs[name], name, p * per_plane + g)
                acc = jnp.where(group == g, roll(x, GROUP * g + 4, 1), acc)
            planes[a * plane_count + p] = acc
        return carry

    lax.fori_loop(0, plane_count, columns, 0)
    total = len(NAMES) * plane_count
    planes[total] = roll(count[...].astype(F32), 4, 1)
    for p in range(total + 1, planes.shape[0]):
        planes[p] = jnp.zeros(shape, F32)


def merge_rows(north, south):
    return jnp.where(sublane(north.shape) % 2 == 0, north, south)


def halves_kernel(planes, corners_n, corners_s, rows, one, two, rows_out):
    odd = odd_column()
    pairs = planes.shape[0] // 2
    ny = planes.shape[1]

    def put(place, x, y):
        low = iota(x.shape, 1) % GROUP < 4
        to_east = jnp.where(low, x, roll(y, 4, 1))
        to_west = jnp.where(low, roll(x, -4, 1), y)
        one[place] = jnp.where(odd, to_west, to_east)
        two[place] = jnp.where(odd, to_east, to_west)

    for h in range(pairs):
        put(pl.ds(h * ny, ny), planes[2 * h], planes[2 * h + 1])

    count = corners_n.shape[0]
    rows_out[...] = rows[...]
    two[pl.ds(one.shape[0], 8)] = jnp.zeros((8, one.shape[1]), F32)

    def corner(p):
        return merge_rows(corners_n[p], corners_s[p])

    for h in range(count // 2):
        put(pl.ds(pairs * ny + h * 8, 8), corner(2 * h), corner(2 * h + 1))


def extend(main, side, rows=None, corners=None):
    top = jnp.concatenate([main, side], axis=1)
    if rows is None:
        return top
    return jnp.concatenate([top, jnp.concatenate([rows, corners], axis=1)], axis=0)


def solve_inward(levels, get, inv_q, carries):
    half = levels // 2
    inv, q = inv_q

    def step(t, carry):
        new = []
        for k, last in ((t, carry[0]), (levels - 1 - t, carry[1])):
            c = get(k) * inv(k) + q(k) * last
            carries[k] = c
            new.append(c)
        return tuple(new)

    zero = jnp.zeros(carries.shape[1:], F32)
    return lax.fori_loop(0, half, step, (zero, zero), unroll=UNROLL)


def solve_outward(levels, ends, ratio, join, carries, use):
    half = levels // 2
    high, low = ends
    upper = (high + ratio(half - 1) * low) * join
    lower = (low + ratio(half) * high) * join

    def step(t, carry):
        t = half - 1 - t
        new = []
        for k, last in ((t, carry[0]), (levels - 1 - t, carry[1])):
            x = carries[k] + ratio(k) * last
            use(k, x)
            new.append(x)
        return tuple(new)

    lax.fori_loop(0, half, step, (lower, upper), unroll=UNROLL)


def merge_halos(odd, from_one, from_two, planes, start):
    size = planes.shape[1]
    low = iota(planes.shape[1:], 1) % GROUP < 4
    for h in range(planes.shape[0] // 2):
        place = pl.ds(start + h * size, size)
        a, b = from_one[place], from_two[place]
        west = jnp.where(odd, a, b)
        east = jnp.where(odd, b, a)
        planes[2 * h] = jnp.where(low, west, roll(east, 4, 1))
        planes[2 * h + 1] = jnp.where(low, roll(west, -4, 1), east)


def part_of_pull(x, ep, em, damp):
    ge = shift_up(x, 1) - x
    return x * damp + ep * ge + shift_down(em * ge, 1), ge


def forward_kernel(
    s, es, ns, mix, relax, vm, obs, count, from_one, from_two, rows_n, rows_s,
    ep_out, em_out, np_out, nm_out, sink_out, inv_out, q_out, r_out, middle_out, damp_out,
    solved_out, counts_out, join_out, start_out, send,
    planes, corners, rhs, links, carries,
):
    refs = dict(zip(NAMES, (s, es, ns, mix, relax, vm, obs)))
    levels, ny, nx = s.shape
    half = levels // 2
    per_plane = 128 // GROUP
    plane_count = levels // per_plane
    odd = odd_column()
    merge_halos(odd, from_one, from_two, planes, 0)
    merge_halos(odd, from_one, from_two, corners, planes.shape[0] // 2 * planes.shape[1])

    def rim(index):
        return merge_rows(rows_n[index], rows_s[index])

    count_ext = extend(
        count[...].astype(F32),
        roll(planes[len(NAMES) * plane_count], 124, 1),
        rim(levels + half),
        roll(corners[2 * plane_count], 124, 1),
    )
    east_count = step_count(count_ext, 1)
    sub = sublane(count_ext.shape)
    north_count = jnp.where(
        (sub < ny) | (sub == ny + 7), step_count(count_ext, 0), 0.0
    )
    counts_out[0] = count_ext
    counts_out[1] = east_count
    counts_out[2] = north_count

    def side_of(name, k):
        p = NAMES.index(name) * plane_count + k // per_plane
        return roll(planes[p], 124 - GROUP * (k % per_plane), 1)

    def rim_ext(index, plane, group):
        corner = roll(corners[plane], 124 - GROUP * group, 1)
        return jnp.concatenate([rim(index), corner], axis=1)

    def prepare(m, carry):
        later = rim_ext(
            levels + m,
            plane_count + m // (per_plane // 2),
            m % (per_plane // 2),
        )
        for q in range(2):
            k = 2 * m + q
            first = rim_ext(k, k // per_plane, k % per_plane)
            x = unpack_rows(first, roll(later, 4, 0) if q else later)
            for name in NAMES[:4] + NAMES[5:6]:
                x[name] = jnp.concatenate(
                    [extend(level_of(refs[name], name, k), side_of(name, k)), x[name]], axis=0
                )
            level = k.astype(F32)
            state = x["s"]
            open_east = level < east_count
            open_north = level < north_count
            ep = jnp.where(open_east, 0.5 * x["es"] + x["mix"], 0.0)
            em = jnp.where(open_east, 0.5 * x["es"] - x["mix"], 0.0)
            np_ = jnp.where(open_north, 0.5 * x["ns"] + x["mix"], 0.0)
            nm = jnp.where(open_north, 0.5 * x["ns"] - x["mix"], 0.0)
            inner = state[:ny]
            sink = extend(level_of(refs["relax"], "relax", k), side_of("relax", k))
            sink = jnp.where(level < count_ext[:ny], sink, 0.0)
            link = jnp.where(level + 1.0 < count_ext, x["vm"], 0.0)
            squeeze = jnp.tanh(inner)
            base = jnp.concatenate([inner - sink * squeeze, x["base"]], axis=0)
            ep_out[k] = ep
            em_out[k] = em
            np_out[k] = np_
            nm_out[k] = nm
            sink_out[k] = sink
            links[k] = link
            start_out[k] = state
            damp_out[k] = 1.0 - sink * (1.0 - squeeze * squeeze)
            rhs[k] = base - spread(state, ep, em, np_, nm)
        return carry

    def spread(state, ep, em, np_, nm):
        fe = ep * state + em * shift_up(state, 1)
        fn = np_ * state + nm * shift_up(state, 0)
        return (fe - shift_down(fe, 1)) + (fn - shift_down(fn, 0))

    lax.fori_loop(0, half, prepare, 0, unroll=UNROLL // 2)

    def factor(t, carry):
        (r_top, c_top), (r_low, c_low) = carry
        k = t
        above = jnp.where(k > 0, links[jnp.maximum(k - 1, 0)], 0.0)
        below = links[k]
        inv = 1.0 / (1.0 + above + below - above * r_top)
        q = above * inv
        r_top = below * inv
        c_top = rhs[k] * inv + q * c_top
        inv_out[k] = inv
        q_out[k] = q
        r_out[k] = r_top
        carries[k] = c_top
        k = levels - 1 - t
        above = links[k - 1]
        below = links[k]
        inv = 1.0 / (1.0 + above + below - below * r_low)
        q = below * inv
        r_low = above * inv
        c_low = rhs[k] * inv + q * c_low
        inv_out[k] = inv
        q_out[k] = q
        r_out[k] = r_low
        carries[k] = c_low
        return (r_top, c_top), (r_low, c_low)

    zero = jnp.zeros(rhs.shape[1:], F32)
    (r_top, c_top), (r_low, c_low) = lax.fori_loop(
        0, half, factor, ((zero, zero), (zero, zero)), unroll=UNROLL
    )
    join = 1.0 / (1.0 - r_top * r_low)
    join_out[...] = join

    def to_second(k, x):
        middle_out[k] = x
        inner = x[:ny]
        squeeze = jnp.tanh(inner)
        sink = sink_out[k]
        damp_out[levels + k] = 1.0 - sink * (1.0 - squeeze * squeeze)
        flow = spread(x, ep_out[k], em_out[k], np_out[k], nm_out[k])
        rhs[k, :ny] = inner - flow[:ny] - sink * squeeze

    solve_outward(levels, (c_top, c_low), lambda k: r_out[k], join, carries, to_second)

    main = carries.at[:, :ny]
    inv_q = (lambda k: inv_out[k, :ny], lambda k: q_out[k, :ny])
    ratio = lambda k: r_out[k, :ny]
    ends = solve_inward(levels, lambda k: rhs[k, :ny], inv_q, main)

    def to_adjoint(k, x):
        seen = extend(level_of(refs["obs"], "obs", k), side_of("obs", k))
        rhs[k, :ny] = jnp.where(k.astype(F32) < count_ext[:ny], x - seen, 0.0)

    solve_outward(levels, ends, ratio, join[:ny], main, to_adjoint)
    ends = solve_inward(levels, lambda k: rhs[k, :ny], inv_q, main)

    def to_solved(k, x):
        solved_out[k] = x

    solve_outward(levels, ends, ratio, join[:ny], main, to_solved)

    def rim_part(k):
        x = edge_rows(solved_out[k])
        edge = lambda ref: edge_rows(ref[k, :ny])
        part, _ = part_of_pull(x, edge(ep_out), edge(em_out), edge_rows(damp_out[levels + k]))
        gn = shift_up(x, 0) - x
        sub = sublane(x.shape)
        part = part + jnp.where(
            sub == 0,
            edge(np_out) * gn,
            jnp.where(sub == 7, shift_down(edge(nm_out) * gn, 0), 0.0),
        )
        return pair_rows(x, part)

    group = iota((8, nx), 1) // GROUP

    def rims(p, carry):
        acc = jnp.zeros((8, nx), F32)
        for g in range(8):
            t = p * 8 + g
            both = two_levels(rim_part(t), rim_part(levels - 1 - t))
            send[t] = both[:, :nx]
            acc = jnp.where(group == g, roll(both[:, nx:], GROUP * g + 4, 1), acc)
        send[half + p] = acc
        return carry

    lax.fori_loop(0, half // 8, rims, 0)


def inner_kernel(
    ep, em, np_, nm, damp, middle, solved, counts, part_out, late_out,
):
    levels, ny, width = solved.shape
    nx = width // 2
    sub = sublane((ny, width))
    inside = sub < ny - 1

    def inner(k, carry):
        x = solved[k]
        state = middle[k]
        part, ge = part_of_pull(x, ep[k, :ny], em[k, :ny], damp[levels + k])
        gn = jnp.where(inside, shift_up(x, 0) - x, 0.0)
        part_out[k] = part + np_[k, :ny] * gn + shift_down(nm[k, :ny] * gn, 0)
        level = k.astype(F32)
        rise = shift_up(state, 0)[:ny, :nx] - state[:ny, :nx]
        run = (shift_up(state[:ny], 1) - state[:ny])[:, :nx]
        late_out[k] = jnp.where(level < counts[1, :ny, :nx], ge[:, :nx] * run, 0.0) + jnp.where(
            level < counts[2, :ny, :nx], gn[:, :nx] * rise, 0.0
        )
        return carry

    lax.fori_loop(0, levels, inner, 0, unroll=UNROLL)


def backward_kernel(
    ep, em, np_, nm, inv, q, r, middle, damp, solved, counts, join, start, part, late,
    rows_n, rows_s,
    adjoint_out, gradient_out, carries,
):
    levels, ny, width = solved.shape
    nx = width // 2
    half = levels // 2
    sub = sublane((8, width))

    def rims(t):
        line = merge_rows(rows_n[t], rows_s[t])
        p = half + t // 8
        corner = roll(merge_rows(rows_n[p], rows_s[p]), 124 - GROUP * (t % 8), 1)
        both = jnp.concatenate([line, corner], axis=1)
        return both, roll(both, 4, 0)

    def across(k, rim):
        inner = part[k]
        near_part = roll(rim, 6, 0)
        south = solved[k, :8] - shift_down(rim, 0)
        north = shift_up(rim, 0) - solved[k, ny - 8 :]
        np_rim, nm_rim = np_[k, ny:], nm[k, ny:]
        np_top, nm_top = np_[k, ny - 8 : ny], nm[k, ny - 8 : ny]
        low = inner[:8] + jnp.where(sub == 0, shift_down(nm_rim, 0) * south, 0.0)
        high = inner[ny - 8 :] + jnp.where(sub == 7, np_top * north, 0.0)
        outer = near_part + jnp.where(
            sub == 0, shift_down(nm_top * north, 0), np_rim * shift_up(south, 0)
        )
        rise = (shift_up(middle[k, ny:], 0) - middle[k, ny - 8 : ny])[:, :nx]
        open_north = (sub[:, :nx] == 7) & (k.astype(F32) < counts[2, ny - 8 : ny, :nx])
        extra = jnp.where(open_north, north[:, :nx] * rise, 0.0)
        gradient_out[k, : ny - 8] = late[k, : ny - 8]
        gradient_out[k, ny - 8 :] = late[k, ny - 8 :] + extra
        middle_rows = [inner[8 : ny - 8]] if ny > 16 else []
        return jnp.concatenate([low, *middle_rows, high, outer], axis=0)

    def late_step(t, carry):
        new = []
        for k, rim, last in zip((t, levels - 1 - t), rims(t), carry):
            c = across(k, rim) * inv[k] + q[k] * last
            carries[k] = c
            new.append(c)
        return tuple(new)

    zero = jnp.zeros(carries.shape[1:], F32)
    ends = lax.fori_loop(0, half, late_step, (zero, zero), unroll=UNROLL // 2)

    def early(k, x):
        state = start[k]
        inner = x[:ny]
        east = shift_up(inner, 1)
        ge = east - inner
        result = inner[:, :nx] * damp[k, :, :nx] + (ep[k, :ny] * ge)[:, :nx]
        result = result + shift_down(em[k, :ny] * ge, 1)[:, :nx]
        column = x[:, :nx]
        gn = shift_up(column, 0) - column
        result = result + (np_[k, :, :nx] * gn + shift_down(nm[k, :, :nx] * gn, 0))[:ny]
        adjoint_out[k] = result
        level = k.astype(F32)
        run = (shift_up(state[:ny], 1) - state[:ny])[:, :nx]
        rise = (shift_up(state[:, :nx], 0) - state[:, :nx])[:ny]
        gradient_out[k] = -(
            gradient_out[k]
            + jnp.where(level < counts[1, :ny, :nx], ge[:, :nx] * run, 0.0)
            + jnp.where(level < counts[2, :ny, :nx], gn[:ny] * rise, 0.0)
        )

    solve_outward(levels, ends, lambda k: r[k], join[...], carries, early)


def ring(axis, distance):
    count = lax.axis_size(axis)
    return [(i, (i + distance) % count) for i in range(count)]


def both_ways(x):
    from_north = lax.ppermute(x, "ty", ring("ty", -1))
    if lax.axis_size("ty") == 2:
        return from_north, from_north
    return from_north, lax.ppermute(x, "ty", ring("ty", 1))


def swap(x, phase):
    nx = lax.axis_size("tx")
    return lax.ppermute(
        x, "tx", [(i, (i + 1) % nx if i % 2 == phase else (i - 1) % nx) for i in range(nx)]
    )


def per_device(
    tracer_start,
    observed,
    east_speed,
    north_speed,
    mixing,
    vertical_mixing,
    relax_rate,
    level_count,
    face_east,
    face_north,
):
    levels, ny, nx = tracer_start.shape
    per_plane = 128 // GROUP
    plane_count = levels // per_plane
    pairs = (len(NAMES) * plane_count + 2) // 2
    fields = (
        tracer_start, east_speed, north_speed, mixing, relax_rate, vertical_mixing, observed,
        level_count,
    )
    half = levels // 2
    corner_planes = 2 * plane_count + 2
    *fields, rows, corners = call(
        rim_kernel,
        [jax.ShapeDtypeStruct(x.shape, x.dtype) for x in fields]
        + [(levels + half + 1, 8, nx), (corner_planes, 8, nx)],
        [pltpu.SemaphoreType.DMA((8,))],
        *[pltpu.with_memory_space_constraint(x, pltpu.HBM) for x in fields],
        space=HBM,
    )
    corners_n, corners_s = both_ways(corners)
    (planes,) = call(column_kernel, [(2 * pairs, ny, nx)], [], *fields)
    packed = (pairs * ny + corner_planes // 2 * 8, nx)
    one, two, rows = call(
        halves_kernel,
        [packed, (packed[0] + 8, nx), rows.shape],
        [],
        planes,
        corners_n,
        corners_s,
        rows,
    )
    from_two = swap(two, 1)
    rows_n, rows_s = both_ways(rows)
    from_one = swap(one, 0)
    ext = (levels, ny + 8, 2 * nx)
    block = (levels, ny, 2 * nx)
    outs = call(
        forward_kernel,
        [ext] * 4 + [block] + [ext] * 4
        + [(2 * levels, ny, 2 * nx), block, (3,) + ext[1:], ext[1:], ext]
        + [(half + half // 8, 8, nx)],
        [(2 * pairs, ny, nx), (corner_planes, 8, nx), ext, ext, ext],
        *fields, from_one, from_two, rows_n, rows_s,
    )
    ep, em, np_, nm, _, inv, q, r, middle, damp, solved, counts, join, start, send = outs
    sent_n, sent_s = both_ways(send)
    part, late = call(
        inner_kernel,
        [block, (levels, ny, nx)],
        [],
        ep, em, np_, nm, damp, middle, solved, counts,
        cost=pl.CostEstimate(flops=0, bytes_accessed=8 << 20, transcendentals=0),
    )
    adjoint, gradient = call(
        backward_kernel,
        [(levels, ny, nx)] * 2,
        [ext],
        ep, em, np_, nm, inv, q, r, middle, damp, solved, counts, join, start, part, late,
        sent_n, sent_s,
    )
    return adjoint, gradient


def solution(mesh):
    block = P(None, "ty", "tx")
    plane = P("ty", "tx")
    return jax.shard_map(
        per_device,
        mesh=mesh,
        in_specs=(block,) * 7 + (plane,) * 3,
        out_specs=(block, block),
        check_vma=False,
    )
```

time: 34.3 us -> 32 us (0.933)
  waiting for transfers between devices: 11 us -> 8.17 us
  Pallas kernels: 14.1 us -> 14.5 us
    ppermute x4 -> x2, waiting for transfers between devices: 6.89 us -> 4.33 us  [swap(): lax.ppermute(x, 'tx', [(i, (i + 1) % nx if i % 2 == phase else (i - 1) %...]
    ppermute x2 -> x3, starting transfers between devices: 3.71 us -> 5.93 us  [both_ways(): from_north = lax.ppermute(x, 'ty', ring('ty', -1))]
    ppermute x4 -> x2, starting transfers between devices: 4.65 us -> 2.54 us  [swap(): lax.ppermute(x, 'tx', [(i, (i + 1) % nx if i % 2 == phase else (i - 1) %...]
    pallas_call x3 -> x6, Pallas kernels: 14.1 us -> 14.5 us  [call(): pl.pallas_call(kernel, out_shape=[typed(x) for x in outs], in_specs=[spac...]
    ppermute x2 -> x3, waiting for transfers between devices: 4.09 us -> 3.84 us  [both_ways(): from_north = lax.ppermute(x, 'ty', ring('ty', -1))]
  transfers between devices with their start and end apart: 6 -> 5, of which waited for: 2 -> 4; matrix products, arithmetic and copies ran while one was open for 0% -> 0% of each run, Pallas kernels for 0% -> 6%
where the time goes in v3:
time: 32 us; the launch traced here: 31.8 us
  Pallas kernels  14.5 us (45%)
  starting transfers between devices  8.47 us (26%)
  waiting for transfers between devices  8.17 us (26%)
  between operations  0.66 us (2%)
    pallas_call x6, Pallas kernels, call(): pl.pallas_call(kernel, out_shape=[typed(x) for x in outs], in_specs=[spac...  14.5 us
    ppermute x3, starting transfers between devices, both_ways(): from_north = lax.ppermute(x, 'ty', ring('ty', -1))  5.93 us
    ppermute x2, waiting for transfers between devices, swap(): lax.ppermute(x, 'tx', [(i, (i + 1) % nx if i % 2 == phase else (i - 1) %...  4.33 us
    ppermute x3, waiting for transfers between devices, both_ways(): from_north = lax.ppermute(x, 'ty', ring('ty', -1))  3.84 us
    ppermute x2, starting transfers between devices, swap(): lax.ppermute(x, 'tx', [(i, (i + 1) % nx if i % 2 == phase else (i - 1) %...  2.54 us
  transfers between devices with their start and end apart: 5, of which 4 were waited for; matrix products, arithmetic and copies ran while one was open for 0% of the time, Pallas kernels for 6%

profile of v3, /device:TPU:0, one launch (start us, length us, event | category | flops | bytes accessed | tf_op | source)
XLA Modules:
  0.0 31.8 jit_solution(2336011150039507735)
XLA Ops:
  0.6 2.0 %shard_map.95 = (f32[48,16,128]{2,1,0:T(8,128)S(1)}, bf16[48,16,128]{2,1,0:T(8,128)(2,1)S(1)}, bf16[48,16,128]{2,1,0:T(8,128)(2,1)S(1)}, bf16[48,16,128]{2,1,0:T...) custom-call(f32[48,16,128]{2,1,0:T(8,128)} %args_0_.4, ...), custom_call_target="tpu_custom_call" | custom-call | tf_op jit(solution)/shard_map/pallas_call | solution.py:22
  2.6 3.0 %collective-permute-start = (f32[8,8,128]{2,1,0:T(8,128)S(1)}, f32[8,8,128]{2,1,0:T(8,128)S(1)}, u32[]{:S(2)}, u32[]{:S(2)}) collective-permute-start(f32[8,8,128]{2,1,0:T(8,128)S(1)} %get-tuple-element.39), channel_id=1, source_target_pairs={{0,16},{16,0},{1,17},{17,1},{2,18},{18,2},{3,19},{19,3},{4,20},{20... | collective-permute-start | bytes 98312 | tf_op jit(solution)/shard_map/ppermute | solution.py:554
  5.6 0.7 %shard_map.96.planes = f32[22,16,128]{2,1,0:T(8,128)S(1)} custom-call(f32[48,16,128]{2,1,0:T(8,128)S(1)} %get-tuple-element.31.s, bf16[48,16,128]{2,1,0:T(8,128)(2,1)S(1)} %get-tuple-element.32.es, bf16[48,16,128]{2,1,0:T(8,128)(2,1)S(1)} %get-tuple-element.33.ns, bf16[48,16,128]{2,1,0:T(8,128)(2,1)S(1)} %get-tuple-element.34.mix, ...), custom_call_target="tpu_custom_call" | custom-call | tf_op jit(solution)/shard_map/pallas_call | solution.py:22
  6.3 1.2 %collective-permute-done.corners_n.corners_s = f32[8,8,128]{2,1,0:T(8,128)S(1)} collective-permute-done((f32[8,8,128]{2,1,0:T(8,128)S(1)}, f32[8,8,128]{2,1,0:T(8,128)S(1)}, u32[]{:S(2)}, u32[]{:S(2)}) %collective-permute-start) | collective-permute-done | bytes 32800 | tf_op jit(solution)/shard_map/ppermute | solution.py:554
  7.5 0.1 shard_map.97
  7.7 2.1 %collective-permute-start.3 = (f32[73,8,128]{2,1,0:T(8,128)S(1)}, f32[73,8,128]{2,1,0:T(8,128)S(1)}, u32[]{:S(2)}, u32[]{:S(2)}) collective-permute-start(f32[73,8,128]{2,1,0:T(8,128)S(1)} %get-tuple-element.43), channel_id=1, source_target_pairs={{0,16},{16,0},{1,17},{17,1},{2,18},{18,2},{3,19},{19,3},{4,20},{20... | collective-permute-start | bytes 897032 | tf_op jit(solution)/shard_map/ppermute | solution.py:554
  9.8 2.5 %collective-permute-start.2 = (f32[216,128]{1,0:T(8,128)S(1)}, f32[216,128]{1,0:T(8,128)S(1)}, u32[]{:S(2)}, u32[]{:S(2)}) collective-permute-start(f32[216,128]{1,0:T(8,128)S(1)} %get-tuple-element.42), channel_id=1, source_target_pairs={{0,15},{1,2},{2,1},{3,4},{4,3},{5,6},{6,5},{7,8},{8,7},{9,10},{10,... | collective-permute-start | bytes 331784 | tf_op jit(solution)/shard_map/ppermute | solution.py:562
  12.3 0.0 collective-permute-start.1
  12.3 1.3 %collective-permute-done.1.from_one = f32[208,128]{1,0:T(8,128)S(1)} collective-permute-done((f32[208,128]{1,0:T(8,128)S(1)}, f32[208,128]{1,0:T(8,128)S(1)}, u32[]{:S(2)}, u32[]{:S(2)}) %collective-permute-start.1) | collective-permute-done | bytes 106528 | tf_op jit(solution)/shard_map/ppermute | solution.py:562
  13.6 3.0 %collective-permute-done.2.from_two = f32[216,128]{1,0:T(8,128)S(1)} collective-permute-done((f32[216,128]{1,0:T(8,128)S(1)}, f32[216,128]{1,0:T(8,128)S(1)}, u32[]{:S(2)}, u32[]{:S(2)}) %collective-permute-start.2) | collective-permute-done | bytes 110624 | tf_op jit(solution)/shard_map/ppermute | solution.py:562
  16.6 0.0 collective-permute-done.3.rows_n.rows_s
  16.6 7.2 %shard_map.98 = (f32[48,24,256]{2,1,0:T(8,128)S(1)}, f32[48,24,256]{2,1,0:T(8,128)S(1)}, f32[48,24,256]{2,1,0:T(8,128)S(1)}, f32[48,24,256]{2,1,0:T(8,128)S(1)},...) custom-call(f32[48,16,128]{2,1,0:T(8,128)S(1)} %get-tuple-element.31, ...), custom_call_target="tpu_custom_call" | custom-call | tf_op jit(solution)/shard_map/pallas_call | solution.py:22
  23.8 0.8 %collective-permute-start.4 = (f32[27,8,128]{2,1,0:T(8,128)S(1)}, f32[27,8,128]{2,1,0:T(8,128)S(1)}, u32[]{:S(2)}, u32[]{:S(2)}) collective-permute-start(f32[27,8,128]{2,1,0:T(8,128)S(1)} %get-tuple-element.59), channel_id=1, source_target_pairs={{0,16},{16,0},{1,17},{17,1},{2,18},{18,2},{3,19},{19,3},{4,20},{20... | collective-permute-start | bytes 331784 | tf_op jit(solution)/shard_map/ppermute | solution.py:554
  24.6 1.3 %shard_map.99 = (f32[48,16,256]{2,1,0:T(8,128)S(1)}, f32[48,16,128]{2,1,0:T(8,128)S(1)}) custom-call(f32[48,24,256]{2,1,0:T(8,128)S(1)} %get-tuple-element.44.ep, f32[48,24,256]{2,1,0:T(8,128)S(1)} %get-tuple-element.45.em, f32[48,24,256]{2,1,0:T(8,128)S(1)} %get-tuple-element.46.np_, f32[48,24,256]{2,1,0:T(8,128)S(1)} %get-tuple-element.47.nm, ...), custom_call_target="tpu_custom_call" | custom-call | bytes 8388608 | tf_op jit(solution)/shard_map/pallas_call | solution.py:22
  25.9 2.6 %collective-permute-done.4.rows_n.rows_s = f32[27,8,128]{2,1,0:T(8,128)S(1)} collective-permute-done((f32[27,8,128]{2,1,0:T(8,128)S(1)}, f32[27,8,128]{2,1,0:T(8,128)S(1)}, u32[]{:S(2)}, u32[]{:S(2)}) %collective-permute-start.4) | collective-permute-done | bytes 110624 | tf_op jit(solution)/shard_map/ppermute | solution.py:554
  28.6 3.3 %shard_map.100 = (f32[48,16,128]{2,1,0:T(8,128)}, f32[48,16,128]{2,1,0:T(8,128)}) custom-call(f32[48,24,256]{2,1,0:T(8,128)S(1)} %get-tuple-element.44.ep, f32[48,24,256]{2,1,0:T(8,128)S(1)} %get-tuple-element.45.em, f32[48,24,256]{2,1,0:T(8,128)S(1)} %get-tuple-element.46.np_, f32[48,24,256]{2,1,0:T(8,128)S(1)} %get-tuple-element.47.nm, ...), custom_call_target="tpu_custom_call" | custom-call | tf_op jit(solution)/shard_map/pallas_call | solution.py:22
Async XLA Ops:
  2.6 4.9 %collective-permute-start = (f32[8,8,128]{2,1,0:T(8,128)S(1)}, f32[8,8,128]{2,1,0:T(8,128)S(1)}, u32[]{:S(2)}, u32[]{:S(2)}) collective-permute-start(f32[8,8,128]{2,1,0:T(8,128)S(1)} %get-tuple-element.39), channel_id=1, source_target_pairs={{0,16},{16,0},{1,17},{17,1},{2,18},{18,2},{3,19},{19,3},{4,20},{20... | collective-permute-start | bytes 98312 | tf_op jit(solution)/shard_map/ppermute | solution.py:554
  7.7 9.0 %collective-permute-start.3 = (f32[73,8,128]{2,1,0:T(8,128)S(1)}, f32[73,8,128]{2,1,0:T(8,128)S(1)}, u32[]{:S(2)}, u32[]{:S(2)}) collective-permute-start(f32[73,8,128]{2,1,0:T(8,128)S(1)} %get-tuple-element.43), channel_id=1, source_target_pairs={{0,16},{16,0},{1,17},{17,1},{2,18},{18,2},{3,19},{19,3},{4,20},{20... | collective-permute-start | bytes 897032 | tf_op jit(solution)/shard_map/ppermute | solution.py:554
  9.8 6.9 %collective-permute-start.2 = (f32[216,128]{1,0:T(8,128)S(1)}, f32[216,128]{1,0:T(8,128)S(1)}, u32[]{:S(2)}, u32[]{:S(2)}) collective-permute-start(f32[216,128]{1,0:T(8,128)S(1)} %get-tuple-element.42), channel_id=1, source_target_pairs={{0,15},{1,2},{2,1},{3,4},{4,3},{5,6},{6,5},{7,8},{8,7},{9,10},{10,... | collective-permute-start | bytes 331784 | tf_op jit(solution)/shard_map/ppermute | solution.py:562
  12.3 1.3 %collective-permute-start.1 = (f32[208,128]{1,0:T(8,128)S(1)}, f32[208,128]{1,0:T(8,128)S(1)}, u32[]{:S(2)}, u32[]{:S(2)}) collective-permute-start(f32[208,128]{1,0:T(8,128)S(1)} %get-tuple-element.41), channel_id=1, source_target_pairs={{0,1},{1,0},{2,3},{3,2},{4,5},{5,4},{6,7},{7,6},{8,9},{9,8},{10,11... | collective-permute-start | bytes 319496 | tf_op jit(solution)/shard_map/ppermute | solution.py:562
  23.8 4.7 %collective-permute-start.4 = (f32[27,8,128]{2,1,0:T(8,128)S(1)}, f32[27,8,128]{2,1,0:T(8,128)S(1)}, u32[]{:S(2)}, u32[]{:S(2)}) collective-permute-start(f32[27,8,128]{2,1,0:T(8,128)S(1)} %get-tuple-element.59), channel_id=1, source_target_pairs={{0,16},{16,0},{1,17},{17,1},{2,18},{18,2},{3,19},{19,3},{4,20},{20... | collective-permute-start | bytes 331784 | tf_op jit(solution)/shard_map/ppermute | solution.py:554

commit v4 on v3

--- a/solution.py
+++ b/solution.py
@@ -15,7 +15,7 @@
 NAMES = ("s", "es", "ns", "mix", "relax", "vm", "obs")
 
 
-def call(kernel, outs, scratch, *args, space=VMEM, cost=None):
+def call(kernel, outs, scratch, *args, space=VMEM, out_space=VMEM, cost=None):
     def typed(x):
         return x if isinstance(x, jax.ShapeDtypeStruct) else jax.ShapeDtypeStruct(x, F32)
 
@@ -23,7 +23,7 @@
         kernel,
         out_shape=[typed(x) for x in outs],
         in_specs=[space] * len(args),
-        out_specs=[VMEM] * len(outs),
+        out_specs=[out_space] * len(outs),
         scratch_shapes=[pltpu.VMEM(x, F32) if isinstance(x, tuple) else x for x in scratch],
         compiler_params=pltpu.CompilerParams(vmem_limit_bytes=16 << 20),
         cost_estimate=cost,
@@ -67,6 +67,10 @@
 def pair_rows(first, second):
     sub = sublane(first.shape)
     return jnp.where((sub == 1) | (sub == 2), roll(second, 2, 0), first)
+
+
+def level_pair(levels, t):
+    return (t, t), (levels - 1 - t, levels - 2 - t)
 
 
 def pack_rows(get, counts, level):
@@ -127,37 +131,36 @@
     small = (8, s.shape[2])
     group = iota(small, 1) // GROUP
     half = per_plane // 2
-    count_planes = levels // per_plane
+    plane_count = levels // per_plane
     counts = edge_rows(count[...].astype(F32))
 
     def rims(p, carry):
         acc = jnp.zeros(small, F32)
         late = jnp.zeros(small, F32)
-        for g in range(0, per_plane, 2):
-            tiles = []
-            for level in (p * per_plane + g, p * per_plane + g + 1):
-                tiles.append(
-                    pack_rows(
-                        lambda name: level_of(refs[name], name, level), counts, level.astype(F32)
-                    )
+        for g in range(half):
+            t = p * half + g
+            seconds = []
+            for j, (k, link) in enumerate(level_pair(levels, t)):
+                first, second = pack_rows(
+                    lambda name: level_of(refs[name], name, link if name == "vm" else k),
+                    counts,
+                    k.astype(F32),
                 )
-            half_tile = two_levels(tiles[0][1], tiles[1][1])
-            h = g // 2
-            rows[levels + p * half + h] = half_tile
-            late = jnp.where(group == h, roll(half_tile, GROUP * h + 4, 1), late)
-            for q in range(2):
-                rows[p * per_plane + g + q] = tiles[q][0]
-                acc = jnp.where(
-                    group == g + q, roll(tiles[q][0], GROUP * (g + q) + 4, 1), acc
-                )
+                seconds.append(second)
+                rows[2 * t + j] = first
+                place = 2 * g + j
+                acc = jnp.where(group == place, roll(first, GROUP * place + 4, 1), acc)
+            second = two_levels(*seconds)
+            rows[levels + t] = second
+            late = jnp.where(group == g, roll(second, GROUP * g + 4, 1), late)
         corners[p] = acc
-        corners[count_planes + p] = late
+        corners[plane_count + p] = late
         return carry
 
-    lax.fori_loop(0, count_planes, rims, 0)
+    lax.fori_loop(0, plane_count, rims, 0)
     rows[levels + levels // 2] = counts
-    corners[2 * count_planes] = roll(counts, 4, 1)
-    for p in range(2 * count_planes + 1, corners.shape[0]):
+    corners[2 * plane_count] = roll(counts, 4, 1)
+    for p in range(2 * plane_count + 1, corners.shape[0]):
         corners[p] = jnp.zeros(small, F32)
 
 
@@ -189,7 +192,7 @@
     return jnp.where(sublane(north.shape) % 2 == 0, north, south)
 
 
-def halves_kernel(planes, corners_n, corners_s, rows, one, two, rows_out):
+def halves_kernel(planes, corners_n, corners_s, one, two):
     odd = odd_column()
     pairs = planes.shape[0] // 2
     ny = planes.shape[1]
@@ -205,7 +208,6 @@
         put(pl.ds(h * ny, ny), planes[2 * h], planes[2 * h + 1])
 
     count = corners_n.shape[0]
-    rows_out[...] = rows[...]
     two[pl.ds(one.shape[0], 8)] = jnp.zeros((8, one.shape[1]), F32)
 
     def corner(p):
@@ -248,9 +250,8 @@
         t = half - 1 - t
         new = []
         for k, last in ((t, carry[0]), (levels - 1 - t, carry[1])):
-            x = carries[k] + ratio(k) * last
-            use(k, x)
-            new.append(x)
+            new.append(carries[k] + ratio(k) * last)
+        use(t, *new)
         return tuple(new)
 
     lax.fori_loop(0, half, step, (lower, upper), unroll=UNROLL)
@@ -277,7 +278,7 @@
     s, es, ns, mix, relax, vm, obs, count, from_one, from_two, rows_n, rows_s,
     ep_out, em_out, np_out, nm_out, sink_out, inv_out, q_out, r_out, middle_out, damp_out,
     solved_out, counts_out, join_out, start_out, send,
-    planes, corners, rhs, links, carries,
+    planes, corners, rhs, carries,
 ):
     refs = dict(zip(NAMES, (s, es, ns, mix, relax, vm, obs)))
     levels, ny, nx = s.shape
@@ -314,84 +315,74 @@
         corner = roll(corners[plane], 124 - GROUP * group, 1)
         return jnp.concatenate([rim(index), corner], axis=1)
 
-    def prepare(m, carry):
-        later = rim_ext(
-            levels + m,
-            plane_count + m // (per_plane // 2),
-            m % (per_plane // 2),
-        )
-        for q in range(2):
-            k = 2 * m + q
-            first = rim_ext(k, k // per_plane, k % per_plane)
-            x = unpack_rows(first, roll(later, 4, 0) if q else later)
-            for name in NAMES[:4] + NAMES[5:6]:
-                x[name] = jnp.concatenate(
-                    [extend(level_of(refs[name], name, k), side_of(name, k)), x[name]], axis=0
-                )
-            level = k.astype(F32)
-            state = x["s"]
-            open_east = level < east_count
-            open_north = level < north_count
-            ep = jnp.where(open_east, 0.5 * x["es"] + x["mix"], 0.0)
-            em = jnp.where(open_east, 0.5 * x["es"] - x["mix"], 0.0)
-            np_ = jnp.where(open_north, 0.5 * x["ns"] + x["mix"], 0.0)
-            nm = jnp.where(open_north, 0.5 * x["ns"] - x["mix"], 0.0)
-            inner = state[:ny]
-            sink = extend(level_of(refs["relax"], "relax", k), side_of("relax", k))
-            sink = jnp.where(level < count_ext[:ny], sink, 0.0)
-            link = jnp.where(level + 1.0 < count_ext, x["vm"], 0.0)
-            squeeze = jnp.tanh(inner)
-            base = jnp.concatenate([inner - sink * squeeze, x["base"]], axis=0)
-            ep_out[k] = ep
-            em_out[k] = em
-            np_out[k] = np_
-            nm_out[k] = nm
-            sink_out[k] = sink
-            links[k] = link
-            start_out[k] = state
-            damp_out[k] = 1.0 - sink * (1.0 - squeeze * squeeze)
-            rhs[k] = base - spread(state, ep, em, np_, nm)
-        return carry
+    def prepare(t, j, k, link_level, second):
+        per_half = per_plane // 2
+        first = rim_ext(2 * t + j, t // per_half, 2 * (t % per_half) + j)
+        x = unpack_rows(first, roll(second, 4, 0) if j else second)
+        for name in NAMES[:4] + NAMES[5:6]:
+            at = link_level if name == "vm" else k
+            x[name] = jnp.concatenate(
+                [extend(level_of(refs[name], name, at), side_of(name, at)), x[name]], axis=0
+            )
+        level = k.astype(F32)
+        state = x["s"]
+        open_east = level < east_count
+        open_north = level < north_count
+        ep = jnp.where(open_east, 0.5 * x["es"] + x["mix"], 0.0)
+        em = jnp.where(open_east, 0.5 * x["es"] - x["mix"], 0.0)
+        np_ = jnp.where(open_north, 0.5 * x["ns"] + x["mix"], 0.0)
+        nm = jnp.where(open_north, 0.5 * x["ns"] - x["mix"], 0.0)
+        inner = state[:ny]
+        sink = extend(level_of(refs["relax"], "relax", k), side_of("relax", k))
+        sink = jnp.where(level < count_ext[:ny], sink, 0.0)
+        link = jnp.where(link_level.astype(F32) + 1.0 < count_ext, x["vm"], 0.0)
+        squeeze = jnp.tanh(inner)
+        base = jnp.concatenate([inner - sink * squeeze, x["base"]], axis=0)
+        ep_out[k] = ep
+        em_out[k] = em
+        np_out[k] = np_
+        nm_out[k] = nm
+        sink_out[k] = sink
+        start_out[k] = state
+        damp_out[k] = 1.0 - sink * (1.0 - squeeze * squeeze)
+        return base - spread(state, ep, em, np_, nm), link
 
     def spread(state, ep, em, np_, nm):
         fe = ep * state + em * shift_up(state, 1)
         fn = np_ * state + nm * shift_up(state, 0)
         return (fe - shift_down(fe, 1)) + (fn - shift_down(fn, 0))
 
-    lax.fori_loop(0, half, prepare, 0, unroll=UNROLL // 2)
-
     def factor(t, carry):
-        (r_top, c_top), (r_low, c_low) = carry
-        k = t
-        above = jnp.where(k > 0, links[jnp.maximum(k - 1, 0)], 0.0)
-        below = links[k]
-        inv = 1.0 / (1.0 + above + below - above * r_top)
-        q = above * inv
-        r_top = below * inv
-        c_top = rhs[k] * inv + q * c_top
-        inv_out[k] = inv
-        q_out[k] = q
-        r_out[k] = r_top
-        carries[k] = c_top
-        k = levels - 1 - t
-        above = links[k - 1]
-        below = links[k]
-        inv = 1.0 / (1.0 + above + below - below * r_low)
-        q = below * inv
-        r_low = above * inv
-        c_low = rhs[k] * inv + q * c_low
-        inv_out[k] = inv
-        q_out[k] = q
-        r_out[k] = r_low
-        carries[k] = c_low
-        return (r_top, c_top), (r_low, c_low)
+        per_half = per_plane // 2
+        second = rim_ext(levels + t, plane_count + t // per_half, t % per_half)
+        new = []
+        for j, (k, link_level) in enumerate(level_pair(levels, t)):
+            ratio, c, outer = carry[j]
+            rhs_k, link = prepare(t, j, k, link_level, second)
+            inv = 1.0 / (1.0 + outer + link - outer * ratio)
+            q = outer * inv
+            ratio = link * inv
+            c = rhs_k * inv + q * c
+            inv_out[k] = inv
+            q_out[k] = q
+            r_out[k] = ratio
+            carries[k] = c
+            new.append((ratio, c, link))
+        return tuple(new)
 
     zero = jnp.zeros(rhs.shape[1:], F32)
-    (r_top, c_top), (r_low, c_low) = lax.fori_loop(
-        0, half, factor, ((zero, zero), (zero, zero)), unroll=UNROLL
+    (r_top, c_top, _), (r_low, c_low, _) = lax.fori_loop(
+        0, half, factor, ((zero,) * 3,) * 2, unroll=UNROLL // 2
     )
     join = 1.0 / (1.0 - r_top * r_low)
     join_out[...] = join
+
+    def both(one):
+        def use(t, top, low):
+            one(t, top)
+            one(levels - 1 - t, low)
+
+        return use
 
     def to_second(k, x):
         middle_out[k] = x
@@ -402,7 +393,7 @@
         flow = spread(x, ep_out[k], em_out[k], np_out[k], nm_out[k])
         rhs[k, :ny] = inner - flow[:ny] - sink * squeeze
 
-    solve_outward(levels, (c_top, c_low), lambda k: r_out[k], join, carries, to_second)
+    solve_outward(levels, (c_top, c_low), lambda k: r_out[k], join, carries, both(to_second))
 
     main = carries.at[:, :ny]
     inv_q = (lambda k: inv_out[k, :ny], lambda k: q_out[k, :ny])
@@ -413,16 +404,12 @@
         seen = extend(level_of(refs["obs"], "obs", k), side_of("obs", k))
         rhs[k, :ny] = jnp.where(k.astype(F32) < count_ext[:ny], x - seen, 0.0)
 
-    solve_outward(levels, ends, ratio, join[:ny], main, to_adjoint)
+    solve_outward(levels, ends, ratio, join[:ny], main, both(to_adjoint))
     ends = solve_inward(levels, lambda k: rhs[k, :ny], inv_q, main)
 
-    def to_solved(k, x):
-        solved_out[k] = x
-
-    solve_outward(levels, ends, ratio, join[:ny], main, to_solved)
-
-    def rim_part(k):
-        x = edge_rows(solved_out[k])
+    def rim_part(k, solved):
+        solved_out[k] = solved
+        x = edge_rows(solved)
         edge = lambda ref: edge_rows(ref[k, :ny])
         part, _ = part_of_pull(x, edge(ep_out), edge(em_out), edge_rows(damp_out[levels + k]))
         gn = shift_up(x, 0) - x
@@ -435,22 +422,20 @@
         return pair_rows(x, part)
 
     group = iota((8, nx), 1) // GROUP
-
-    def rims(p, carry):
-        acc = jnp.zeros((8, nx), F32)
-        for g in range(8):
-            t = p * 8 + g
-            both = two_levels(rim_part(t), rim_part(levels - 1 - t))
-            send[t] = both[:, :nx]
-            acc = jnp.where(group == g, roll(both[:, nx:], GROUP * g + 4, 1), acc)
-        send[half + p] = acc
-        return carry
-
-    lax.fori_loop(0, half // 8, rims, 0)
+    for p in range(half // 8):
+        send[half + p] = jnp.zeros((8, nx), F32)
+
+    def to_send(t, top, low):
+        pair = two_levels(rim_part(t, top), rim_part(levels - 1 - t, low))
+        send[t] = pair[:, :nx]
+        p, g = half + t // 8, t % 8
+        send[p] = jnp.where(group == g, roll(pair[:, nx:], GROUP * g + 4, 1), send[p])
+
+    solve_outward(levels, ends, ratio, join[:ny], main, to_send)
 
 
 def inner_kernel(
-    ep, em, np_, nm, damp, middle, solved, counts, part_out, late_out,
+    ep, em, np_, nm, damp, middle, solved, counts, start, part_out, late_out, run_out, rise_out,
 ):
     levels, ny, width = solved.shape
     nx = width // 2
@@ -464,20 +449,26 @@
         gn = jnp.where(inside, shift_up(x, 0) - x, 0.0)
         part_out[k] = part + np_[k, :ny] * gn + shift_down(nm[k, :ny] * gn, 0)
         level = k.astype(F32)
-        rise = shift_up(state, 0)[:ny, :nx] - state[:ny, :nx]
-        run = (shift_up(state[:ny], 1) - state[:ny])[:, :nx]
-        late_out[k] = jnp.where(level < counts[1, :ny, :nx], ge[:, :nx] * run, 0.0) + jnp.where(
-            level < counts[2, :ny, :nx], gn[:, :nx] * rise, 0.0
-        )
+        open_east = level < counts[1, :ny, :nx]
+        open_north = level < counts[2, :ny, :nx]
+
+        def slopes(state):
+            run = (shift_up(state[:ny], 1) - state[:ny])[:, :nx]
+            rise = shift_up(state[:, :nx], 0)[:ny] - state[:ny, :nx]
+            return jnp.where(open_east, run, 0.0), jnp.where(open_north, rise, 0.0)
+
+        run, rise = slopes(state)
+        late_out[k] = ge[:, :nx] * run + gn[:, :nx] * rise
+        run_out[k], rise_out[k] = slopes(start[k])
         return carry
 
-    lax.fori_loop(0, levels, inner, 0, unroll=UNROLL)
+    lax.fori_loop(0, levels, inner, 0, unroll=UNROLL // 2)
 
 
 def backward_kernel(
-    ep, em, np_, nm, inv, q, r, middle, damp, solved, counts, join, start, part, late,
+    ep, em, np_, nm, inv, q, r, middle, damp, solved, counts, join, part, late, run, rise,
     rows_n, rows_s,
-    adjoint_out, gradient_out, carries,
+    adjoint_out, gradient_out, carries, adjoint, gradient, sent,
 ):
     levels, ny, width = solved.shape
     nx = width // 2
@@ -506,8 +497,8 @@
         rise = (shift_up(middle[k, ny:], 0) - middle[k, ny - 8 : ny])[:, :nx]
         open_north = (sub[:, :nx] == 7) & (k.astype(F32) < counts[2, ny - 8 : ny, :nx])
         extra = jnp.where(open_north, north[:, :nx] * rise, 0.0)
-        gradient_out[k, : ny - 8] = late[k, : ny - 8]
-        gradient_out[k, ny - 8 :] = late[k, ny - 8 :] + extra
+        gradient[k, : ny - 8] = late[k, : ny - 8]
+        gradient[k, ny - 8 :] = late[k, ny - 8 :] + extra
         middle_rows = [inner[8 : ny - 8]] if ny > 16 else []
         return jnp.concatenate([low, *middle_rows, high, outer], axis=0)
 
@@ -523,26 +514,52 @@
     ends = lax.fori_loop(0, half, late_step, (zero, zero), unroll=UNROLL // 2)
 
     def early(k, x):
-        state = start[k]
         inner = x[:ny]
-        east = shift_up(inner, 1)
-        ge = east - inner
+        ge = shift_up(inner, 1) - inner
         result = inner[:, :nx] * damp[k, :, :nx] + (ep[k, :ny] * ge)[:, :nx]
         result = result + shift_down(em[k, :ny] * ge, 1)[:, :nx]
         column = x[:, :nx]
         gn = shift_up(column, 0) - column
         result = result + (np_[k, :, :nx] * gn + shift_down(nm[k, :, :nx] * gn, 0))[:ny]
-        adjoint_out[k] = result
-        level = k.astype(F32)
-        run = (shift_up(state[:ny], 1) - state[:ny])[:, :nx]
-        rise = (shift_up(state[:, :nx], 0) - state[:, :nx])[:ny]
-        gradient_out[k] = -(
-            gradient_out[k]
-            + jnp.where(level < counts[1, :ny, :nx], ge[:, :nx] * run, 0.0)
-            + jnp.where(level < counts[2, :ny, :nx], gn[:ny] * rise, 0.0)
-        )
-
-    solve_outward(levels, ends, lambda k: r[k], join[...], carries, early)
+        adjoint[k] = result
+        gradient[k] = -(gradient[k] + ge[:, :nx] * run[k] + gn[:ny] * rise[k])
+
+    def copies(p):
+        out = []
+        for i, begin in enumerate((p * UNROLL, levels - (p + 1) * UNROLL)):
+            place = pl.ds(begin, UNROLL)
+            for j, (source, target) in enumerate(
+                ((adjoint, adjoint_out), (gradient, gradient_out))
+            ):
+                out.append(
+                    pltpu.make_async_copy(
+                        source.at[place], target.at[place], sent.at[p, 2 * i + j]
+                    )
+                )
+        return out
+
+    high, low = ends
+    steps = half // UNROLL
+    last = (low + r[half] * high) * join[...], (high + r[half - 1] * low) * join[...]
+
+    def block(i, last):
+        p = steps - 1 - i
+        for g in range(UNROLL - 1, -1, -1):
+            t = p * UNROLL + g
+            new = []
+            for k, x in ((t, last[0]), (levels - 1 - t, last[1])):
+                x = carries[k] + r[k] * x
+                early(k, x)
+                new.append(x)
+            last = tuple(new)
+        for copy in copies(p):
+            copy.start()
+        return last
+
+    lax.fori_loop(0, steps, block, last)
+    for p in range(steps):
+        for copy in copies(p):
+            copy.wait()
 
 
 def ring(axis, distance):
@@ -595,19 +612,14 @@
         space=HBM,
     )
     corners_n, corners_s = both_ways(corners)
+    rows_n, rows_s = both_ways(rows)
     (planes,) = call(column_kernel, [(2 * pairs, ny, nx)], [], *fields)
     packed = (pairs * ny + corner_planes // 2 * 8, nx)
-    one, two, rows = call(
-        halves_kernel,
-        [packed, (packed[0] + 8, nx), rows.shape],
-        [],
-        planes,
-        corners_n,
-        corners_s,
-        rows,
+    one, two = call(
+        halves_kernel, [packed, (packed[0] + 8, nx)], [], planes, corners_n, corners_s,
+        cost=pl.CostEstimate(flops=10**10, bytes_accessed=0, transcendentals=0),
     )
     from_two = swap(two, 1)
-    rows_n, rows_s = both_ways(rows)
     from_one = swap(one, 0)
     ext = (levels, ny + 8, 2 * nx)
     block = (levels, ny, 2 * nx)
@@ -616,24 +628,25 @@
         [ext] * 4 + [block] + [ext] * 4
         + [(2 * levels, ny, 2 * nx), block, (3,) + ext[1:], ext[1:], ext]
         + [(half + half // 8, 8, nx)],
-        [(2 * pairs, ny, nx), (corner_planes, 8, nx), ext, ext, ext],
+        [(2 * pairs, ny, nx), (corner_planes, 8, nx), ext, ext],
         *fields, from_one, from_two, rows_n, rows_s,
     )
     ep, em, np_, nm, _, inv, q, r, middle, damp, solved, counts, join, start, send = outs
     sent_n, sent_s = both_ways(send)
-    part, late = call(
+    part, late, run, rise = call(
         inner_kernel,
-        [block, (levels, ny, nx)],
+        [block] + [(levels, ny, nx)] * 3,
         [],
-        ep, em, np_, nm, damp, middle, solved, counts,
+        ep, em, np_, nm, damp, middle, solved, counts, start,
         cost=pl.CostEstimate(flops=0, bytes_accessed=8 << 20, transcendentals=0),
     )
     adjoint, gradient = call(
         backward_kernel,
         [(levels, ny, nx)] * 2,
-        [ext],
-        ep, em, np_, nm, inv, q, r, middle, damp, solved, counts, join, start, part, late,
+        [ext] + [(levels, ny, nx)] * 2 + [pltpu.SemaphoreType.DMA((half // UNROLL, 4))],
+        ep, em, np_, nm, inv, q, r, middle, damp, solved, counts, join, part, late, run, rise,
         sent_n, sent_s,
+        out_space=HBM,
     )
     return adjoint, gradient
 

time: 32 us -> 29 us (0.906)
  waiting for transfers between devices: 8.17 us -> 5.45 us
  Pallas kernels: 14.5 us -> 13.9 us
  starting transfers between devices: 8.47 us -> 8.88 us
    ppermute x3, waiting for transfers between devices: 3.84 us -> 1.9 us  [both_ways(): from_north = lax.ppermute(x, 'ty', ring('ty', -1))]
    ppermute x2, starting transfers between devices: 2.54 us -> 3.39 us  [swap(): lax.ppermute(x, 'tx', [(i, (i + 1) % nx if i % 2 == phase else (i - 1) %...]
    ppermute x2, waiting for transfers between devices: 4.33 us -> 3.55 us  [swap(): lax.ppermute(x, 'tx', [(i, (i + 1) % nx if i % 2 == phase else (i - 1) %...]
    pallas_call x6, Pallas kernels: 14.5 us -> 13.9 us  [call(): pl.pallas_call(kernel, out_shape=[typed(x) for x in outs], in_specs=[spac...]
    ppermute x3, starting transfers between devices: 5.93 us -> 5.49 us  [both_ways(): from_north = lax.ppermute(x, 'ty', ring('ty', -1))]
  transfers between devices with their start and end apart: 5 -> 5, of which waited for: 4 -> 4; matrix products, arithmetic and copies ran while one was open for 0% -> 0% of each run, Pallas kernels for 6% -> 10%
where the time goes in v4:
time: 29 us; the launch traced here: 28.9 us
  Pallas kernels  13.9 us (48%)
  starting transfers between devices  8.88 us (31%)
  waiting for transfers between devices  5.45 us (19%)
  between operations  0.66 us (2%)
    pallas_call x6, Pallas kernels, call(): pl.pallas_call(kernel, out_shape=[typed(x) for x in outs], in_specs=[spac...  13.9 us
    ppermute x3, starting transfers between devices, both_ways(): from_north = lax.ppermute(x, 'ty', ring('ty', -1))  5.49 us
    ppermute x2, waiting for transfers between devices, swap(): lax.ppermute(x, 'tx', [(i, (i + 1) % nx if i % 2 == phase else (i - 1) %...  3.55 us
    ppermute x2, starting transfers between devices, swap(): lax.ppermute(x, 'tx', [(i, (i + 1) % nx if i % 2 == phase else (i - 1) %...  3.39 us
    ppermute x3, waiting for transfers between devices, both_ways(): from_north = lax.ppermute(x, 'ty', ring('ty', -1))  1.9 us
  transfers between devices with their start and end apart: 5, of which 4 were waited for; matrix products, arithmetic and copies ran while one was open for 0% of the time, Pallas kernels for 10%

profile of v4, /device:TPU:0, one launch (start us, length us, event | category | flops | bytes accessed | tf_op | source)
XLA Modules:
  0.0 28.9 jit_solution(18380602905327069195)
XLA Ops:
  0.6 2.0 %shard_map.95 = (f32[48,16,128]{2,1,0:T(8,128)S(1)}, bf16[48,16,128]{2,1,0:T(8,128)(2,1)S(1)}, bf16[48,16,128]{2,1,0:T(8,128)(2,1)S(1)}, bf16[48,16,128]{2,1,0:T...) custom-call(f32[48,16,128]{2,1,0:T(8,128)} %args_0_.4, ...), custom_call_target="tpu_custom_call" | custom-call | tf_op jit(solution)/shard_map/pallas_call | solution.py:22
  2.6 3.0 %collective-permute-start = (f32[8,8,128]{2,1,0:T(8,128)S(1)}, f32[8,8,128]{2,1,0:T(8,128)S(1)}, u32[]{:S(2)}, u32[]{:S(2)}) collective-permute-start(f32[8,8,128]{2,1,0:T(8,128)S(1)} %get-tuple-element.40), channel_id=1, source_target_pairs={{0,16},{16,0},{1,17},{17,1},{2,18},{18,2},{3,19},{19,3},{4,20},{20... | collective-permute-start | bytes 98312 | tf_op jit(solution)/shard_map/ppermute | solution.py:571
  5.7 0.1 collective-permute-start.3
  5.7 0.7 %shard_map.96.planes = f32[22,16,128]{2,1,0:T(8,128)S(1)} custom-call(f32[48,16,128]{2,1,0:T(8,128)S(1)} %get-tuple-element.32.s, bf16[48,16,128]{2,1,0:T(8,128)(2,1)S(1)} %get-tuple-element.33.es, bf16[48,16,128]{2,1,0:T(8,128)(2,1)S(1)} %get-tuple-element.34.ns, bf16[48,16,128]{2,1,0:T(8,128)(2,1)S(1)} %get-tuple-element.35.mix, ...), custom_call_target="tpu_custom_call" | custom-call | tf_op jit(solution)/shard_map/pallas_call | solution.py:22
  6.4 1.1 %collective-permute-done.corners_n.corners_s = f32[8,8,128]{2,1,0:T(8,128)S(1)} collective-permute-done((f32[8,8,128]{2,1,0:T(8,128)S(1)}, f32[8,8,128]{2,1,0:T(8,128)S(1)}, u32[]{:S(2)}, u32[]{:S(2)}) %collective-permute-start) | collective-permute-done | bytes 32800 | tf_op jit(solution)/shard_map/ppermute | solution.py:571
  7.5 0.1 shard_map.97
  7.7 3.4 %collective-permute-start.2 = (f32[216,128]{1,0:T(8,128)S(1)}, f32[216,128]{1,0:T(8,128)S(1)}, u32[]{:S(2)}, u32[]{:S(2)}) collective-permute-start(f32[216,128]{1,0:T(8,128)S(1)} %get-tuple-element.42), channel_id=1, source_target_pairs={{0,15},{1,2},{2,1},{3,4},{4,3},{5,6},{6,5},{7,8},{8,7},{9,10},{10,... | collective-permute-start | bytes 331784 | tf_op jit(solution)/shard_map/ppermute | solution.py:579
  11.1 0.0 collective-permute-start.1
  11.1 1.3 %collective-permute-done.1.from_one = f32[208,128]{1,0:T(8,128)S(1)} collective-permute-done((f32[208,128]{1,0:T(8,128)S(1)}, f32[208,128]{1,0:T(8,128)S(1)}, u32[]{:S(2)}, u32[]{:S(2)}) %collective-permute-start.1) | collective-permute-done | bytes 106528 | tf_op jit(solution)/shard_map/ppermute | solution.py:579
  12.4 2.2 %collective-permute-done.2.from_two = f32[216,128]{1,0:T(8,128)S(1)} collective-permute-done((f32[216,128]{1,0:T(8,128)S(1)}, f32[216,128]{1,0:T(8,128)S(1)}, u32[]{:S(2)}, u32[]{:S(2)}) %collective-permute-start.2) | collective-permute-done | bytes 110624 | tf_op jit(solution)/shard_map/ppermute | solution.py:579
  14.6 0.0 collective-permute-done.3.rows_n.rows_s
  14.6 6.8 %shard_map.98 = (f32[48,24,256]{2,1,0:T(8,128)S(1)}, f32[48,24,256]{2,1,0:T(8,128)S(1)}, f32[48,24,256]{2,1,0:T(8,128)S(1)}, f32[48,24,256]{2,1,0:T(8,128)S(1)},...) custom-call(f32[48,16,128]{2,1,0:T(8,128)S(1)} %get-tuple-element.32, ...), custom_call_target="tpu_custom_call" | custom-call | tf_op jit(solution)/shard_map/pallas_call | solution.py:22
  21.5 2.4 %collective-permute-start.4 = (f32[27,8,128]{2,1,0:T(8,128)S(1)}, f32[27,8,128]{2,1,0:T(8,128)S(1)}, u32[]{:S(2)}, u32[]{:S(2)}) collective-permute-start(f32[27,8,128]{2,1,0:T(8,128)S(1)} %get-tuple-element.61), channel_id=1, source_target_pairs={{0,16},{16,0},{1,17},{17,1},{2,18},{18,2},{3,19},{19,3},{4,20},{20... | collective-permute-start | bytes 331784 | tf_op jit(solution)/shard_map/ppermute | solution.py:571
  23.8 2.0 %shard_map.99 = (f32[48,16,256]{2,1,0:T(8,128)S(1)}, f32[48,16,128]{2,1,0:T(8,128)S(1)}, f32[48,16,128]{2,1,0:T(8,128)S(1)}, f32[48,16,128]{2,1,0:T(8,128)S(1)}) custom-call(f32[48,24,256]{2,1,0:T(8,128)S(1)} %get-tuple-element.44.ep, f32[48,24,256]{2,1,0:T(8,128)S(1)} %get-tuple-element.45.em, f32[48,24,256]{2,1,0:T(8,128)S(1)} %get-tuple-element.46.np_, ...), custom_call_target="tpu_custom_call" | custom-call | bytes 8388608 | tf_op jit(solution)/shard_map/pallas_call | solution.py:22
  25.8 0.8 %collective-permute-done.4.rows_n.rows_s = f32[27,8,128]{2,1,0:T(8,128)S(1)} collective-permute-done((f32[27,8,128]{2,1,0:T(8,128)S(1)}, f32[27,8,128]{2,1,0:T(8,128)S(1)}, u32[]{:S(2)}, u32[]{:S(2)}) %collective-permute-start.4) | collective-permute-done | bytes 110624 | tf_op jit(solution)/shard_map/ppermute | solution.py:571
  26.6 2.3 %shard_map.100 = (f32[48,16,128]{2,1,0:T(8,128)}, f32[48,16,128]{2,1,0:T(8,128)}) custom-call(f32[48,24,256]{2,1,0:T(8,128)S(1)} %get-tuple-element.44.ep, f32[48,24,256]{2,1,0:T(8,128)S(1)} %get-tuple-element.45.em, f32[48,24,256]{2,1,0:T(8,128)S(1)} %get-tuple-element.46.np_, f32[48,24,256]{2,1,0:T(8,128)S(1)} %get-tuple-element.47.nm, ...), custom_call_target="tpu_custom_call" | custom-call | tf_op jit(solution)/shard_map/pallas_call | solution.py:22
Async XLA Ops:
  2.6 4.9 %collective-permute-start = (f32[8,8,128]{2,1,0:T(8,128)S(1)}, f32[8,8,128]{2,1,0:T(8,128)S(1)}, u32[]{:S(2)}, u32[]{:S(2)}) collective-permute-start(f32[8,8,128]{2,1,0:T(8,128)S(1)} %get-tuple-element.40), channel_id=1, source_target_pairs={{0,16},{16,0},{1,17},{17,1},{2,18},{18,2},{3,19},{19,3},{4,20},{20... | collective-permute-start | bytes 98312 | tf_op jit(solution)/shard_map/ppermute | solution.py:571
  5.7 9.0 %collective-permute-start.3 = (f32[73,8,128]{2,1,0:T(8,128)S(1)}, f32[73,8,128]{2,1,0:T(8,128)S(1)}, u32[]{:S(2)}, u32[]{:S(2)}) collective-permute-start(f32[73,8,128]{2,1,0:T(8,128)S(1)} %get-tuple-element.43), channel_id=1, source_target_pairs={{0,16},{16,0},{1,17},{17,1},{2,18},{18,2},{3,19},{19,3},{4,20},{20... | collective-permute-start | bytes 897032 | tf_op jit(solution)/shard_map/ppermute | solution.py:571
  7.7 6.9 %collective-permute-start.2 = (f32[216,128]{1,0:T(8,128)S(1)}, f32[216,128]{1,0:T(8,128)S(1)}, u32[]{:S(2)}, u32[]{:S(2)}) collective-permute-start(f32[216,128]{1,0:T(8,128)S(1)} %get-tuple-element.42), channel_id=1, source_target_pairs={{0,15},{1,2},{2,1},{3,4},{4,3},{5,6},{6,5},{7,8},{8,7},{9,10},{10,... | collective-permute-start | bytes 331784 | tf_op jit(solution)/shard_map/ppermute | solution.py:579
  11.1 1.3 %collective-permute-start.1 = (f32[208,128]{1,0:T(8,128)S(1)}, f32[208,128]{1,0:T(8,128)S(1)}, u32[]{:S(2)}, u32[]{:S(2)}) collective-permute-start(f32[208,128]{1,0:T(8,128)S(1)} %get-tuple-element.41), channel_id=1, source_target_pairs={{0,1},{1,0},{2,3},{3,2},{4,5},{5,4},{6,7},{7,6},{8,9},{9,8},{10,11... | collective-permute-start | bytes 319496 | tf_op jit(solution)/shard_map/ppermute | solution.py:579
  21.5 5.1 %collective-permute-start.4 = (f32[27,8,128]{2,1,0:T(8,128)S(1)}, f32[27,8,128]{2,1,0:T(8,128)S(1)}, u32[]{:S(2)}, u32[]{:S(2)}) collective-permute-start(f32[27,8,128]{2,1,0:T(8,128)S(1)} %get-tuple-element.61), channel_id=1, source_target_pairs={{0,16},{16,0},{1,17},{17,1},{2,18},{18,2},{3,19},{19,3},{4,20},{20... | collective-permute-start | bytes 331784 | tf_op jit(solution)/shard_map/ppermute | solution.py:571

commit v5 on v4

v5 whole, which is shorter than its diff:
```python
import functools

import jax
import jax.numpy as jnp
from jax import lax
from jax.experimental import pallas as pl
from jax.experimental.pallas import tpu as pltpu
from jax.sharding import PartitionSpec as P

F32 = jnp.float32
VMEM = pl.BlockSpec(memory_space=pltpu.VMEM)
HBM = pl.BlockSpec(memory_space=pltpu.HBM)
UNROLL = 8
STEPS = 4
GROUP = 8
NAMES = ("s", "es", "ns", "mix", "relax", "vm", "obs")


def call(kernel, outs, scratch, *args, space=VMEM, out_space=VMEM, cost=None):
    def typed(x):
        return x if isinstance(x, jax.ShapeDtypeStruct) else jax.ShapeDtypeStruct(x, F32)

    return pl.pallas_call(
        kernel,
        out_shape=[typed(x) for x in outs],
        in_specs=[space] * len(args),
        out_specs=[out_space] * len(outs),
        scratch_shapes=[pltpu.VMEM(x, F32) if isinstance(x, tuple) else x for x in scratch],
        compiler_params=pltpu.CompilerParams(vmem_limit_bytes=16 << 20),
        cost_estimate=cost,
    )(*args)


def iota(shape, dim):
    return lax.broadcasted_iota(jnp.int32, shape, dim)


def roll(x, shift, axis):
    if isinstance(shift, int):
        shift = shift % x.shape[axis]
        if shift == 0:
            return x
    return pltpu.roll(x, shift, axis)


def odd_column():
    return lax.rem(lax.axis_index("tx"), 2) == 1


def level_of(ref, name, level):
    if name == "vm":
        level = jnp.minimum(level, ref.shape[0] - 1)
    return ref[level].astype(F32)


def edge_rows(block):
    return jnp.where(iota((8, block.shape[1]), 0) < 4, block[:8], block[-8:])


def sublane(shape):
    return iota(shape, 0)


def step_count(counts, axis):
    return jnp.minimum(counts, shift_up(counts, axis))


def pair_rows(first, second):
    sub = sublane(first.shape)
    return jnp.where((sub == 1) | (sub == 2), roll(second, 2, 0), first)


def level_pair(levels, t):
    return (t, t), (levels - 1 - t, levels - 2 - t)


def in_all_groups(x):
    group = iota(x.shape, 1) // GROUP
    out = jnp.zeros(x.shape, F32)
    for g in range(x.shape[1] // GROUP):
        out = jnp.where(group == g, roll(x, GROUP * g + 4, 1), out)
    return out


def pack_rows(get, counts, level):
    tile = {name: edge_rows(get(name)) for name in NAMES[:6]}
    s = tile["s"]
    sub = sublane(s.shape)
    open_north = level < step_count(counts, 0)
    fn = jnp.where(
        open_north,
        (0.5 * tile["ns"] + tile["mix"]) * s + (0.5 * tile["ns"] - tile["mix"]) * shift_up(s, 0),
        0.0,
    )
    sink = jnp.where(level < counts, tile["relax"], 0.0)
    inner = jnp.where(sub == 0, -fn, jnp.where(sub == 7, shift_down(fn, 0), 0.0))
    base = s - sink * jnp.tanh(s) + inner
    first = pair_rows(s, base)
    first = jnp.where((sub == 3) | (sub == 4), roll(tile["es"], 4, 0), first)
    first = jnp.where((sub == 5) | (sub == 6), roll(tile["mix"], 6, 0), first)
    return first, pair_rows(tile["vm"], tile["ns"])


def unpack_rows(first, second):
    return {
        "s": first,
        "base": roll(first, 6, 0),
        "es": roll(first, 4, 0),
        "mix": roll(first, 2, 0),
        "vm": second,
        "ns": roll(second, 6, 0),
    }


def two_levels(x, y):
    sub = sublane(x.shape)
    return jnp.where((sub >= 3) & (sub <= 6), roll(y, 4, 0), x)


def shift_up(x, axis):
    return roll(x, -1, axis)


def shift_down(x, axis):
    return roll(x, 1, axis)


def rim_kernel(*args):
    fields = args[:10]
    s, es, ns, mix, relax, vm, obs, count, *_ = kept = args[10:20]
    rows, corners, arrived = args[20:]
    copies = [pltpu.make_async_copy(fields[i], kept[i], arrived.at[i]) for i in range(10)]
    first = (7, 0, 1, 2, 3, 4, 5)
    rest = (6, 8, 9)
    for i in first + rest:
        copies[i].start()
    for i in first:
        copies[i].wait()
    refs = dict(zip(NAMES, (s, es, ns, mix, relax, vm, obs)))
    levels = s.shape[0]
    per_plane = 128 // GROUP
    small = (8, s.shape[2])
    group = iota(small, 1) // GROUP
    half = per_plane // 2
    plane_count = levels // per_plane
    counts = edge_rows(count[...].astype(F32))

    def rims(p, carry):
        acc = jnp.zeros(small, F32)
        late = jnp.zeros(small, F32)
        for g in range(half):
            t = p * half + g
            seconds = []
            for j, (k, link) in enumerate(level_pair(levels, t)):
                first, second = pack_rows(
                    lambda name: level_of(refs[name], name, link if name == "vm" else k),
                    counts,
                    k.astype(F32),
                )
                seconds.append(second)
                rows[2 * t + j] = first
                place = 2 * g + j
                acc = jnp.where(group == place, roll(first, GROUP * place + 4, 1), acc)
                late = jnp.where(group == place, roll(second, GROUP * place + 4, 1), late)
            rows[levels + t] = two_levels(*seconds)
        corners[p] = acc
        corners[plane_count + p] = late
        return carry

    lax.fori_loop(0, plane_count, rims, 0)
    rows[levels + levels // 2] = counts
    corners[2 * plane_count] = in_all_groups(counts)
    for p in range(2 * plane_count + 1, corners.shape[0]):
        corners[p] = jnp.zeros(small, F32)
    for i in rest:
        copies[i].wait()


def column_kernel(s, es, ns, mix, relax, vm, obs, count, planes):
    refs = dict(zip(NAMES, (s, es, ns, mix, relax, vm, obs)))
    levels = s.shape[0]
    per_plane = 128 // GROUP
    plane_count = levels // per_plane
    shape = s.shape[1:]
    group = iota(shape, 1) // GROUP

    def columns(p, carry):
        for a, name in enumerate(NAMES):
            acc = jnp.zeros(shape, F32)
            for g in range(per_plane):
                pair = level_pair(levels, p * (per_plane // 2) + g // 2)
                x = refs[name][pair[g % 2][name == "vm"]].astype(F32)
                acc = jnp.where(group == g, roll(x, GROUP * g + 4, 1), acc)
            planes[a * plane_count + p] = acc
        return carry

    lax.fori_loop(0, plane_count, columns, 0)
    total = len(NAMES) * plane_count
    planes[total] = in_all_groups(count[...].astype(F32))
    for p in range(total + 1, planes.shape[0]):
        planes[p] = jnp.zeros(shape, F32)


def merge_rows(north, south):
    return jnp.where(sublane(north.shape) % 2 == 0, north, south)


def halves_kernel(planes, corners_n, corners_s, one, two, kept):
    odd = odd_column()
    pairs = planes.shape[0] // 2
    ny = planes.shape[1]

    def put(place, x, y):
        low = iota(x.shape, 1) % GROUP < 4
        to_east = jnp.where(low, x, roll(y, 4, 1))
        to_west = jnp.where(low, roll(x, -4, 1), y)
        one[place] = jnp.where(odd, to_west, to_east)
        two[place] = jnp.where(odd, to_east, to_west)

    for h in range(pairs):
        put(pl.ds(h * ny, ny), planes[2 * h], planes[2 * h + 1])

    count = corners_n.shape[0]
    two[pl.ds(one.shape[0], 8)] = jnp.zeros((8, one.shape[1]), F32)

    def corner(p):
        return merge_rows(corners_n[p], corners_s[p])

    for h in range(count // 2):
        x, y = corner(2 * h), corner(2 * h + 1)
        kept[2 * h] = x
        kept[2 * h + 1] = y
        put(pl.ds(pairs * ny + h * 8, 8), x, y)


def extend(main, side, rows=None, corners=None):
    top = jnp.concatenate([main, side], axis=1)
    if rows is None:
        return top
    return jnp.concatenate([top, jnp.concatenate([rows, corners], axis=1)], axis=0)


def solve_inward(levels, get, inv_q, carries):
    half = levels // 2
    inv, q = inv_q

    def step(t, carry):
        new = []
        for k, last in ((t, carry[0]), (levels - 1 - t, carry[1])):
            c = get(k) * inv(k) + q(k) * last
            carries[k] = c
            new.append(c)
        return tuple(new)

    zero = jnp.zeros(carries.shape[1:], F32)
    return lax.fori_loop(0, half, step, (zero, zero), unroll=UNROLL)


def solve_outward(levels, ends, ratio, join, carries, use):
    half = levels // 2
    high, low = ends
    upper = (high + ratio(half - 1) * low) * join
    lower = (low + ratio(half) * high) * join

    def block(i, last):
        m = half // STEPS - 1 - i
        for u in range(STEPS - 1, -1, -1):
            t = m * STEPS + u
            new = []
            for k, x in ((t, last[0]), (levels - 1 - t, last[1])):
                new.append(carries[k] + ratio(k) * x)
            use(t, m, u, *new)
            last = tuple(new)
        return last

    lax.fori_loop(0, half // STEPS, block, (lower, upper), unroll=2)


def merge_halos(odd, from_one, from_two, planes, start):
    size = planes.shape[1]
    low = iota(planes.shape[1:], 1) % GROUP < 4
    for h in range(planes.shape[0] // 2):
        place = pl.ds(start + h * size, size)
        a, b = from_one[place], from_two[place]
        west = jnp.where(odd, a, b)
        east = jnp.where(odd, b, a)
        planes[2 * h] = jnp.where(low, west, roll(east, 4, 1))
        planes[2 * h + 1] = jnp.where(low, roll(west, -4, 1), east)


def part_of_pull(x, ep, em, damp):
    ge = shift_up(x, 1) - x
    return x * damp + ep * ge + shift_down(em * ge, 1), ge


def local_kernel(
    s, es, ns, mix, relax, vm, count, east, north, after,
    ep_out, em_out, np_out, nm_out, sink_out, damp_out, local_out, inv_out, q_out, r_out,
    moves_out,
):
    levels, ny, nx = s.shape
    half = levels // 2
    counts = count[...].astype(F32)
    east_count = east[...].astype(F32)
    north_count = north[...].astype(F32)
    lane = iota((ny, nx), 1)
    sub = sublane((ny, nx))

    def prepare(k):
        level = k.astype(F32)
        state = s[k]
        diffusion = mix[k].astype(F32)
        speed_east = 0.5 * es[k].astype(F32)
        speed_north = 0.5 * ns[k].astype(F32)
        open_east = level < east_count
        open_north = level < north_count
        ep = jnp.where(open_east, speed_east + diffusion, 0.0)
        em = jnp.where(open_east, speed_east - diffusion, 0.0)
        np_ = jnp.where(open_north, speed_north + diffusion, 0.0)
        nm = jnp.where(open_north, speed_north - diffusion, 0.0)
        sink = jnp.where(level < counts, relax[k].astype(F32), 0.0)
        squeeze = jnp.tanh(state)
        ep_out[k] = ep
        em_out[k] = em
        np_out[k] = np_
        nm_out[k] = nm
        sink_out[k] = sink
        damp_out[k] = 1.0 - sink * (1.0 - squeeze * squeeze)
        fe = ep * state + em * shift_up(state, 1)
        fe = jnp.where(lane == nx - 1, 0.0, fe)
        fn = np_ * state + nm * jnp.where(sub == ny - 1, 0.0, shift_up(state, 0))
        flow = fe - shift_down(fe, 1)
        flow = flow + (fn - jnp.where(sub == 0, 0.0, shift_down(fn, 0)))
        local_out[k] = state - sink * squeeze - flow

    def factor(t, carry):
        new = []
        for (k, link_level), (ratio, outer) in zip(level_pair(levels, t), carry):
            prepare(k)
            link = jnp.where(
                link_level.astype(F32) + 1.0 < counts, vm[link_level].astype(F32), 0.0
            )
            inv = 1.0 / (1.0 + outer + link - outer * ratio)
            ratio = link * inv
            inv_out[k] = inv
            q_out[k] = outer * inv
            r_out[k] = ratio
            new.append((ratio, link))
        return tuple(new)

    zero = jnp.zeros((ny, nx), F32)
    lax.fori_loop(0, half, factor, ((zero, zero), (zero, zero)), unroll=UNROLL)

    source = iota((2 * nx, 2 * nx), 0) % nx
    target = iota((2 * nx, 2 * nx), 1)
    for u in range(STEPS):
        group = 2 * u + target // nx
        hit = source == (target + 4 + GROUP * group) % nx
        moves_out[u] = jnp.where(hit, 1.0, 0.0).astype(jnp.bfloat16)


def whole(own, halo):
    ny = own.shape[0]
    return extend(own, halo[:ny], halo[ny + 8 :], halo[ny : ny + 8])


def forward_kernel(
    s, obs, count, from_one, from_two, own_planes, own_corners, rows_n, rows_s,
    ep, em, np_, nm, sink, local, inv, q, r, moves,
    ep_halo, em_halo, np_halo, nm_halo, sink_halo, inv_halo, q_halo, r_halo, s_halo,
    middle_out, damp_out, solved_out, counts_out, join_out, send,
    planes, corners, rhs, carries, packed, moved, moved_rows, sides,
):
    levels, ny, nx = s.shape
    half = levels // 2
    per_plane = 128 // GROUP
    plane_count = levels // per_plane
    odd = odd_column()
    merge_halos(odd, from_one, from_two, planes, 0)
    merge_halos(odd, from_one, from_two, corners, planes.shape[0] // 2 * planes.shape[1])

    def rim(index):
        return merge_rows(rows_n[index], rows_s[index])

    count_plane = len(NAMES) * plane_count
    count_ext = extend(
        count[...].astype(F32),
        roll(planes[count_plane], 124, 1),
        rim(levels + half),
        roll(corners[2 * plane_count], 124, 1),
    )
    east_ext = step_count(count_ext, 1)
    counts_out[0] = count_ext
    counts_out[1] = east_ext
    counts_out[2] = step_count(count_ext, 0)
    count_halo = jnp.concatenate(
        [count_ext[:ny, nx:], count_ext[ny:, nx:], count_ext[ny:, :nx]], axis=0
    )
    small_sub = sublane((8, nx))
    east_rows = east_ext[ny:, :nx]
    north_rows = jnp.where(small_sub == 7, counts_out[2, ny:, :nx], 0.0)
    lane = iota((ny, nx), 1)
    per_half = per_plane // 2

    strip = (ny + 8, nx)
    place = iota(strip, 1) % GROUP
    low = place < 4
    groups = iota(strip, 1) // GROUP
    from_top = groups % 2 == 0
    strip_sub = sublane(strip)

    def columns(p, carry):
        t = p * per_half + groups // 2
        level = jnp.where(from_top, t, levels - 1 - t).astype(F32)
        link_level = jnp.where(from_top, t, levels - 2 - t).astype(F32)

        def side_and_corner(a, c):
            return jnp.concatenate([a, c], axis=0)

        def strips(west):
            def pick(halo, own):
                near_side = low[: halo.shape[0]]
                return jnp.where(near_side, halo, own) if west else jnp.where(near_side, own, halo)

            x = unpack_rows(
                pick(corners[p], own_corners[p]),
                pick(corners[plane_count + p], own_corners[plane_count + p]),
            )
            side = {}
            for a, name in enumerate(NAMES[:6]):
                at = a * plane_count + p
                side[name] = pick(planes[at], own_planes[at])
            for name in NAMES[:4] + NAMES[5:6]:
                x[name] = side_and_corner(side[name], x[name])
            counts = side_and_corner(
                pick(planes[count_plane], own_planes[count_plane]),
                pick(corners[2 * plane_count], own_corners[2 * plane_count]),
            )
            state = x["s"]
            open_east = level < step_count(counts, 1)
            open_north = (level < step_count(counts, 0)) & (
                (strip_sub < ny) | (strip_sub == ny + 7)
            )
            ep_s = jnp.where(open_east, 0.5 * x["es"] + x["mix"], 0.0)
            em_s = jnp.where(open_east, 0.5 * x["es"] - x["mix"], 0.0)
            np_s = jnp.where(open_north, 0.5 * x["ns"] + x["mix"], 0.0)
            nm_s = jnp.where(open_north, 0.5 * x["ns"] - x["mix"], 0.0)
            sink_s = jnp.where(level[:ny] < counts[:ny], side["relax"], 0.0)
            link = jnp.where(link_level + 1.0 < counts, x["vm"], 0.0)
            fe = ep_s * state + em_s * shift_up(state, 1)
            fe_west = shift_down(fe, 1)
            fn = np_s * state + nm_s * shift_up(state, 0)
            base = side_and_corner(side["s"] - sink_s * jnp.tanh(side["s"]), x["base"])
            right = base - (fe - fe_west) - (fn - shift_down(fn, 0))
            return (right, link, np_s, nm_s, ep_s, em_s, sink_s, state), fe, fe_west

        west, _, through_west = strips(True)
        east, through_east, _ = strips(False)
        seam = jnp.where(place == 3, through_east, through_west)
        both = [jnp.where(low[: a.shape[0]], a, b) for a, b in zip(west, east)]
        right, link, np_c, nm_c = (x[ny:] for x in both[:4])
        corner = pair_rows(right, link)
        corner = jnp.where((small_sub == 3) | (small_sub == 4), roll(seam[ny:], 4, 0), corner)
        corner = jnp.where(small_sub == 5, roll(np_c, 6, 0), corner)
        corner = jnp.where(small_sub == 6, roll(nm_c, 7, 0), corner)
        both = [x[:ny] for x in both]
        seen = planes[NAMES.index("obs") * plane_count + p]
        both = both[:2] + [seam[:ny], seen] + both[2:] + [jnp.concatenate([corner] * 2, axis=0)]
        for i, x in enumerate(both):
            split(p, i * ny, x)
        return carry

    def split(p, at, x):
        for h, y in enumerate((x, roll(x, nx // 2, 1))):
            high = y.astype(jnp.bfloat16)
            packed[2 * p + h, at : at + ny, :nx] = high
            packed[2 * p + h, at : at + ny, nx:] = (y - high.astype(F32)).astype(jnp.bfloat16)

    lax.fori_loop(0, plane_count, columns, 0, unroll=plane_count)

    def unpack(u):
        move = moves[u]

        def place_both(m, carry):
            out = jnp.dot(packed[m], move, preferred_element_type=F32)
            t = m * STEPS + u
            for j, k in enumerate((t, levels - 1 - t)):
                x = out[:, j * nx : (j + 1) * nx]
                np_x, nm_x, ep_x, em_x, sink_x, s_x, corner = (
                    x[i * ny : (i + 1) * ny] for i in range(4, 11)
                )
                corner = corner[:8]
                moved[k] = x[: 4 * ny]
                moved_rows[k] = corner
                ep_halo[k, :ny] = ep_x
                em_halo[k, :ny] = em_x
                np_halo[k, :ny] = np_x
                nm_halo[k, :ny] = nm_x
                np_halo[k, ny : ny + 8] = roll(corner, 2, 0)
                nm_halo[k, ny : ny + 8] = roll(corner, 1, 0)
                sink_halo[k] = sink_x
                s_halo[k, :ny] = s_x
            return carry

        lax.fori_loop(0, 2 * plane_count, place_both, 0, unroll=2 * plane_count)

    for u in range(STEPS):
        unpack(u)

    def prepare(m, u, j, k, link_level, second):
        t = m * STEPS + u
        x = unpack_rows(rim(2 * t + j), roll(second, 4, 0) if j else second)
        level = k.astype(F32)
        row = x["s"]
        open_east = level < east_rows
        open_north = level < north_rows
        ep_r = jnp.where(open_east, 0.5 * x["es"] + x["mix"], 0.0)
        em_r = jnp.where(open_east, 0.5 * x["es"] - x["mix"], 0.0)
        np_r = jnp.where(open_north, 0.5 * x["ns"] + x["mix"], 0.0)
        nm_r = jnp.where(open_north, 0.5 * x["ns"] - x["mix"], 0.0)
        link_r = jnp.where(link_level.astype(F32) + 1.0 < count_halo[ny + 8 :], x["vm"], 0.0)
        corner = moved_rows[k]
        right, link, seam = (moved[k, i * ny : (i + 1) * ny] for i in range(3))
        seam_rows = roll(corner, 4, 0)
        np_halo[k, ny + 8 :] = np_r
        nm_halo[k, ny + 8 :] = nm_r
        s_halo[k, ny + 8 :] = row

        own = s[k]
        last, first = lane == nx - 1, lane == 0
        fe = ep_r * row + em_r * shift_up(row, 1)
        flow = jnp.where(last[:8], seam_rows, fe) - jnp.where(
            first[:8], seam_rows, shift_down(fe, 1)
        )
        fn = np_r * row + nm_r * shift_up(own[:8], 0)
        top = np_[k, ny - 8 :] * own[ny - 8 :]
        cross = nm[k, ny - 8 :] * shift_up(row, 0)
        from_block = jnp.where(small_sub == 0, shift_down(top + cross, 0), 0.0)
        right_r = x["base"] - flow - (fn - from_block)

        inner = local[k] + jnp.where(first, seam, jnp.where(last, -seam, 0.0))
        low_rows = inner[:8] + jnp.where(small_sub == 0, shift_down(fn, 0), 0.0)
        high_rows = inner[ny - 8 :] - jnp.where(small_sub == 7, cross, 0.0)
        between = [inner[8 : ny - 8]] if ny > 16 else []
        inner = jnp.concatenate([low_rows] + between + [high_rows], axis=0)
        halo = jnp.concatenate([right, corner, right_r], axis=0)
        return inner, halo, jnp.concatenate([link, roll(corner, 6, 0), link_r], axis=0)

    def factor(m, carry):
        for u in range(STEPS):
            carry = factor_step(m, u, carry)
        return carry

    def factor_step(m, u, carry):
        t = m * STEPS + u
        second = rim(levels + t)
        new = []
        for j, (k, link_level) in enumerate(level_pair(levels, t)):
            ratio, c_own, c_halo, outer = carry[j]
            own, halo, link = prepare(m, u, j, k, link_level, second)
            inv_h = 1.0 / (1.0 + outer + link - outer * ratio)
            q_h = outer * inv_h
            ratio = link * inv_h
            c_own = own * inv[k] + q[k] * c_own
            c_halo = halo * inv_h + q_h * c_halo
            inv_halo[k] = inv_h
            q_halo[k] = q_h
            r_halo[k] = ratio
            carries[k] = whole(c_own, c_halo)
            new.append((ratio, c_own, c_halo, link))
        return tuple(new)

    zero = jnp.zeros(count_halo.shape, F32)
    begin = (zero, jnp.zeros((ny, nx), F32), zero, zero)
    (r_top, top_own, top_halo, _), (r_low, low_own, low_halo, _) = lax.fori_loop(
        0, half // STEPS, factor, (begin, begin), unroll=2
    )
    c_top, c_low = whole(top_own, top_halo), whole(low_own, low_halo)
    join = 1.0 / (1.0 - whole(r[half - 1], r_top) * whole(r[half], r_low))
    join_out[...] = join

    def ext(own, halo):
        return lambda k: whole(own[k], halo[k])

    def inner(own, halo):
        return lambda k: extend(own[k], halo[k, :ny])

    def spread(state, ep, em, np_, nm):
        fe = ep * state + em * shift_up(state, 1)
        fn = np_ * state + nm * shift_up(state, 0)
        return (fe - shift_down(fe, 1)) + (fn - shift_down(fn, 0))

    def both(one):
        def use(t, m, u, top, low):
            one(t, top, m, u, 0)
            one(levels - 1 - t, low, m, u, 1)

        return use

    def to_second(k, x, m, u, j):
        middle_out[k] = x
        state = x[:ny]
        squeeze = jnp.tanh(state)
        loss = inner(sink, sink_halo)(k)
        damp_out[k] = 1.0 - loss * (1.0 - squeeze * squeeze)
        fields = (ext(ep, ep_halo), ext(em, em_halo), ext(np_, np_halo), ext(nm, nm_halo))
        flow = spread(x, *(field(k) for field in fields))
        rhs[k] = state - flow[:ny] - loss * squeeze

    solve_outward(levels, (c_top, c_low), ext(r, r_halo), join, carries, both(to_second))

    main = carries.at[:, :ny]
    inv_q = inner(inv, inv_halo), inner(q, q_halo)
    ratio = inner(r, r_halo)
    ends = solve_inward(levels, lambda k: rhs[k], inv_q, main)

    def to_adjoint(k, x, m, u, j):
        seen = extend(obs[k].astype(F32), moved[k, 3 * ny :])
        rhs[k] = jnp.where(k.astype(F32) < count_ext[:ny], x - seen, 0.0)

    solve_outward(levels, ends, ratio, join[:ny], main, both(to_adjoint))
    ends = solve_inward(levels, lambda k: rhs[k], inv_q, main)

    def rim_part(k, solved):
        solved_out[k] = solved
        x = edge_rows(solved)
        rows_of = lambda own, halo: edge_rows(inner(own, halo)(k))
        part, _ = part_of_pull(
            x, rows_of(ep, ep_halo), rows_of(em, em_halo), edge_rows(damp_out[k])
        )
        gn = shift_up(x, 0) - x
        sub = sublane(x.shape)
        part = part + jnp.where(
            sub == 0,
            rows_of(np_, np_halo) * gn,
            jnp.where(sub == 7, shift_down(rows_of(nm, nm_halo) * gn, 0), 0.0),
        )
        return pair_rows(x, part)

    group = iota((8, nx), 1) // GROUP

    def to_send(t, m, u, top, low):
        pair = two_levels(rim_part(t, top), rim_part(levels - 1 - t, low))
        send[t] = pair[:, :nx]
        before = jnp.zeros((8, nx), F32) if u == STEPS - 1 else sides[m]
        moved = roll(pair[:, nx:], 2 * GROUP * u + 4, 1)
        sides[m] = jnp.where(group == 2 * u, moved, before)

    solve_outward(levels, ends, ratio, join[:ny], main, to_send)
    for p in range(half // 8):
        send[half + p] = jnp.where(group % 2 == 0, sides[2 * p], roll(sides[2 * p + 1], GROUP, 1))


def inner_kernel(
    ep, em, np_, nm, ep_halo, em_halo, np_halo, nm_halo, damp, middle, solved, counts,
    s, s_halo, part_out, late_out, run_out, rise_out,
):
    levels, ny, width = solved.shape
    nx = width // 2
    sub = sublane((ny, width))
    inside = sub < ny - 1

    def inner(k, carry):
        x = solved[k]
        state = middle[k]
        field = lambda own, halo: extend(own[k], halo[k, :ny])
        part, ge = part_of_pull(x, field(ep, ep_halo), field(em, em_halo), damp[k])
        gn = jnp.where(inside, shift_up(x, 0) - x, 0.0)
        part_out[k] = (
            part + field(np_, np_halo) * gn + shift_down(field(nm, nm_halo) * gn, 0)
        )
        level = k.astype(F32)
        open_east = level < counts[1, :ny, :nx]
        open_north = level < counts[2, :ny, :nx]

        def slopes(state):
            run = (shift_up(state[:ny], 1) - state[:ny])[:, :nx]
            rise = shift_up(state[:, :nx], 0)[:ny] - state[:ny, :nx]
            return jnp.where(open_east, run, 0.0), jnp.where(open_north, rise, 0.0)

        run, rise = slopes(state)
        late_out[k] = ge[:, :nx] * run + gn[:, :nx] * rise
        run_out[k], rise_out[k] = slopes(whole(s[k], s_halo[k]))
        return carry

    lax.fori_loop(0, levels, inner, 0, unroll=UNROLL)


def backward_kernel(
    ep, em, np_, nm, inv, q, r, ep_halo, em_halo, np_halo, nm_halo, inv_halo, q_halo, r_halo,
    middle, damp, solved, counts, join, part, late, run, rise, rows_n, rows_s,
    adjoint_out, gradient_out, carries, adjoint, gradient, sides, sent,
):
    levels, ny, width = solved.shape
    nx = width // 2
    half = levels // 2
    sub = sublane((8, width))

    for p in range(half // 8):
        side = merge_rows(rows_n[half + p], rows_s[half + p])
        sides[2 * p] = side
        sides[2 * p + 1] = roll(side, -GROUP, 1)

    def rims(m, u):
        t = m * STEPS + u
        line = merge_rows(rows_n[t], rows_s[t])
        corner = roll(sides[m], 124 - 2 * GROUP * u, 1)
        both = jnp.concatenate([line, corner], axis=1)
        return both, roll(both, 4, 0)

    def across(k, rim):
        inner = part[k]
        near_part = roll(rim, 6, 0)
        south = solved[k, :8] - shift_down(rim, 0)
        north = shift_up(rim, 0) - solved[k, ny - 8 :]
        north_plus = whole(np_[k], np_halo[k])
        north_minus = whole(nm[k], nm_halo[k])
        np_rim, nm_rim = north_plus[ny:], north_minus[ny:]
        np_top, nm_top = north_plus[ny - 8 : ny], north_minus[ny - 8 : ny]
        low = inner[:8] + jnp.where(sub == 0, shift_down(nm_rim, 0) * south, 0.0)
        high = inner[ny - 8 :] + jnp.where(sub == 7, np_top * north, 0.0)
        outer = near_part + jnp.where(
            sub == 0, shift_down(nm_top * north, 0), np_rim * shift_up(south, 0)
        )
        rise = (shift_up(middle[k, ny:], 0) - middle[k, ny - 8 : ny])[:, :nx]
        open_north = (sub[:, :nx] == 7) & (k.astype(F32) < counts[2, ny - 8 : ny, :nx])
        extra = jnp.where(open_north, north[:, :nx] * rise, 0.0)
        gradient[k, : ny - 8] = late[k, : ny - 8]
        gradient[k, ny - 8 :] = late[k, ny - 8 :] + extra
        middle_rows = [inner[8 : ny - 8]] if ny > 16 else []
        return jnp.concatenate([low, *middle_rows, high, outer], axis=0)

    def late_steps(m, carry):
        for u in range(STEPS):
            t = m * STEPS + u
            new = []
            for k, rim, last in zip((t, levels - 1 - t), rims(m, u), carry):
                c = across(k, rim) * whole(inv[k], inv_halo[k])
                c = c + whole(q[k], q_halo[k]) * last
                carries[k] = c
                new.append(c)
            carry = tuple(new)
        return carry

    zero = jnp.zeros(carries.shape[1:], F32)
    ends = lax.fori_loop(0, half // STEPS, late_steps, (zero, zero), unroll=2)

    def early(k, x):
        inner = x[:ny]
        ge = shift_up(inner, 1) - inner
        result = inner[:, :nx] * damp[k] + ep[k] * ge[:, :nx]
        result = result + shift_down(extend(em[k], em_halo[k, :ny]) * ge, 1)[:, :nx]
        column = x[:, :nx]
        gn = shift_up(column, 0) - column
        minus = jnp.concatenate([nm[k], nm_halo[k, ny + 8 :]], axis=0)
        result = result + np_[k] * gn[:ny] + shift_down(minus * gn, 0)[:ny]
        adjoint[k] = result
        gradient[k] = -(gradient[k] + ge[:, :nx] * run[k] + gn[:ny] * rise[k])

    def copies(p):
        out = []
        for i, begin in enumerate((p * UNROLL, levels - (p + 1) * UNROLL)):
            place = pl.ds(begin, UNROLL)
            for j, (source, target) in enumerate(
                ((adjoint, adjoint_out), (gradient, gradient_out))
            ):
                out.append(
                    pltpu.make_async_copy(
                        source.at[place], target.at[place], sent.at[p, 2 * i + j]
                    )
                )
        return out

    high, low = ends
    steps = half // UNROLL
    ratio = lambda k: whole(r[k], r_halo[k])
    last = (low + ratio(half) * high) * join[...], (high + ratio(half - 1) * low) * join[...]

    def block(i, last):
        p = steps - 1 - i
        for g in range(UNROLL - 1, -1, -1):
            t = p * UNROLL + g
            new = []
            for k, x in ((t, last[0]), (levels - 1 - t, last[1])):
                x = carries[k] + ratio(k) * x
                early(k, x)
                new.append(x)
            last = tuple(new)
        for copy in copies(p):
            copy.start()
        return last

    lax.fori_loop(0, steps, block, last)
    for p in range(steps):
        for copy in copies(p):
            copy.wait()


def ring(axis, distance):
    count = lax.axis_size(axis)
    return [(i, (i + distance) % count) for i in range(count)]


def both_ways(x):
    from_north = lax.ppermute(x, "ty", ring("ty", -1))
    if lax.axis_size("ty") == 2:
        return from_north, from_north
    return from_north, lax.ppermute(x, "ty", ring("ty", 1))


def swap(x, phase):
    nx = lax.axis_size("tx")
    return lax.ppermute(
        x, "tx", [(i, (i + 1) % nx if i % 2 == phase else (i - 1) % nx) for i in range(nx)]
    )


def per_device(
    tracer_start,
    observed,
    east_speed,
    north_speed,
    mixing,
    vertical_mixing,
    relax_rate,
    level_count,
    face_east,
    face_north,
):
    levels, ny, nx = tracer_start.shape
    per_plane = 128 // GROUP
    plane_count = levels // per_plane
    pairs = (len(NAMES) * plane_count + 2) // 2
    fields = (
        tracer_start, east_speed, north_speed, mixing, relax_rate, vertical_mixing, observed,
        level_count, face_east, face_north,
    )
    half = levels // 2
    corner_planes = 2 * plane_count + 2
    *fields, rows, corners = call(
        rim_kernel,
        [jax.ShapeDtypeStruct(x.shape, x.dtype) for x in fields]
        + [(levels + half + 1, 8, nx), (corner_planes, 8, nx)],
        [pltpu.SemaphoreType.DMA((10,))],
        *[pltpu.with_memory_space_constraint(x, pltpu.HBM) for x in fields],
        space=HBM,
    )
    corners_n, corners_s = both_ways(corners)
    rows_n, rows_s = both_ways(rows)
    (planes,) = call(column_kernel, [(2 * pairs, ny, nx)], [], *fields[:8])
    packed = (pairs * ny + corner_planes // 2 * 8, nx)
    one, two, own_corners = call(
        halves_kernel, [packed, (packed[0] + 8, nx), corners.shape], [],
        planes, corners_n, corners_s,
        cost=pl.CostEstimate(flops=10**10, bytes_accessed=0, transcendentals=0),
    )
    from_two = swap(two, 1)
    from_one = swap(one, 0)
    ext = (levels, ny + 8, 2 * nx)
    block = (levels, ny, 2 * nx)
    own = (levels, ny, nx)
    halo = (levels, ny + 16, nx)
    s, es, ns, mix, relax, vm, obs, count, east, north = fields
    *coefficients, damp, local, inv, q, r, moves = call(
        local_kernel,
        [own] * 10 + [jax.ShapeDtypeStruct((STEPS, 2 * nx, 2 * nx), jnp.bfloat16)],
        [],
        s, es, ns, mix, relax, vm, count, east, north, one,
        cost=pl.CostEstimate(flops=10**9, bytes_accessed=0, transcendentals=0),
    )
    ep, em, np_, nm, sink = coefficients
    outs = call(
        forward_kernel,
        [halo] * 4 + [own] + [halo] * 4 + [ext, block, block, (3,) + ext[1:], ext[1:]]
        + [(half + half // 8, 8, nx)],
        [
            planes.shape,
            corners.shape,
            block,
            ext,
            pltpu.VMEM((2 * plane_count, 11 * ny, 2 * nx), jnp.bfloat16),
            (levels, 4 * ny, nx),
            (levels, 8, nx),
            (2 * plane_count, 8, nx),
        ],
        s, obs, count, from_one, from_two, planes, own_corners, rows_n, rows_s,
        ep, em, np_, nm, sink, local, inv, q, r, moves,
    )
    ep_h, em_h, np_h, nm_h, _, inv_h, q_h, r_h, s_h, *outs = outs
    middle, late_damp, solved, counts, join, send = outs
    sent_n, sent_s = both_ways(send)
    faces = ep, em, np_, nm
    halo_faces = ep_h, em_h, np_h, nm_h
    part, late, run, rise = call(
        inner_kernel,
        [block] + [own] * 3,
        [],
        *faces, *halo_faces, late_damp, middle, solved, counts, s, s_h,
        cost=pl.CostEstimate(flops=0, bytes_accessed=8 << 20, transcendentals=0),
    )
    adjoint, gradient = call(
        backward_kernel,
        [own] * 2,
        [ext, own, own, (2 * plane_count, 8, nx), pltpu.SemaphoreType.DMA((half // UNROLL, 4))],
        *faces, inv, q, r, *halo_faces, inv_h, q_h, r_h,
        middle, damp, solved, counts, join, part, late, run, rise, sent_n, sent_s,
        out_space=HBM,
    )
    return adjoint, gradient


def solution(mesh):
    block = P(None, "ty", "tx")
    plane = P("ty", "tx")
    return jax.shard_map(
        per_device,
        mesh=mesh,
        in_specs=(block,) * 7 + (plane,) * 3,
        out_specs=(block, block),
        check_vma=False,
    )
```

time: 29 us -> 27.4 us (0.945)
  Pallas kernels: 13.9 us -> 12.8 us
  waiting for transfers between devices: 5.45 us -> 4.81 us
    pallas_call x6 -> x7, Pallas kernels: 13.9 us -> 12.8 us  [call(): pl.pallas_call(kernel, out_shape=[typed(x) for x in outs], in_specs=[spac...]
    ppermute x2, waiting for transfers between devices: 3.55 us -> 2.66 us  [swap(): lax.ppermute(x, 'tx', [(i, (i + 1) % nx if i % 2 == phase else (i - 1) %...]
  transfers between devices with their start and end apart: 5 -> 5, of which waited for: 4 -> 4; matrix products, arithmetic and copies ran while one was open for 0% -> 0% of each run, Pallas kernels for 10% -> 12%
where the time goes in v5:
time: 27.4 us; the launch traced here: 27.2 us
  Pallas kernels  12.8 us (47%)
  starting transfers between devices  8.88 us (32%)
  waiting for transfers between devices  4.81 us (18%)
  between operations  0.68 us (2%)
    pallas_call x7, Pallas kernels, call(): pl.pallas_call(kernel, out_shape=[typed(x) for x in outs], in_specs=[spac...  12.8 us
    ppermute x3, starting transfers between devices, both_ways(): from_north = lax.ppermute(x, 'ty', ring('ty', -1))  5.49 us
    ppermute x2, starting transfers between devices, swap(): lax.ppermute(x, 'tx', [(i, (i + 1) % nx if i % 2 == phase else (i - 1) %...  3.39 us
    ppermute x2, waiting for transfers between devices, swap(): lax.ppermute(x, 'tx', [(i, (i + 1) % nx if i % 2 == phase else (i - 1) %...  2.66 us
    ppermute x3, waiting for transfers between devices, both_ways(): from_north = lax.ppermute(x, 'ty', ring('ty', -1))  2.15 us
  transfers between devices with their start and end apart: 5, of which 4 were waited for; matrix products, arithmetic and copies ran while one was open for 0% of the time, Pallas kernels for 12%

profile of v5, /device:TPU:0, one launch (start us, length us, event | category | flops | bytes accessed | tf_op | source)
XLA Modules:
  0.0 27.2 jit_solution(10908884657888890783)
XLA Ops:
  0.6 2.0 %shard_map.113 = (f32[48,16,128]{2,1,0:T(8,128)S(1)}, bf16[48,16,128]{2,1,0:T(8,128)(2,1)S(1)}, bf16[48,16,128]{2,1,0:T(8,128)(2,1)S(1)}, bf16[48,16,128]{2,1,0:...) custom-call(f32[48,16,128]{2,1,0:T(8,128)} %args_0_.4, ...), custom_call_target="tpu_custom_call" | custom-call | tf_op jit(solution)/shard_map/pallas_call | solution.py:23
  2.6 3.0 %collective-permute-start = (f32[8,8,128]{2,1,0:T(8,128)S(1)}, f32[8,8,128]{2,1,0:T(8,128)S(1)}, u32[]{:S(2)}, u32[]{:S(2)}) collective-permute-start(f32[8,8,128]{2,1,0:T(8,128)S(1)} %get-tuple-element.56), channel_id=1, source_target_pairs={{0,16},{16,0},{1,17},{17,1},{2,18},{18,2},{3,19},{19,3},{4,20},{20... | collective-permute-start | bytes 98312 | tf_op jit(solution)/shard_map/ppermute | solution.py:805
  5.7 0.1 collective-permute-start.3
  5.7 0.7 %shard_map.114.planes.own_planes = f32[22,16,128]{2,1,0:T(8,128)S(1)} custom-call(f32[48,16,128]{2,1,0:T(8,128)S(1)} %get-tuple-element.46.s, bf16[48,16,128]{2,1,0:T(8,128)(2,1)S(1)} %get-tuple-element.47.es, bf16[48,16,128]{2,1,0:T(8,128)(2,1)S(1)} %get-tuple-element.48.ns, bf16[48,16,128]{2,1,0:T(8,128)(2,1)S(1)} %get-tuple-element.49.mix, ...), custom_call_target="tpu_custom_call" | custom-call | tf_op jit(solution)/shard_map/pallas_call | solution.py:23
  6.5 1.1 %collective-permute-done.corners_n.corners_s = f32[8,8,128]{2,1,0:T(8,128)S(1)} collective-permute-done((f32[8,8,128]{2,1,0:T(8,128)S(1)}, f32[8,8,128]{2,1,0:T(8,128)S(1)}, u32[]{:S(2)}, u32[]{:S(2)}) %collective-permute-start) | collective-permute-done | bytes 32800 | tf_op jit(solution)/shard_map/ppermute | solution.py:805
  7.5 0.1 shard_map.115
  7.7 3.4 %collective-permute-start.2 = (f32[216,128]{1,0:T(8,128)S(1)}, f32[216,128]{1,0:T(8,128)S(1)}, u32[]{:S(2)}, u32[]{:S(2)}) collective-permute-start(f32[216,128]{1,0:T(8,128)S(1)} %get-tuple-element.65), channel_id=1, source_target_pairs={{0,15},{1,2},{2,1},{3,4},{4,3},{5,6},{6,5},{7,8},{8,7},{9,10},{10,... | collective-permute-start | bytes 331784 | tf_op jit(solution)/shard_map/ppermute | solution.py:813
  11.1 0.0 collective-permute-start.1
  11.1 0.9 %shard_map.116 = (f32[48,16,128]{2,1,0:T(8,128)S(1)}, f32[48,16,128]{2,1,0:T(8,128)S(1)}, f32[48,16,128]{2,1,0:T(8,128)S(1)}, f32[48,16,128]{2,1,0:T(8,128)S(1)}...) custom-call(f32[48,16,128]{2,1,0:T(8,128)S(1)} %get-tuple-element.46, ...), custom_call_target="tpu_custom_call" | custom-call | flops 1000000000 | tf_op jit(solution)/shard_map/pallas_call | solution.py:23
  11.9 0.4 %collective-permute-done.1.from_one = f32[208,128]{1,0:T(8,128)S(1)} collective-permute-done((f32[208,128]{1,0:T(8,128)S(1)}, f32[208,128]{1,0:T(8,128)S(1)}, u32[]{:S(2)}, u32[]{:S(2)}) %collective-permute-start.1) | collective-permute-done | bytes 106528 | tf_op jit(solution)/shard_map/ppermute | solution.py:813
  12.4 2.2 %collective-permute-done.2.from_two = f32[216,128]{1,0:T(8,128)S(1)} collective-permute-done((f32[216,128]{1,0:T(8,128)S(1)}, f32[216,128]{1,0:T(8,128)S(1)}, u32[]{:S(2)}, u32[]{:S(2)}) %collective-permute-start.2) | collective-permute-done | bytes 110624 | tf_op jit(solution)/shard_map/ppermute | solution.py:813
  14.6 0.0 collective-permute-done.3.rows_n.rows_s
  14.6 5.2 %shard_map.117 = (f32[48,32,128]{2,1,0:T(8,128)S(1)}, f32[48,32,128]{2,1,0:T(8,128)S(1)}, f32[48,32,128]{2,1,0:T(8,128)S(1)}, f32[48,32,128]{2,1,0:T(8,128)S(1)}...) custom-call(f32[48,16,128]{2,1,0:T(8,128)S(1)} %get-tuple-element.46, ...), custom_call_target="tpu_custom_call" | custom-call | tf_op jit(solution)/shard_map/pallas_call | solution.py:23
  19.8 2.4 %collective-permute-start.4 = (f32[27,8,128]{2,1,0:T(8,128)S(1)}, f32[27,8,128]{2,1,0:T(8,128)S(1)}, u32[]{:S(2)}, u32[]{:S(2)}) collective-permute-start(f32[27,8,128]{2,1,0:T(8,128)S(1)} %get-tuple-element.89), channel_id=1, source_target_pairs={{0,16},{16,0},{1,17},{17,1},{2,18},{18,2},{3,19},{19,3},{4,20},{20... | collective-permute-start | bytes 331784 | tf_op jit(solution)/shard_map/ppermute | solution.py:805
  22.2 1.7 %shard_map.118 = (f32[48,16,256]{2,1,0:T(8,128)S(1)}, f32[48,16,128]{2,1,0:T(8,128)S(1)}, f32[48,16,128]{2,1,0:T(8,128)S(1)}, f32[48,16,128]{2,1,0:T(8,128)S(1)}) custom-call(f32[48,16,128]{2,1,0:T(8,128)S(1)} %get-tuple-element.58.ep, f32[48,16,128]{2,1,0:T(8,128)S(1)} %get-tuple-element.59.em, f32[48,16,128]{2,1,0:T(8,128)S(1)} %get-tuple-element.60.np_, ...), custom_call_target="tpu_custom_call" | custom-call | bytes 8388608 | tf_op jit(solution)/shard_map/pallas_call | solution.py:23
  23.9 1.0 %collective-permute-done.4.rows_n.rows_s = f32[27,8,128]{2,1,0:T(8,128)S(1)} collective-permute-done((f32[27,8,128]{2,1,0:T(8,128)S(1)}, f32[27,8,128]{2,1,0:T(8,128)S(1)}, u32[]{:S(2)}, u32[]{:S(2)}) %collective-permute-start.4) | collective-permute-done | bytes 110624 | tf_op jit(solution)/shard_map/ppermute | solution.py:805
  24.9 2.2 %shard_map.119 = (f32[48,16,128]{2,1,0:T(8,128)}, f32[48,16,128]{2,1,0:T(8,128)}) custom-call(f32[48,16,128]{2,1,0:T(8,128)S(1)} %get-tuple-element.58.ep, f32[48,16,128]{2,1,0:T(8,128)S(1)} %get-tuple-element.59.em, f32[48,16,128]{2,1,0:T(8,128)S(1)} %get-tuple-element.60.np_, f32[48,16,128]{2,1,0:T(8,128)S(1)} %get-tuple-element.61.nm, ...), custom_call_target="tpu_custom_call" | custom-call | tf_op jit(solution)/shard_map/pallas_call | solution.py:23
Async XLA Ops:
  2.6 4.9 %collective-permute-start = (f32[8,8,128]{2,1,0:T(8,128)S(1)}, f32[8,8,128]{2,1,0:T(8,128)S(1)}, u32[]{:S(2)}, u32[]{:S(2)}) collective-permute-start(f32[8,8,128]{2,1,0:T(8,128)S(1)} %get-tuple-element.56), channel_id=1, source_target_pairs={{0,16},{16,0},{1,17},{17,1},{2,18},{18,2},{3,19},{19,3},{4,20},{20... | collective-permute-start | bytes 98312 | tf_op jit(solution)/shard_map/ppermute | solution.py:805
  5.7 9.0 %collective-permute-start.3 = (f32[73,8,128]{2,1,0:T(8,128)S(1)}, f32[73,8,128]{2,1,0:T(8,128)S(1)}, u32[]{:S(2)}, u32[]{:S(2)}) collective-permute-start(f32[73,8,128]{2,1,0:T(8,128)S(1)} %get-tuple-element.67), channel_id=1, source_target_pairs={{0,16},{16,0},{1,17},{17,1},{2,18},{18,2},{3,19},{19,3},{4,20},{20... | collective-permute-start | bytes 897032 | tf_op jit(solution)/shard_map/ppermute | solution.py:805
  7.7 6.9 %collective-permute-start.2 = (f32[216,128]{1,0:T(8,128)S(1)}, f32[216,128]{1,0:T(8,128)S(1)}, u32[]{:S(2)}, u32[]{:S(2)}) collective-permute-start(f32[216,128]{1,0:T(8,128)S(1)} %get-tuple-element.65), channel_id=1, source_target_pairs={{0,15},{1,2},{2,1},{3,4},{4,3},{5,6},{6,5},{7,8},{8,7},{9,10},{10,... | collective-permute-start | bytes 331784 | tf_op jit(solution)/shard_map/ppermute | solution.py:813
  11.1 1.3 %collective-permute-start.1 = (f32[208,128]{1,0:T(8,128)S(1)}, f32[208,128]{1,0:T(8,128)S(1)}, u32[]{:S(2)}, u32[]{:S(2)}) collective-permute-start(f32[208,128]{1,0:T(8,128)S(1)} %get-tuple-element.57.after), channel_id=1, source_target_pairs={{0,1},{1,0},{2,3},{3,2},{4,5},{5,4},{6,7},{7,6},{8,9},{9,8},{10,11... | collective-permute-start | bytes 319496 | tf_op jit(solution)/shard_map/ppermute | solution.py:813
  19.8 5.1 %collective-permute-start.4 = (f32[27,8,128]{2,1,0:T(8,128)S(1)}, f32[27,8,128]{2,1,0:T(8,128)S(1)}, u32[]{:S(2)}, u32[]{:S(2)}) collective-permute-start(f32[27,8,128]{2,1,0:T(8,128)S(1)} %get-tuple-element.89), channel_id=1, source_target_pairs={{0,16},{16,0},{1,17},{17,1},{2,18},{18,2},{3,19},{19,3},{4,20},{20... | collective-permute-start | bytes 331784 | tf_op jit(solution)/shard_map/ppermute | solution.py:805

commit v6 on v5

--- a/solution.py
+++ b/solution.py
@@ -233,6 +233,41 @@
         put(pl.ds(pairs * ny + h * 8, 8), x, y)
 
 
+def halves(x):
+    nx = x.shape[1] // 2
+    return x[:, :nx], x[:, nx:]
+
+
+def east(x):
+    main, side = halves(x)
+    lane = iota(main.shape, 1)
+    return jnp.concatenate(
+        [
+            jnp.where(lane == lane.shape[1] - 1, side, roll(main, -1, 1)),
+            jnp.where(lane == 0, main, roll(side, 1, 1)),
+        ],
+        axis=1,
+    )
+
+
+def west(x):
+    main, side = halves(x)
+    lane = iota(main.shape, 1)
+    return jnp.concatenate(
+        [
+            jnp.where(lane == 0, side, roll(main, 1, 1)),
+            jnp.where(lane == lane.shape[1] - 1, main, roll(side, -1, 1)),
+        ],
+        axis=1,
+    )
+
+
+def pull_x(main, side, ep, em, em_side):
+    lane = iota(main.shape, 1)
+    ge = jnp.where(lane == lane.shape[1] - 1, side, roll(main, -1, 1)) - main
+    return ep * ge + jnp.where(lane == 0, em_side * (main - side), roll(em * ge, 1, 1)), ge
+
+
 def extend(main, side, rows=None, corners=None):
     top = jnp.concatenate([main, side], axis=1)
     if rows is None:
@@ -289,8 +324,8 @@
 
 
 def part_of_pull(x, ep, em, damp):
-    ge = shift_up(x, 1) - x
-    return x * damp + ep * ge + shift_down(em * ge, 1), ge
+    ge = east(x) - x
+    return x * damp + ep * ge + west(em * ge), ge
 
 
 def local_kernel(
@@ -355,7 +390,9 @@
     target = iota((2 * nx, 2 * nx), 1)
     for u in range(STEPS):
         group = 2 * u + target // nx
-        hit = source == (target + 4 + GROUP * group) % nx
+        lane = target % nx
+        column = jnp.where(lane < 4, 3 - lane, jnp.where(lane >= nx - 4, nx + 3 - lane, -nx))
+        hit = source == GROUP * group + column
         moves_out[u] = jnp.where(hit, 1.0, 0.0).astype(jnp.bfloat16)
 
 
@@ -383,13 +420,20 @@
         return merge_rows(rows_n[index], rows_s[index])
 
     count_plane = len(NAMES) * plane_count
+    side_counts = jnp.dot(
+        jnp.concatenate([planes[count_plane]] + [corners[2 * plane_count]] * 2, axis=0).astype(
+            jnp.bfloat16
+        ),
+        moves[0, :nx, :nx],
+        preferred_element_type=F32,
+    )
     count_ext = extend(
         count[...].astype(F32),
-        roll(planes[count_plane], 124, 1),
+        side_counts[:ny],
         rim(levels + half),
-        roll(corners[2 * plane_count], 124, 1),
-    )
-    east_ext = step_count(count_ext, 1)
+        side_counts[ny : ny + 8],
+    )
+    east_ext = jnp.minimum(count_ext, east(count_ext))
     counts_out[0] = count_ext
     counts_out[1] = east_ext
     counts_out[2] = step_count(count_ext, 0)
@@ -454,10 +498,10 @@
             right = base - (fe - fe_west) - (fn - shift_down(fn, 0))
             return (right, link, np_s, nm_s, ep_s, em_s, sink_s, state), fe, fe_west
 
-        west, _, through_west = strips(True)
-        east, through_east, _ = strips(False)
-        seam = jnp.where(place == 3, through_east, through_west)
-        both = [jnp.where(low[: a.shape[0]], a, b) for a, b in zip(west, east)]
+        western, through_west, _ = strips(True)
+        eastern, _, through_east = strips(False)
+        seam = jnp.where(place == 3, through_west, through_east)
+        both = [jnp.where(low[: a.shape[0]], a, b) for a, b in zip(western, eastern)]
         right, link, np_c, nm_c = (x[ny:] for x in both[:4])
         corner = pair_rows(right, link)
         corner = jnp.where((small_sub == 3) | (small_sub == 4), roll(seam[ny:], 4, 0), corner)
@@ -586,9 +630,9 @@
         return lambda k: extend(own[k], halo[k, :ny])
 
     def spread(state, ep, em, np_, nm):
-        fe = ep * state + em * shift_up(state, 1)
+        fe = ep * state + em * east(state)
         fn = np_ * state + nm * shift_up(state, 0)
-        return (fe - shift_down(fe, 1)) + (fn - shift_down(fn, 0))
+        return (fe - west(fe)) + (fn - shift_down(fn, 0))
 
     def both(one):
         def use(t, m, u, top, low):
@@ -624,18 +668,18 @@
     def rim_part(k, solved):
         solved_out[k] = solved
         x = edge_rows(solved)
-        rows_of = lambda own, halo: edge_rows(inner(own, halo)(k))
-        part, _ = part_of_pull(
-            x, rows_of(ep, ep_halo), rows_of(em, em_halo), edge_rows(damp_out[k])
-        )
-        gn = shift_up(x, 0) - x
-        sub = sublane(x.shape)
+        main, side = halves(x)
+        rows_of = lambda ref: edge_rows(ref[k])
+        part, _ = pull_x(main, side, rows_of(ep), rows_of(em), edge_rows(em_halo[k, :ny]))
+        part = part + main * edge_rows(damp_out[k, :, :nx])
+        gn = shift_up(main, 0) - main
+        sub = sublane(main.shape)
         part = part + jnp.where(
             sub == 0,
-            rows_of(np_, np_halo) * gn,
-            jnp.where(sub == 7, shift_down(rows_of(nm, nm_halo) * gn, 0), 0.0),
+            rows_of(np_) * gn,
+            jnp.where(sub == 7, shift_down(rows_of(nm) * gn, 0), 0.0),
         )
-        return pair_rows(x, part)
+        return jnp.concatenate([pair_rows(main, part), side], axis=1)
 
     group = iota((8, nx), 1) // GROUP
 
@@ -674,7 +718,7 @@
         open_north = level < counts[2, :ny, :nx]
 
         def slopes(state):
-            run = (shift_up(state[:ny], 1) - state[:ny])[:, :nx]
+            run = (east(state[:ny]) - state[:ny])[:, :nx]
             rise = shift_up(state[:, :nx], 0)[:ny] - state[:ny, :nx]
             return jnp.where(open_east, run, 0.0), jnp.where(open_north, rise, 0.0)
 
@@ -746,16 +790,15 @@
     ends = lax.fori_loop(0, half // STEPS, late_steps, (zero, zero), unroll=2)
 
     def early(k, x):
-        inner = x[:ny]
-        ge = shift_up(inner, 1) - inner
-        result = inner[:, :nx] * damp[k] + ep[k] * ge[:, :nx]
-        result = result + shift_down(extend(em[k], em_halo[k, :ny]) * ge, 1)[:, :nx]
+        main, side = halves(x[:ny])
+        flow, ge = pull_x(main, side, ep[k], em[k], em_halo[k, :ny])
+        result = main * damp[k] + flow
         column = x[:, :nx]
         gn = shift_up(column, 0) - column
         minus = jnp.concatenate([nm[k], nm_halo[k, ny + 8 :]], axis=0)
         result = result + np_[k] * gn[:ny] + shift_down(minus * gn, 0)[:ny]
         adjoint[k] = result
-        gradient[k] = -(gradient[k] + ge[:, :nx] * run[k] + gn[:ny] * rise[k])
+        gradient[k] = -(gradient[k] + ge * run[k] + gn[:ny] * rise[k])
 
     def copies(p):
         out = []

time: 27.4 us -> 27 us (0.985)
  Pallas kernels: 12.8 us -> 12.1 us
  waiting for transfers between devices: 4.81 us -> 5.13 us
    pallas_call x7, Pallas kernels: 12.8 us -> 12.1 us  [call(): pl.pallas_call(kernel, out_shape=[typed(x) for x in outs], in_specs=[spac...]
    ppermute x3, waiting for transfers between devices: 2.15 us -> 2.46 us  [both_ways(): from_north = lax.ppermute(x, 'ty', ring('ty', -1))]
  transfers between devices with their start and end apart: 5 -> 5, of which waited for: 4 -> 4; matrix products, arithmetic and copies ran while one was open for 0% -> 0% of each run, Pallas kernels for 12% -> 11%
where the time goes in v6:
time: 27 us; the launch traced here: 26.8 us
  Pallas kernels  12.1 us (45%)
  starting transfers between devices  8.88 us (33%)
  waiting for transfers between devices  5.13 us (19%)
  between operations  0.68 us (3%)
    pallas_call x7, Pallas kernels, call(): pl.pallas_call(kernel, out_shape=[typed(x) for x in outs], in_specs=[spac...  12.1 us
    ppermute x3, starting transfers between devices, both_ways(): from_north = lax.ppermute(x, 'ty', ring('ty', -1))  5.49 us
    ppermute x2, starting transfers between devices, swap(): lax.ppermute(x, 'tx', [(i, (i + 1) % nx if i % 2 == phase else (i - 1) %...  3.39 us
    ppermute x2, waiting for transfers between devices, swap(): lax.ppermute(x, 'tx', [(i, (i + 1) % nx if i % 2 == phase else (i - 1) %...  2.67 us
    ppermute x3, waiting for transfers between devices, both_ways(): from_north = lax.ppermute(x, 'ty', ring('ty', -1))  2.46 us
  transfers between devices with their start and end apart: 5, of which 4 were waited for; matrix products, arithmetic and copies ran while one was open for 0% of the time, Pallas kernels for 11%

profile of v6, /device:TPU:0, one launch (start us, length us, event | category | flops | bytes accessed | tf_op | source)
XLA Modules:
  0.0 26.8 jit_solution(2882273974068199245)
XLA Ops:
  0.6 2.0 %shard_map.113 = (f32[48,16,128]{2,1,0:T(8,128)S(1)}, bf16[48,16,128]{2,1,0:T(8,128)(2,1)S(1)}, bf16[48,16,128]{2,1,0:T(8,128)(2,1)S(1)}, bf16[48,16,128]{2,1,0:...) custom-call(f32[48,16,128]{2,1,0:T(8,128)} %args_0_.4, ...), custom_call_target="tpu_custom_call" | custom-call | tf_op jit(solution)/shard_map/pallas_call | solution.py:23
  2.6 3.0 %collective-permute-start = (f32[8,8,128]{2,1,0:T(8,128)S(1)}, f32[8,8,128]{2,1,0:T(8,128)S(1)}, u32[]{:S(2)}, u32[]{:S(2)}) collective-permute-start(f32[8,8,128]{2,1,0:T(8,128)S(1)} %get-tuple-element.56), channel_id=1, source_target_pairs={{0,16},{16,0},{1,17},{17,1},{2,18},{18,2},{3,19},{19,3},{4,20},{20... | collective-permute-start | bytes 98312 | tf_op jit(solution)/shard_map/ppermute | solution.py:848
  5.7 0.1 collective-permute-start.3
  5.7 0.7 %shard_map.114.planes.own_planes = f32[22,16,128]{2,1,0:T(8,128)S(1)} custom-call(f32[48,16,128]{2,1,0:T(8,128)S(1)} %get-tuple-element.46.s, bf16[48,16,128]{2,1,0:T(8,128)(2,1)S(1)} %get-tuple-element.47.es, bf16[48,16,128]{2,1,0:T(8,128)(2,1)S(1)} %get-tuple-element.48.ns, bf16[48,16,128]{2,1,0:T(8,128)(2,1)S(1)} %get-tuple-element.49.mix, ...), custom_call_target="tpu_custom_call" | custom-call | tf_op jit(solution)/shard_map/pallas_call | solution.py:23
  6.5 1.1 %collective-permute-done.corners_n.corners_s = f32[8,8,128]{2,1,0:T(8,128)S(1)} collective-permute-done((f32[8,8,128]{2,1,0:T(8,128)S(1)}, f32[8,8,128]{2,1,0:T(8,128)S(1)}, u32[]{:S(2)}, u32[]{:S(2)}) %collective-permute-start) | collective-permute-done | bytes 32800 | tf_op jit(solution)/shard_map/ppermute | solution.py:848
  7.5 0.1 shard_map.115
  7.7 3.4 %collective-permute-start.2 = (f32[216,128]{1,0:T(8,128)S(1)}, f32[216,128]{1,0:T(8,128)S(1)}, u32[]{:S(2)}, u32[]{:S(2)}) collective-permute-start(f32[216,128]{1,0:T(8,128)S(1)} %get-tuple-element.65), channel_id=1, source_target_pairs={{0,15},{1,2},{2,1},{3,4},{4,3},{5,6},{6,5},{7,8},{8,7},{9,10},{10,... | collective-permute-start | bytes 331784 | tf_op jit(solution)/shard_map/ppermute | solution.py:856
  11.1 0.0 collective-permute-start.1
  11.1 0.9 %shard_map.116 = (f32[48,16,128]{2,1,0:T(8,128)S(1)}, f32[48,16,128]{2,1,0:T(8,128)S(1)}, f32[48,16,128]{2,1,0:T(8,128)S(1)}, f32[48,16,128]{2,1,0:T(8,128)S(1)}...) custom-call(f32[48,16,128]{2,1,0:T(8,128)S(1)} %get-tuple-element.46, ...), custom_call_target="tpu_custom_call" | custom-call | flops 1000000000 | tf_op jit(solution)/shard_map/pallas_call | solution.py:23
  11.9 0.4 %collective-permute-done.1.from_one = f32[208,128]{1,0:T(8,128)S(1)} collective-permute-done((f32[208,128]{1,0:T(8,128)S(1)}, f32[208,128]{1,0:T(8,128)S(1)}, u32[]{:S(2)}, u32[]{:S(2)}) %collective-permute-start.1) | collective-permute-done | bytes 106528 | tf_op jit(solution)/shard_map/ppermute | solution.py:856
  12.4 2.2 %collective-permute-done.2.from_two = f32[216,128]{1,0:T(8,128)S(1)} collective-permute-done((f32[216,128]{1,0:T(8,128)S(1)}, f32[216,128]{1,0:T(8,128)S(1)}, u32[]{:S(2)}, u32[]{:S(2)}) %collective-permute-start.2) | collective-permute-done | bytes 110624 | tf_op jit(solution)/shard_map/ppermute | solution.py:856
  14.6 0.0 collective-permute-done.3.rows_n.rows_s
  14.6 4.8 %shard_map.117 = (f32[48,32,128]{2,1,0:T(8,128)S(1)}, f32[48,32,128]{2,1,0:T(8,128)S(1)}, f32[48,32,128]{2,1,0:T(8,128)S(1)}, f32[48,32,128]{2,1,0:T(8,128)S(1)}...) custom-call(f32[48,16,128]{2,1,0:T(8,128)S(1)} %get-tuple-element.46, ...), custom_call_target="tpu_custom_call" | custom-call | tf_op jit(solution)/shard_map/pallas_call | solution.py:23
  19.5 2.4 %collective-permute-start.4 = (f32[27,8,128]{2,1,0:T(8,128)S(1)}, f32[27,8,128]{2,1,0:T(8,128)S(1)}, u32[]{:S(2)}, u32[]{:S(2)}) collective-permute-start(f32[27,8,128]{2,1,0:T(8,128)S(1)} %get-tuple-element.89), channel_id=1, source_target_pairs={{0,16},{16,0},{1,17},{17,1},{2,18},{18,2},{3,19},{19,3},{4,20},{20... | collective-permute-start | bytes 331784 | tf_op jit(solution)/shard_map/ppermute | solution.py:848
  21.8 1.4 %shard_map.118 = (f32[48,16,256]{2,1,0:T(8,128)S(1)}, f32[48,16,128]{2,1,0:T(8,128)S(1)}, f32[48,16,128]{2,1,0:T(8,128)S(1)}, f32[48,16,128]{2,1,0:T(8,128)S(1)}) custom-call(f32[48,16,128]{2,1,0:T(8,128)S(1)} %get-tuple-element.58.ep, f32[48,16,128]{2,1,0:T(8,128)S(1)} %get-tuple-element.59.em, f32[48,16,128]{2,1,0:T(8,128)S(1)} %get-tuple-element.60.np_, ...), custom_call_target="tpu_custom_call" | custom-call | bytes 8388608 | tf_op jit(solution)/shard_map/pallas_call | solution.py:23
  23.2 1.4 %collective-permute-done.4.rows_n.rows_s = f32[27,8,128]{2,1,0:T(8,128)S(1)} collective-permute-done((f32[27,8,128]{2,1,0:T(8,128)S(1)}, f32[27,8,128]{2,1,0:T(8,128)S(1)}, u32[]{:S(2)}, u32[]{:S(2)}) %collective-permute-start.4) | collective-permute-done | bytes 110624 | tf_op jit(solution)/shard_map/ppermute | solution.py:848
  24.6 2.2 %shard_map.119 = (f32[48,16,128]{2,1,0:T(8,128)}, f32[48,16,128]{2,1,0:T(8,128)}) custom-call(f32[48,16,128]{2,1,0:T(8,128)S(1)} %get-tuple-element.58.ep, f32[48,16,128]{2,1,0:T(8,128)S(1)} %get-tuple-element.59.em, f32[48,16,128]{2,1,0:T(8,128)S(1)} %get-tuple-element.60.np_, f32[48,16,128]{2,1,0:T(8,128)S(1)} %get-tuple-element.61.nm, ...), custom_call_target="tpu_custom_call" | custom-call | tf_op jit(solution)/shard_map/pallas_call | solution.py:23
Async XLA Ops:
  2.6 4.9 %collective-permute-start = (f32[8,8,128]{2,1,0:T(8,128)S(1)}, f32[8,8,128]{2,1,0:T(8,128)S(1)}, u32[]{:S(2)}, u32[]{:S(2)}) collective-permute-start(f32[8,8,128]{2,1,0:T(8,128)S(1)} %get-tuple-element.56), channel_id=1, source_target_pairs={{0,16},{16,0},{1,17},{17,1},{2,18},{18,2},{3,19},{19,3},{4,20},{20... | collective-permute-start | bytes 98312 | tf_op jit(solution)/shard_map/ppermute | solution.py:848
  5.7 9.0 %collective-permute-start.3 = (f32[73,8,128]{2,1,0:T(8,128)S(1)}, f32[73,8,128]{2,1,0:T(8,128)S(1)}, u32[]{:S(2)}, u32[]{:S(2)}) collective-permute-start(f32[73,8,128]{2,1,0:T(8,128)S(1)} %get-tuple-element.67), channel_id=1, source_target_pairs={{0,16},{16,0},{1,17},{17,1},{2,18},{18,2},{3,19},{19,3},{4,20},{20... | collective-permute-start | bytes 897032 | tf_op jit(solution)/shard_map/ppermute | solution.py:848
  7.7 6.9 %collective-permute-start.2 = (f32[216,128]{1,0:T(8,128)S(1)}, f32[216,128]{1,0:T(8,128)S(1)}, u32[]{:S(2)}, u32[]{:S(2)}) collective-permute-start(f32[216,128]{1,0:T(8,128)S(1)} %get-tuple-element.65), channel_id=1, source_target_pairs={{0,15},{1,2},{2,1},{3,4},{4,3},{5,6},{6,5},{7,8},{8,7},{9,10},{10,... | collective-permute-start | bytes 331784 | tf_op jit(solution)/shard_map/ppermute | solution.py:856
  11.1 1.3 %collective-permute-start.1 = (f32[208,128]{1,0:T(8,128)S(1)}, f32[208,128]{1,0:T(8,128)S(1)}, u32[]{:S(2)}, u32[]{:S(2)}) collective-permute-start(f32[208,128]{1,0:T(8,128)S(1)} %get-tuple-element.57.after), channel_id=1, source_target_pairs={{0,1},{1,0},{2,3},{3,2},{4,5},{5,4},{6,7},{7,6},{8,9},{9,8},{10,11... | collective-permute-start | bytes 319496 | tf_op jit(solution)/shard_map/ppermute | solution.py:856
  19.5 5.1 %collective-permute-start.4 = (f32[27,8,128]{2,1,0:T(8,128)S(1)}, f32[27,8,128]{2,1,0:T(8,128)S(1)}, u32[]{:S(2)}, u32[]{:S(2)}) collective-permute-start(f32[27,8,128]{2,1,0:T(8,128)S(1)} %get-tuple-element.89), channel_id=1, source_target_pairs={{0,16},{16,0},{1,17},{17,1},{2,18},{18,2},{3,19},{19,3},{4,20},{20... | collective-permute-start | bytes 331784 | tf_op jit(solution)/shard_map/ppermute | solution.py:848

commit v7 on v6

--- a/solution.py
+++ b/solution.py
@@ -144,6 +144,7 @@
     half = per_plane // 2
     plane_count = levels // per_plane
     counts = edge_rows(count[...].astype(F32))
+    sub = sublane(small)
 
     def rims(p, carry):
         acc = jnp.zeros(small, F32)
@@ -161,6 +162,7 @@
                 rows[2 * t + j] = first
                 place = 2 * g + j
                 acc = jnp.where(group == place, roll(first, GROUP * place + 4, 1), acc)
+                second = jnp.where((sub == 3) | (sub == 4), roll(counts, 4, 0), second)
                 late = jnp.where(group == place, roll(second, GROUP * place + 4, 1), late)
             rows[levels + t] = two_levels(*seconds)
         corners[p] = acc
@@ -169,9 +171,6 @@
 
     lax.fori_loop(0, plane_count, rims, 0)
     rows[levels + levels // 2] = counts
-    corners[2 * plane_count] = in_all_groups(counts)
-    for p in range(2 * plane_count + 1, corners.shape[0]):
-        corners[p] = jnp.zeros(small, F32)
     for i in rest:
         copies[i].wait()
 
@@ -184,18 +183,28 @@
     shape = s.shape[1:]
     group = iota(shape, 1) // GROUP
 
+    place = iota(shape, 1) % GROUP
+
     def columns(p, carry):
-        for a, name in enumerate(NAMES):
+        packed = []
+        for name in NAMES:
             acc = jnp.zeros(shape, F32)
             for g in range(per_plane):
                 pair = level_pair(levels, p * (per_plane // 2) + g // 2)
                 x = refs[name][pair[g % 2][name == "vm"]].astype(F32)
                 acc = jnp.where(group == g, roll(x, GROUP * g + 4, 1), acc)
-            planes[a * plane_count + p] = acc
+            packed.append(acc)
+        seen = packed.pop()
+        for name, distance in (("ns", 2), ("relax", 3)):
+            i = NAMES.index(name)
+            x = jnp.where(place == 0, roll(seen, -distance, 1), packed[i])
+            packed[i] = jnp.where(place == GROUP - 1, roll(seen, distance, 1), x)
+        for a, x in enumerate(packed):
+            planes[a * plane_count + p] = x
         return carry
 
     lax.fori_loop(0, plane_count, columns, 0)
-    total = len(NAMES) * plane_count
+    total = len(NAMES[:6]) * plane_count
     planes[total] = in_all_groups(count[...].astype(F32))
     for p in range(total + 1, planes.shape[0]):
         planes[p] = jnp.zeros(shape, F32)
@@ -221,8 +230,6 @@
         put(pl.ds(h * ny, ny), planes[2 * h], planes[2 * h + 1])
 
     count = corners_n.shape[0]
-    two[pl.ds(one.shape[0], 8)] = jnp.zeros((8, one.shape[1]), F32)
-
     def corner(p):
         return merge_rows(corners_n[p], corners_s[p])
 
@@ -419,9 +426,9 @@
     def rim(index):
         return merge_rows(rows_n[index], rows_s[index])
 
-    count_plane = len(NAMES) * plane_count
+    count_plane = len(NAMES[:6]) * plane_count
     side_counts = jnp.dot(
-        jnp.concatenate([planes[count_plane]] + [corners[2 * plane_count]] * 2, axis=0).astype(
+        jnp.concatenate([planes[count_plane]] + [roll(corners[plane_count], 4, 0)] * 2, axis=0).astype(
             jnp.bfloat16
         ),
         moves[0, :nx, :nx],
@@ -478,7 +485,7 @@
                 x[name] = side_and_corner(side[name], x[name])
             counts = side_and_corner(
                 pick(planes[count_plane], own_planes[count_plane]),
-                pick(corners[2 * plane_count], own_corners[2 * plane_count]),
+                roll(pick(corners[plane_count + p], own_corners[plane_count + p]), 4, 0),
             )
             state = x["s"]
             open_east = level < step_count(counts, 1)
@@ -508,7 +515,12 @@
         corner = jnp.where(small_sub == 5, roll(np_c, 6, 0), corner)
         corner = jnp.where(small_sub == 6, roll(nm_c, 7, 0), corner)
         both = [x[:ny] for x in both]
-        seen = planes[NAMES.index("obs") * plane_count + p]
+        near_seam = planes[NAMES.index("relax") * plane_count + p]
+        further = planes[NAMES.index("ns") * plane_count + p]
+        side_place = place[:ny]
+        seen = jnp.where(side_place < 3, roll(further, 2, 1), roll(near_seam, 3, 1))
+        beyond = jnp.where(side_place > 4, roll(further, -2, 1), roll(near_seam, -3, 1))
+        seen = jnp.where(side_place < 4, seen, beyond)
         both = both[:2] + [seam[:ny], seen] + both[2:] + [jnp.concatenate([corner] * 2, axis=0)]
         for i, x in enumerate(both):
             split(p, i * ny, x)
@@ -681,18 +693,21 @@
         )
         return jnp.concatenate([pair_rows(main, part), side], axis=1)
 
-    group = iota((8, nx), 1) // GROUP
+    lane8 = iota((8, nx), 1)
 
     def to_send(t, m, u, top, low):
         pair = two_levels(rim_part(t, top), rim_part(levels - 1 - t, low))
         send[t] = pair[:, :nx]
         before = jnp.zeros((8, nx), F32) if u == STEPS - 1 else sides[m]
-        moved = roll(pair[:, nx:], 2 * GROUP * u + 4, 1)
-        sides[m] = jnp.where(group == 2 * u, moved, before)
+        moved = roll(pair[:, nx:], 2 * u + 1, 1)
+        sides[m] = jnp.where(lane8 // 2 == u, moved, before)
 
     solve_outward(levels, ends, ratio, join[:ny], main, to_send)
-    for p in range(half // 8):
-        send[half + p] = jnp.where(group % 2 == 0, sides[2 * p], roll(sides[2 * p + 1], GROUP, 1))
+    both_sides = sides[0]
+    for m in range(1, half // STEPS):
+        place = m * 2 * STEPS
+        both_sides = jnp.where(lane8 < place, both_sides, roll(sides[m], place, 1))
+    send[half] = both_sides
 
 
 def inner_kernel(
@@ -740,15 +755,14 @@
     half = levels // 2
     sub = sublane((8, width))
 
-    for p in range(half // 8):
-        side = merge_rows(rows_n[half + p], rows_s[half + p])
-        sides[2 * p] = side
-        sides[2 * p + 1] = roll(side, -GROUP, 1)
+    side = merge_rows(rows_n[half], rows_s[half])
+    for m in range(half // STEPS):
+        sides[m] = roll(side, -2 * STEPS * m, 1)
 
     def rims(m, u):
         t = m * STEPS + u
         line = merge_rows(rows_n[t], rows_s[t])
-        corner = roll(sides[m], 124 - 2 * GROUP * u, 1)
+        corner = roll(sides[m], -1 - 2 * u, 1)
         both = jnp.concatenate([line, corner], axis=1)
         return both, roll(both, 4, 0)
 
@@ -873,13 +887,13 @@
     levels, ny, nx = tracer_start.shape
     per_plane = 128 // GROUP
     plane_count = levels // per_plane
-    pairs = (len(NAMES) * plane_count + 2) // 2
+    pairs = (len(NAMES[:6]) * plane_count + 2) // 2
     fields = (
         tracer_start, east_speed, north_speed, mixing, relax_rate, vertical_mixing, observed,
         level_count, face_east, face_north,
     )
     half = levels // 2
-    corner_planes = 2 * plane_count + 2
+    corner_planes = 2 * plane_count
     *fields, rows, corners = call(
         rim_kernel,
         [jax.ShapeDtypeStruct(x.shape, x.dtype) for x in fields]
@@ -893,7 +907,7 @@
     (planes,) = call(column_kernel, [(2 * pairs, ny, nx)], [], *fields[:8])
     packed = (pairs * ny + corner_planes // 2 * 8, nx)
     one, two, own_corners = call(
-        halves_kernel, [packed, (packed[0] + 8, nx), corners.shape], [],
+        halves_kernel, [packed, packed, corners.shape], [],
         planes, corners_n, corners_s,
         cost=pl.CostEstimate(flops=10**10, bytes_accessed=0, transcendentals=0),
     )
@@ -915,7 +929,7 @@
     outs = call(
         forward_kernel,
         [halo] * 4 + [own] + [halo] * 4 + [ext, block, block, (3,) + ext[1:], ext[1:]]
-        + [(half + half // 8, 8, nx)],
+        + [(half + 1, 8, nx)],
         [
             planes.shape,
             corners.shape,

time: 27 us -> 26.5 us (0.981)
  waiting for transfers between devices: 5.13 us -> 4.68 us
    ppermute x3, waiting for transfers between devices: 2.46 us -> 2.18 us  [both_ways(): from_north = lax.ppermute(x, 'ty', ring('ty', -1))]
  transfers between devices with their start and end apart: 5 -> 5, of which waited for: 4 -> 3; matrix products, arithmetic and copies ran while one was open for 0% -> 0% of each run, Pallas kernels for 11% -> 12%
where the time goes in v7:
time: 26.5 us; the launch traced here: 26.2 us
  Pallas kernels  12.1 us (46%)
  starting transfers between devices  8.79 us (33%)
  waiting for transfers between devices  4.68 us (18%)
  between operations  0.68 us (3%)
    pallas_call x7, Pallas kernels, call(): pl.pallas_call(kernel, out_shape=[typed(x) for x in outs], in_specs=[spac...  12.1 us
    ppermute x3, starting transfers between devices, both_ways(): from_north = lax.ppermute(x, 'ty', ring('ty', -1))  5.4 us
    ppermute x2, starting transfers between devices, swap(): lax.ppermute(x, 'tx', [(i, (i + 1) % nx if i % 2 == phase else (i - 1) %...  3.39 us
    ppermute x2, waiting for transfers between devices, swap(): lax.ppermute(x, 'tx', [(i, (i + 1) % nx if i % 2 == phase else (i - 1) %...  2.5 us
    ppermute x3, waiting for transfers between devices, both_ways(): from_north = lax.ppermute(x, 'ty', ring('ty', -1))  2.18 us
  transfers between devices with their start and end apart: 5, of which 3 were waited for; matrix products, arithmetic and copies ran while one was open for 0% of the time, Pallas kernels for 12%

profile of v7, /device:TPU:0, one launch (start us, length us, event | category | flops | bytes accessed | tf_op | source)
XLA Modules:
  0.0 26.2 jit_solution(3074574193732149394)
XLA Ops:
  0.6 2.0 %shard_map.113 = (f32[48,16,128]{2,1,0:T(8,128)S(1)}, bf16[48,16,128]{2,1,0:T(8,128)(2,1)S(1)}, bf16[48,16,128]{2,1,0:T(8,128)(2,1)S(1)}, bf16[48,16,128]{2,1,0:...) custom-call(f32[48,16,128]{2,1,0:T(8,128)} %args_0_.4, ...), custom_call_target="tpu_custom_call" | custom-call | tf_op jit(solution)/shard_map/pallas_call | solution.py:23
  2.6 3.0 %collective-permute-start = (f32[6,8,128]{2,1,0:T(8,128)S(1)}, f32[6,8,128]{2,1,0:T(8,128)S(1)}, u32[]{:S(2)}, u32[]{:S(2)}) collective-permute-start(f32[6,8,128]{2,1,0:T(8,128)S(1)} %get-tuple-element.56), channel_id=1, source_target_pairs={{0,16},{16,0},{1,17},{17,1},{2,18},{18,2},{3,19},{19,3},{4,20},{20... | collective-permute-start | bytes 73736 | tf_op jit(solution)/shard_map/ppermute | solution.py:862
  5.6 0.1 collective-permute-start.3
  5.7 0.9 %shard_map.114.planes.own_planes = f32[20,16,128]{2,1,0:T(8,128)S(1)} custom-call(f32[48,16,128]{2,1,0:T(8,128)S(1)} %get-tuple-element.46.s, bf16[48,16,128]{2,1,0:T(8,128)(2,1)S(1)} %get-tuple-element.47.es, bf16[48,16,128]{2,1,0:T(8,128)(2,1)S(1)} %get-tuple-element.48.ns, bf16[48,16,128]{2,1,0:T(8,128)(2,1)S(1)} %get-tuple-element.49.mix, ...), custom_call_target="tpu_custom_call" | custom-call | tf_op jit(solution)/shard_map/pallas_call | solution.py:23
  6.6 0.8 %collective-permute-done.corners_n.corners_s = f32[6,8,128]{2,1,0:T(8,128)S(1)} collective-permute-done((f32[6,8,128]{2,1,0:T(8,128)S(1)}, f32[6,8,128]{2,1,0:T(8,128)S(1)}, u32[]{:S(2)}, u32[]{:S(2)}) %collective-permute-start) | collective-permute-done | bytes 24608 | tf_op jit(solution)/shard_map/ppermute | solution.py:862
  7.5 0.1 shard_map.115
  7.6 3.4 %collective-permute-start.2 = (f32[184,128]{1,0:T(8,128)S(1)}, f32[184,128]{1,0:T(8,128)S(1)}, u32[]{:S(2)}, u32[]{:S(2)}) collective-permute-start(f32[184,128]{1,0:T(8,128)S(1)} %get-tuple-element.65), channel_id=1, source_target_pairs={{0,15},{1,2},{2,1},{3,4},{4,3},{5,6},{6,5},{7,8},{8,7},{9,10},{10,... | collective-permute-start | bytes 282632 | tf_op jit(solution)/shard_map/ppermute | solution.py:870
  11.0 0.0 collective-permute-start.1
  11.0 0.9 %shard_map.116 = (f32[48,16,128]{2,1,0:T(8,128)S(1)}, f32[48,16,128]{2,1,0:T(8,128)S(1)}, f32[48,16,128]{2,1,0:T(8,128)S(1)}, f32[48,16,128]{2,1,0:T(8,128)S(1)}...) custom-call(f32[48,16,128]{2,1,0:T(8,128)S(1)} %get-tuple-element.46, ...), custom_call_target="tpu_custom_call" | custom-call | flops 1000000000 | tf_op jit(solution)/shard_map/pallas_call | solution.py:23
  11.8 2.5 %collective-permute-done.2.from_two = f32[184,128]{1,0:T(8,128)S(1)} collective-permute-done((f32[184,128]{1,0:T(8,128)S(1)}, f32[184,128]{1,0:T(8,128)S(1)}, u32[]{:S(2)}, u32[]{:S(2)}) %collective-permute-start.2) | collective-permute-done | bytes 94240 | tf_op jit(solution)/shard_map/ppermute | solution.py:870
  14.3 0.0 collective-permute-done.1.from_one
  14.3 0.0 collective-permute-done.3.rows_n.rows_s
  14.3 4.8 %shard_map.117 = (f32[48,32,128]{2,1,0:T(8,128)S(1)}, f32[48,32,128]{2,1,0:T(8,128)S(1)}, f32[48,32,128]{2,1,0:T(8,128)S(1)}, f32[48,32,128]{2,1,0:T(8,128)S(1)}...) custom-call(f32[48,16,128]{2,1,0:T(8,128)S(1)} %get-tuple-element.46, ...), custom_call_target="tpu_custom_call" | custom-call | tf_op jit(solution)/shard_map/pallas_call | solution.py:23
  19.2 2.3 %collective-permute-start.4 = (f32[25,8,128]{2,1,0:T(8,128)S(1)}, f32[25,8,128]{2,1,0:T(8,128)S(1)}, u32[]{:S(2)}, u32[]{:S(2)}) collective-permute-start(f32[25,8,128]{2,1,0:T(8,128)S(1)} %get-tuple-element.89), channel_id=1, source_target_pairs={{0,16},{16,0},{1,17},{17,1},{2,18},{18,2},{3,19},{19,3},{4,20},{20... | collective-permute-start | bytes 307208 | tf_op jit(solution)/shard_map/ppermute | solution.py:862
  21.4 1.3 %shard_map.118 = (f32[48,16,256]{2,1,0:T(8,128)S(1)}, f32[48,16,128]{2,1,0:T(8,128)S(1)}, f32[48,16,128]{2,1,0:T(8,128)S(1)}, f32[48,16,128]{2,1,0:T(8,128)S(1)}) custom-call(f32[48,16,128]{2,1,0:T(8,128)S(1)} %get-tuple-element.58.ep, f32[48,16,128]{2,1,0:T(8,128)S(1)} %get-tuple-element.59.em, f32[48,16,128]{2,1,0:T(8,128)S(1)} %get-tuple-element.60.np_, ...), custom_call_target="tpu_custom_call" | custom-call | bytes 8388608 | tf_op jit(solution)/shard_map/pallas_call | solution.py:23
  22.7 1.3 %collective-permute-done.4.rows_n.rows_s = f32[25,8,128]{2,1,0:T(8,128)S(1)} collective-permute-done((f32[25,8,128]{2,1,0:T(8,128)S(1)}, f32[25,8,128]{2,1,0:T(8,128)S(1)}, u32[]{:S(2)}, u32[]{:S(2)}) %collective-permute-start.4) | collective-permute-done | bytes 102432 | tf_op jit(solution)/shard_map/ppermute | solution.py:862
  24.1 2.2 %shard_map.119 = (f32[48,16,128]{2,1,0:T(8,128)}, f32[48,16,128]{2,1,0:T(8,128)}) custom-call(f32[48,16,128]{2,1,0:T(8,128)S(1)} %get-tuple-element.58.ep, f32[48,16,128]{2,1,0:T(8,128)S(1)} %get-tuple-element.59.em, f32[48,16,128]{2,1,0:T(8,128)S(1)} %get-tuple-element.60.np_, f32[48,16,128]{2,1,0:T(8,128)S(1)} %get-tuple-element.61.nm, ...), custom_call_target="tpu_custom_call" | custom-call | tf_op jit(solution)/shard_map/pallas_call | solution.py:23
Async XLA Ops:
  2.6 4.8 %collective-permute-start = (f32[6,8,128]{2,1,0:T(8,128)S(1)}, f32[6,8,128]{2,1,0:T(8,128)S(1)}, u32[]{:S(2)}, u32[]{:S(2)}) collective-permute-start(f32[6,8,128]{2,1,0:T(8,128)S(1)} %get-tuple-element.56), channel_id=1, source_target_pairs={{0,16},{16,0},{1,17},{17,1},{2,18},{18,2},{3,19},{19,3},{4,20},{20... | collective-permute-start | bytes 73736 | tf_op jit(solution)/shard_map/ppermute | solution.py:862
  5.6 8.7 %collective-permute-start.3 = (f32[73,8,128]{2,1,0:T(8,128)S(1)}, f32[73,8,128]{2,1,0:T(8,128)S(1)}, u32[]{:S(2)}, u32[]{:S(2)}) collective-permute-start(f32[73,8,128]{2,1,0:T(8,128)S(1)} %get-tuple-element.67), channel_id=1, source_target_pairs={{0,16},{16,0},{1,17},{17,1},{2,18},{18,2},{3,19},{19,3},{4,20},{20... | collective-permute-start | bytes 897032 | tf_op jit(solution)/shard_map/ppermute | solution.py:862
  7.6 6.8 %collective-permute-start.2 = (f32[184,128]{1,0:T(8,128)S(1)}, f32[184,128]{1,0:T(8,128)S(1)}, u32[]{:S(2)}, u32[]{:S(2)}) collective-permute-start(f32[184,128]{1,0:T(8,128)S(1)} %get-tuple-element.65), channel_id=1, source_target_pairs={{0,15},{1,2},{2,1},{3,4},{4,3},{5,6},{6,5},{7,8},{8,7},{9,10},{10,... | collective-permute-start | bytes 282632 | tf_op jit(solution)/shard_map/ppermute | solution.py:870
  11.0 3.4 %collective-permute-start.1 = (f32[184,128]{1,0:T(8,128)S(1)}, f32[184,128]{1,0:T(8,128)S(1)}, u32[]{:S(2)}, u32[]{:S(2)}) collective-permute-start(f32[184,128]{1,0:T(8,128)S(1)} %get-tuple-element.57.after), channel_id=1, source_target_pairs={{0,1},{1,0},{2,3},{3,2},{4,5},{5,4},{6,7},{7,6},{8,9},{9,8},{10,11... | collective-permute-start | bytes 282632 | tf_op jit(solution)/shard_map/ppermute | solution.py:870
  19.2 4.9 %collective-permute-start.4 = (f32[25,8,128]{2,1,0:T(8,128)S(1)}, f32[25,8,128]{2,1,0:T(8,128)S(1)}, u32[]{:S(2)}, u32[]{:S(2)}) collective-permute-start(f32[25,8,128]{2,1,0:T(8,128)S(1)} %get-tuple-element.89), channel_id=1, source_target_pairs={{0,16},{16,0},{1,17},{17,1},{2,18},{18,2},{3,19},{19,3},{4,20},{20... | collective-permute-start | bytes 307208 | tf_op jit(solution)/shard_map/ppermute | solution.py:862

commit v8 on v7

--- a/solution.py
+++ b/solution.py
@@ -98,7 +98,30 @@
     first = pair_rows(s, base)
     first = jnp.where((sub == 3) | (sub == 4), roll(tile["es"], 4, 0), first)
     first = jnp.where((sub == 5) | (sub == 6), roll(tile["mix"], 6, 0), first)
-    return first, pair_rows(tile["vm"], tile["ns"])
+    lane = iota(s.shape, 1)
+    fe = (0.5 * tile["es"] + tile["mix"]) * s
+    fe = fe + (0.5 * tile["es"] - tile["mix"]) * shift_up(s, 1)
+    fe = jnp.where((level < step_count(counts, 1)) & (lane < s.shape[1] - 1), fe, 0.0)
+    line = pair_rows(s, base - (fe - shift_down(fe, 1)))
+    line = jnp.where((sub == 3) | (sub == 4), roll(tile["vm"], 4, 0), line)
+    line = jnp.where(sub == 5, roll(tile["ns"], 6, 0), line)
+    line = jnp.where(sub == 6, roll(tile["mix"], 7, 0), line)
+    return line, first, pair_rows(tile["vm"], tile["ns"])
+
+
+def merge_lines(north, south):
+    sub = sublane(north.shape)
+    return jnp.where((sub == 0) | (sub == 2) | (sub == 4), north, south)
+
+
+def unpack_line(line):
+    return {
+        "s": line,
+        "base": roll(line, 6, 0),
+        "vm": roll(line, 4, 0),
+        "ns": roll(line, 2, 0),
+        "mix": roll(line, 1, 0),
+    }
 
 
 def unpack_rows(first, second):
@@ -128,7 +151,7 @@
 def rim_kernel(*args):
     fields = args[:10]
     s, es, ns, mix, relax, vm, obs, count, *_ = kept = args[10:20]
-    rows, corners, arrived = args[20:]
+    corners, arrived = args[20:]
     copies = [pltpu.make_async_copy(fields[i], kept[i], arrived.at[i]) for i in range(10)]
     first = (7, 0, 1, 2, 3, 4, 5)
     rest = (6, 8, 9)
@@ -151,31 +174,26 @@
         late = jnp.zeros(small, F32)
         for g in range(half):
             t = p * half + g
-            seconds = []
             for j, (k, link) in enumerate(level_pair(levels, t)):
-                first, second = pack_rows(
+                _, first, second = pack_rows(
                     lambda name: level_of(refs[name], name, link if name == "vm" else k),
                     counts,
                     k.astype(F32),
                 )
-                seconds.append(second)
-                rows[2 * t + j] = first
                 place = 2 * g + j
                 acc = jnp.where(group == place, roll(first, GROUP * place + 4, 1), acc)
                 second = jnp.where((sub == 3) | (sub == 4), roll(counts, 4, 0), second)
                 late = jnp.where(group == place, roll(second, GROUP * place + 4, 1), late)
-            rows[levels + t] = two_levels(*seconds)
         corners[p] = acc
         corners[plane_count + p] = late
         return carry
 
     lax.fori_loop(0, plane_count, rims, 0)
-    rows[levels + levels // 2] = counts
     for i in rest:
         copies[i].wait()
 
 
-def column_kernel(s, es, ns, mix, relax, vm, obs, count, planes):
+def column_kernel(s, es, ns, mix, relax, vm, obs, count, planes, rows):
     refs = dict(zip(NAMES, (s, es, ns, mix, relax, vm, obs)))
     levels = s.shape[0]
     per_plane = 128 // GROUP
@@ -184,6 +202,19 @@
     group = iota(shape, 1) // GROUP
 
     place = iota(shape, 1) % GROUP
+    counts = edge_rows(count[...].astype(F32))
+    rows[levels] = counts
+
+    def lines(t, carry):
+        for j, (k, link) in enumerate(level_pair(levels, t)):
+            rows[2 * t + j], _, _ = pack_rows(
+                lambda name: level_of(refs[name], name, link if name == "vm" else k),
+                counts,
+                k.astype(F32),
+            )
+        return carry
+
+    lax.fori_loop(0, levels // 2, lines, 0, unroll=UNROLL)
 
     def columns(p, carry):
         packed = []
@@ -424,7 +455,7 @@
     merge_halos(odd, from_one, from_two, corners, planes.shape[0] // 2 * planes.shape[1])
 
     def rim(index):
-        return merge_rows(rows_n[index], rows_s[index])
+        return merge_lines(rows_n[index], rows_s[index])
 
     count_plane = len(NAMES[:6]) * plane_count
     side_counts = jnp.dot(
@@ -437,7 +468,7 @@
     count_ext = extend(
         count[...].astype(F32),
         side_counts[:ny],
-        rim(levels + half),
+        rim(levels),
         side_counts[ny : ny + 8],
     )
     east_ext = jnp.minimum(count_ext, east(count_ext))
@@ -448,7 +479,6 @@
         [count_ext[:ny, nx:], count_ext[ny:, nx:], count_ext[ny:, :nx]], axis=0
     )
     small_sub = sublane((8, nx))
-    east_rows = east_ext[ny:, :nx]
     north_rows = jnp.where(small_sub == 7, counts_out[2, ny:, :nx], 0.0)
     lane = iota((ny, nx), 1)
     per_half = per_plane // 2
@@ -563,15 +593,12 @@
     for u in range(STEPS):
         unpack(u)
 
-    def prepare(m, u, j, k, link_level, second):
+    def prepare(m, u, j, k, link_level):
         t = m * STEPS + u
-        x = unpack_rows(rim(2 * t + j), roll(second, 4, 0) if j else second)
+        x = unpack_line(rim(2 * t + j))
         level = k.astype(F32)
         row = x["s"]
-        open_east = level < east_rows
         open_north = level < north_rows
-        ep_r = jnp.where(open_east, 0.5 * x["es"] + x["mix"], 0.0)
-        em_r = jnp.where(open_east, 0.5 * x["es"] - x["mix"], 0.0)
         np_r = jnp.where(open_north, 0.5 * x["ns"] + x["mix"], 0.0)
         nm_r = jnp.where(open_north, 0.5 * x["ns"] - x["mix"], 0.0)
         link_r = jnp.where(link_level.astype(F32) + 1.0 < count_halo[ny + 8 :], x["vm"], 0.0)
@@ -584,15 +611,12 @@
 
         own = s[k]
         last, first = lane == nx - 1, lane == 0
-        fe = ep_r * row + em_r * shift_up(row, 1)
-        flow = jnp.where(last[:8], seam_rows, fe) - jnp.where(
-            first[:8], seam_rows, shift_down(fe, 1)
-        )
+        through = jnp.where(first[:8], seam_rows, jnp.where(last[:8], -seam_rows, 0.0))
         fn = np_r * row + nm_r * shift_up(own[:8], 0)
         top = np_[k, ny - 8 :] * own[ny - 8 :]
         cross = nm[k, ny - 8 :] * shift_up(row, 0)
         from_block = jnp.where(small_sub == 0, shift_down(top + cross, 0), 0.0)
-        right_r = x["base"] - flow - (fn - from_block)
+        right_r = x["base"] + through - (fn - from_block)
 
         inner = local[k] + jnp.where(first, seam, jnp.where(last, -seam, 0.0))
         low_rows = inner[:8] + jnp.where(small_sub == 0, shift_down(fn, 0), 0.0)
@@ -609,11 +633,10 @@
 
     def factor_step(m, u, carry):
         t = m * STEPS + u
-        second = rim(levels + t)
         new = []
         for j, (k, link_level) in enumerate(level_pair(levels, t)):
             ratio, c_own, c_halo, outer = carry[j]
-            own, halo, link = prepare(m, u, j, k, link_level, second)
+            own, halo, link = prepare(m, u, j, k, link_level)
             inv_h = 1.0 / (1.0 + outer + link - outer * ratio)
             q_h = outer * inv_h
             ratio = link * inv_h
@@ -894,17 +917,19 @@
     )
     half = levels // 2
     corner_planes = 2 * plane_count
-    *fields, rows, corners = call(
+    *fields, corners = call(
         rim_kernel,
         [jax.ShapeDtypeStruct(x.shape, x.dtype) for x in fields]
-        + [(levels + half + 1, 8, nx), (corner_planes, 8, nx)],
+        + [(corner_planes, 8, nx)],
         [pltpu.SemaphoreType.DMA((10,))],
         *[pltpu.with_memory_space_constraint(x, pltpu.HBM) for x in fields],
         space=HBM,
     )
     corners_n, corners_s = both_ways(corners)
+    planes, rows = call(
+        column_kernel, [(2 * pairs, ny, nx), (levels + 1, 8, nx)], [], *fields[:8]
+    )
     rows_n, rows_s = both_ways(rows)
-    (planes,) = call(column_kernel, [(2 * pairs, ny, nx)], [], *fields[:8])
     packed = (pairs * ny + corner_planes // 2 * 8, nx)
     one, two, own_corners = call(
         halves_kernel, [packed, packed, corners.shape], [],

time: 26.5 us -> 26.2 us (0.989)
  waiting for transfers between devices: 4.68 us -> 3.87 us
  Pallas kernels: 12.1 us -> 12.6 us
    ppermute x3, waiting for transfers between devices: 2.18 us -> 1.66 us  [both_ways(): from_north = lax.ppermute(x, 'ty', ring('ty', -1))]
    pallas_call x7, Pallas kernels: 12.1 us -> 12.6 us  [call(): pl.pallas_call(kernel, out_shape=[typed(x) for x in outs], in_specs=[spac...]
    ppermute x2, starting transfers between devices: 3.39 us -> 3.68 us  [swap(): lax.ppermute(x, 'tx', [(i, (i + 1) % nx if i % 2 == phase else (i - 1) %...]
    ppermute x2, waiting for transfers between devices: 2.5 us -> 2.2 us  [swap(): lax.ppermute(x, 'tx', [(i, (i + 1) % nx if i % 2 == phase else (i - 1) %...]
    ppermute x3, starting transfers between devices: 5.4 us -> 5.13 us  [both_ways(): from_north = lax.ppermute(x, 'ty', ring('ty', -1))]
  transfers between devices with their start and end apart: 5 -> 5, of which waited for: 3 -> 3; matrix products, arithmetic and copies ran while one was open for 0% -> 0% of each run, Pallas kernels for 12% -> 14%
where the time goes in v8:
time: 26.2 us; the launch traced here: 25.9 us
  Pallas kernels  12.6 us (48%)
  starting transfers between devices  8.81 us (34%)
  waiting for transfers between devices  3.87 us (15%)
  between operations  0.68 us (3%)
    pallas_call x7, Pallas kernels, call(): pl.pallas_call(kernel, out_shape=[typed(x) for x in outs], in_specs=[spac...  12.6 us
    ppermute x3, starting transfers between devices, both_ways(): from_north = lax.ppermute(x, 'ty', ring('ty', -1))  5.13 us
    ppermute x2, starting transfers between devices, swap(): lax.ppermute(x, 'tx', [(i, (i + 1) % nx if i % 2 == phase else (i - 1) %...  3.68 us
    ppermute x2, waiting for transfers between devices, swap(): lax.ppermute(x, 'tx', [(i, (i + 1) % nx if i % 2 == phase else (i - 1) %...  2.2 us
    ppermute x3, waiting for transfers between devices, both_ways(): from_north = lax.ppermute(x, 'ty', ring('ty', -1))  1.66 us
  transfers between devices with their start and end apart: 5, of which 3 were waited for; matrix products, arithmetic and copies ran while one was open for 0% of the time, Pallas kernels for 14%

profile of v8, /device:TPU:0, one launch (start us, length us, event | category | flops | bytes accessed | tf_op | source)
XLA Modules:
  0.0 25.9 jit_solution(10377372167083397195)
XLA Ops:
  0.6 2.0 %shard_map.113 = (f32[48,16,128]{2,1,0:T(8,128)S(1)}, bf16[48,16,128]{2,1,0:T(8,128)(2,1)S(1)}, bf16[48,16,128]{2,1,0:T(8,128)(2,1)S(1)}, bf16[48,16,128]{2,1,0:...) custom-call(f32[48,16,128]{2,1,0:T(8,128)} %args_0_.4, ...), custom_call_target="tpu_custom_call" | custom-call | tf_op jit(solution)/shard_map/pallas_call | solution.py:23
  2.6 3.0 %collective-permute-start = (f32[6,8,128]{2,1,0:T(8,128)S(1)}, f32[6,8,128]{2,1,0:T(8,128)S(1)}, u32[]{:S(2)}, u32[]{:S(2)}) collective-permute-start(f32[6,8,128]{2,1,0:T(8,128)S(1)} %get-tuple-element.58), channel_id=1, source_target_pairs={{0,16},{16,0},{1,17},{17,1},{2,18},{18,2},{3,19},{19,3},{4,20},{20... | collective-permute-start | bytes 73736 | tf_op jit(solution)/shard_map/ppermute | solution.py:885
  5.6 1.4 %shard_map.114 = (f32[20,16,128]{2,1,0:T(8,128)S(1)}, f32[49,8,128]{2,1,0:T(8,128)S(1)}) custom-call(f32[48,16,128]{2,1,0:T(8,128)S(1)} %get-tuple-element.47.s, bf16[48,16,128]{2,1,0:T(8,128)(2,1)S(1)} %get-tuple-element.48.es, bf16[48,16,128]{2,1,0:T(8,128)(2,1)S(1)} %get-tuple-element.49.ns, bf16[48,16,128]{2,1,0:T(8,128)(2,1)S(1)} %get-tuple-element.50.mix, ...), custom_call_target="tpu_custom_call" | custom-call | tf_op jit(solution)/shard_map/pallas_call | solution.py:23
  7.1 0.1 collective-permute-start.3
  7.2 0.3 %collective-permute-done.corners_n.corners_s = f32[6,8,128]{2,1,0:T(8,128)S(1)} collective-permute-done((f32[6,8,128]{2,1,0:T(8,128)S(1)}, f32[6,8,128]{2,1,0:T(8,128)S(1)}, u32[]{:S(2)}, u32[]{:S(2)}) %collective-permute-start) | collective-permute-done | bytes 24608 | tf_op jit(solution)/shard_map/ppermute | solution.py:885
  7.4 0.1 shard_map.115
  7.6 3.7 %collective-permute-start.2 = (f32[184,128]{1,0:T(8,128)S(1)}, f32[184,128]{1,0:T(8,128)S(1)}, u32[]{:S(2)}, u32[]{:S(2)}) collective-permute-start(f32[184,128]{1,0:T(8,128)S(1)} %get-tuple-element.67), channel_id=1, source_target_pairs={{0,15},{1,2},{2,1},{3,4},{4,3},{5,6},{6,5},{7,8},{8,7},{9,10},{10,... | collective-permute-start | bytes 282632 | tf_op jit(solution)/shard_map/ppermute | solution.py:893
  11.2 0.0 collective-permute-start.1
  11.3 0.9 %shard_map.116 = (f32[48,16,128]{2,1,0:T(8,128)S(1)}, f32[48,16,128]{2,1,0:T(8,128)S(1)}, f32[48,16,128]{2,1,0:T(8,128)S(1)}, f32[48,16,128]{2,1,0:T(8,128)S(1)}...) custom-call(f32[48,16,128]{2,1,0:T(8,128)S(1)} %get-tuple-element.47, ...), custom_call_target="tpu_custom_call" | custom-call | flops 1000000000 | tf_op jit(solution)/shard_map/pallas_call | solution.py:23
  12.1 2.2 %collective-permute-done.2.from_two = f32[184,128]{1,0:T(8,128)S(1)} collective-permute-done((f32[184,128]{1,0:T(8,128)S(1)}, f32[184,128]{1,0:T(8,128)S(1)}, u32[]{:S(2)}, u32[]{:S(2)}) %collective-permute-start.2) | collective-permute-done | bytes 94240 | tf_op jit(solution)/shard_map/ppermute | solution.py:893
  14.3 0.0 collective-permute-done.1.from_one
  14.3 0.0 collective-permute-done.3.rows_n.rows_s
  14.3 4.8 %shard_map.117 = (f32[48,32,128]{2,1,0:T(8,128)S(1)}, f32[48,32,128]{2,1,0:T(8,128)S(1)}, f32[48,32,128]{2,1,0:T(8,128)S(1)}, f32[48,32,128]{2,1,0:T(8,128)S(1)}...) custom-call(f32[48,16,128]{2,1,0:T(8,128)S(1)} %get-tuple-element.47, ...), custom_call_target="tpu_custom_call" | custom-call | tf_op jit(solution)/shard_map/pallas_call | solution.py:23
  19.1 2.0 %collective-permute-start.4 = (f32[25,8,128]{2,1,0:T(8,128)S(1)}, f32[25,8,128]{2,1,0:T(8,128)S(1)}, u32[]{:S(2)}, u32[]{:S(2)}) collective-permute-start(f32[25,8,128]{2,1,0:T(8,128)S(1)} %get-tuple-element.91), channel_id=1, source_target_pairs={{0,16},{16,0},{1,17},{17,1},{2,18},{18,2},{3,19},{19,3},{4,20},{20... | collective-permute-start | bytes 307208 | tf_op jit(solution)/shard_map/ppermute | solution.py:885
  21.1 1.3 %shard_map.118 = (f32[48,16,256]{2,1,0:T(8,128)S(1)}, f32[48,16,128]{2,1,0:T(8,128)S(1)}, f32[48,16,128]{2,1,0:T(8,128)S(1)}, f32[48,16,128]{2,1,0:T(8,128)S(1)}) custom-call(f32[48,16,128]{2,1,0:T(8,128)S(1)} %get-tuple-element.60.ep, f32[48,16,128]{2,1,0:T(8,128)S(1)} %get-tuple-element.61.em, f32[48,16,128]{2,1,0:T(8,128)S(1)} %get-tuple-element.62.np_, ...), custom_call_target="tpu_custom_call" | custom-call | bytes 8388608 | tf_op jit(solution)/shard_map/pallas_call | solution.py:23
  22.4 1.4 %collective-permute-done.4.rows_n.rows_s = f32[25,8,128]{2,1,0:T(8,128)S(1)} collective-permute-done((f32[25,8,128]{2,1,0:T(8,128)S(1)}, f32[25,8,128]{2,1,0:T(8,128)S(1)}, u32[]{:S(2)}, u32[]{:S(2)}) %collective-permute-start.4) | collective-permute-done | bytes 102432 | tf_op jit(solution)/shard_map/ppermute | solution.py:885
  23.8 2.2 %shard_map.119 = (f32[48,16,128]{2,1,0:T(8,128)}, f32[48,16,128]{2,1,0:T(8,128)}) custom-call(f32[48,16,128]{2,1,0:T(8,128)S(1)} %get-tuple-element.60.ep, f32[48,16,128]{2,1,0:T(8,128)S(1)} %get-tuple-element.61.em, f32[48,16,128]{2,1,0:T(8,128)S(1)} %get-tuple-element.62.np_, f32[48,16,128]{2,1,0:T(8,128)S(1)} %get-tuple-element.63.nm, ...), custom_call_target="tpu_custom_call" | custom-call | tf_op jit(solution)/shard_map/pallas_call | solution.py:23
Async XLA Ops:
  2.6 4.8 %collective-permute-start = (f32[6,8,128]{2,1,0:T(8,128)S(1)}, f32[6,8,128]{2,1,0:T(8,128)S(1)}, u32[]{:S(2)}, u32[]{:S(2)}) collective-permute-start(f32[6,8,128]{2,1,0:T(8,128)S(1)} %get-tuple-element.58), channel_id=1, source_target_pairs={{0,16},{16,0},{1,17},{17,1},{2,18},{18,2},{3,19},{19,3},{4,20},{20... | collective-permute-start | bytes 73736 | tf_op jit(solution)/shard_map/ppermute | solution.py:885
  7.1 7.3 %collective-permute-start.3 = (f32[49,8,128]{2,1,0:T(8,128)S(1)}, f32[49,8,128]{2,1,0:T(8,128)S(1)}, u32[]{:S(2)}, u32[]{:S(2)}) collective-permute-start(f32[49,8,128]{2,1,0:T(8,128)S(1)} %get-tuple-element.69), channel_id=1, source_target_pairs={{0,16},{16,0},{1,17},{17,1},{2,18},{18,2},{3,19},{19,3},{4,20},{20... | collective-permute-start | bytes 602120 | tf_op jit(solution)/shard_map/ppermute | solution.py:885
  7.6 6.8 %collective-permute-start.2 = (f32[184,128]{1,0:T(8,128)S(1)}, f32[184,128]{1,0:T(8,128)S(1)}, u32[]{:S(2)}, u32[]{:S(2)}) collective-permute-start(f32[184,128]{1,0:T(8,128)S(1)} %get-tuple-element.67), channel_id=1, source_target_pairs={{0,15},{1,2},{2,1},{3,4},{4,3},{5,6},{6,5},{7,8},{8,7},{9,10},{10,... | collective-permute-start | bytes 282632 | tf_op jit(solution)/shard_map/ppermute | solution.py:893
  11.2 3.1 %collective-permute-start.1 = (f32[184,128]{1,0:T(8,128)S(1)}, f32[184,128]{1,0:T(8,128)S(1)}, u32[]{:S(2)}, u32[]{:S(2)}) collective-permute-start(f32[184,128]{1,0:T(8,128)S(1)} %get-tuple-element.59.after), channel_id=1, source_target_pairs={{0,1},{1,0},{2,3},{3,2},{4,5},{5,4},{6,7},{7,6},{8,9},{9,8},{10,11... | collective-permute-start | bytes 282632 | tf_op jit(solution)/shard_map/ppermute | solution.py:893
  19.1 4.7 %collective-permute-start.4 = (f32[25,8,128]{2,1,0:T(8,128)S(1)}, f32[25,8,128]{2,1,0:T(8,128)S(1)}, u32[]{:S(2)}, u32[]{:S(2)}) collective-permute-start(f32[25,8,128]{2,1,0:T(8,128)S(1)} %get-tuple-element.91), channel_id=1, source_target_pairs={{0,16},{16,0},{1,17},{17,1},{2,18},{18,2},{3,19},{19,3},{4,20},{20... | collective-permute-start | bytes 307208 | tf_op jit(solution)/shard_map/ppermute | solution.py:885

commit v9 on v8

--- a/solution.py
+++ b/solution.py
@@ -538,6 +538,7 @@
         western, through_west, _ = strips(True)
         eastern, _, through_east = strips(False)
         seam = jnp.where(place == 3, through_west, through_east)
+        seam = jnp.where(place == 5, roll(eastern[7], 1, 1), seam)
         both = [jnp.where(low[: a.shape[0]], a, b) for a, b in zip(western, eastern)]
         right, link, np_c, nm_c = (x[ny:] for x in both[:4])
         corner = pair_rows(right, link)
@@ -551,7 +552,7 @@
         seen = jnp.where(side_place < 3, roll(further, 2, 1), roll(near_seam, 3, 1))
         beyond = jnp.where(side_place > 4, roll(further, -2, 1), roll(near_seam, -3, 1))
         seen = jnp.where(side_place < 4, seen, beyond)
-        both = both[:2] + [seam[:ny], seen] + both[2:] + [jnp.concatenate([corner] * 2, axis=0)]
+        both = both[:2] + [seen, seam[:ny]] + both[2:7] + [jnp.concatenate([corner] * 2, axis=0)]
         for i, x in enumerate(both):
             split(p, i * ny, x)
         return carry
@@ -572,11 +573,11 @@
             t = m * STEPS + u
             for j, k in enumerate((t, levels - 1 - t)):
                 x = out[:, j * nx : (j + 1) * nx]
-                np_x, nm_x, ep_x, em_x, sink_x, s_x, corner = (
-                    x[i * ny : (i + 1) * ny] for i in range(4, 11)
+                seam_x, np_x, nm_x, ep_x, em_x, sink_x, corner = (
+                    x[i * ny : (i + 1) * ny] for i in range(3, 10)
                 )
                 corner = corner[:8]
-                moved[k] = x[: 4 * ny]
+                moved[k] = x[: 3 * ny]
                 moved_rows[k] = corner
                 ep_halo[k, :ny] = ep_x
                 em_halo[k, :ny] = em_x
@@ -585,7 +586,7 @@
                 np_halo[k, ny : ny + 8] = roll(corner, 2, 0)
                 nm_halo[k, ny : ny + 8] = roll(corner, 1, 0)
                 sink_halo[k] = sink_x
-                s_halo[k, :ny] = s_x
+                s_halo[k, :ny] = seam_x
             return carry
 
         lax.fori_loop(0, 2 * plane_count, place_both, 0, unroll=2 * plane_count)
@@ -603,7 +604,8 @@
         nm_r = jnp.where(open_north, 0.5 * x["ns"] - x["mix"], 0.0)
         link_r = jnp.where(link_level.astype(F32) + 1.0 < count_halo[ny + 8 :], x["vm"], 0.0)
         corner = moved_rows[k]
-        right, link, seam = (moved[k, i * ny : (i + 1) * ny] for i in range(3))
+        right, link = moved[k, :ny], moved[k, ny : 2 * ny]
+        seam = s_halo[k, :ny]
         seam_rows = roll(corner, 4, 0)
         np_halo[k, ny + 8 :] = np_r
         nm_halo[k, ny + 8 :] = nm_r
@@ -694,7 +696,7 @@
     ends = solve_inward(levels, lambda k: rhs[k], inv_q, main)
 
     def to_adjoint(k, x, m, u, j):
-        seen = extend(obs[k].astype(F32), moved[k, 3 * ny :])
+        seen = extend(obs[k].astype(F32), moved[k, 2 * ny :])
         rhs[k] = jnp.where(k.astype(F32) < count_ext[:ny], x - seen, 0.0)
 
     solve_outward(levels, ends, ratio, join[:ny], main, both(to_adjoint))
@@ -741,6 +743,7 @@
     nx = width // 2
     sub = sublane((ny, width))
     inside = sub < ny - 1
+    lane = iota((ny, nx), 1)
 
     def inner(k, carry):
         x = solved[k]
@@ -755,14 +758,16 @@
         open_east = level < counts[1, :ny, :nx]
         open_north = level < counts[2, :ny, :nx]
 
-        def slopes(state):
-            run = (east(state[:ny]) - state[:ny])[:, :nx]
-            rise = shift_up(state[:, :nx], 0)[:ny] - state[:ny, :nx]
+        def slopes(main, next_column, rows):
+            run = jnp.where(lane == nx - 1, next_column, roll(main, -1, 1)) - main
+            rise = shift_up(jnp.concatenate([main, rows], axis=0), 0)[:ny] - main
             return jnp.where(open_east, run, 0.0), jnp.where(open_north, rise, 0.0)
 
-        run, rise = slopes(state)
+        run, rise = slopes(state[:ny, :nx], state[:ny, nx:], state[ny:, :nx])
         late_out[k] = ge[:, :nx] * run + gn[:, :nx] * rise
-        run_out[k], rise_out[k] = slopes(whole(s[k], s_halo[k]))
+        run_out[k], rise_out[k] = slopes(
+            s[k], roll(s_halo[k, :ny], 1, 1), s_halo[k, ny + 8 :]
+        )
         return carry
 
     lax.fori_loop(0, levels, inner, 0, unroll=UNROLL)
@@ -960,8 +965,8 @@
             corners.shape,
             block,
             ext,
-            pltpu.VMEM((2 * plane_count, 11 * ny, 2 * nx), jnp.bfloat16),
-            (levels, 4 * ny, nx),
+            pltpu.VMEM((2 * plane_count, 10 * ny, 2 * nx), jnp.bfloat16),
+            (levels, 3 * ny, nx),
             (levels, 8, nx),
             (2 * plane_count, 8, nx),
         ],

time: 26.2 us -> 25.9 us (0.989)
  transfers between devices with their start and end apart: 5 -> 5, of which waited for: 3 -> 3; matrix products, arithmetic and copies ran while one was open for 0% -> 0% of each run, Pallas kernels for 14% -> 15%
where the time goes in v9:
time: 25.9 us; the launch traced here: 25.7 us
  Pallas kernels  12.5 us (48%)
  starting transfers between devices  8.82 us (34%)
  waiting for transfers between devices  3.74 us (14%)
  between operations  0.68 us (3%)
    pallas_call x7, Pallas kernels, call(): pl.pallas_call(kernel, out_shape=[typed(x) for x in outs], in_specs=[spac...  12.5 us
    ppermute x3, starting transfers between devices, both_ways(): from_north = lax.ppermute(x, 'ty', ring('ty', -1))  5.14 us
    ppermute x2, starting transfers between devices, swap(): lax.ppermute(x, 'tx', [(i, (i + 1) % nx if i % 2 == phase else (i - 1) %...  3.68 us
    ppermute x2, waiting for transfers between devices, swap(): lax.ppermute(x, 'tx', [(i, (i + 1) % nx if i % 2 == phase else (i - 1) %...  2.2 us
    ppermute x3, waiting for transfers between devices, both_ways(): from_north = lax.ppermute(x, 'ty', ring('ty', -1))  1.54 us
  transfers between devices with their start and end apart: 5, of which 3 were waited for; matrix products, arithmetic and copies ran while one was open for 0% of the time, Pallas kernels for 15%

profile of v9, /device:TPU:0, one launch (start us, length us, event | category | flops | bytes accessed | tf_op | source)
XLA Modules:
  0.0 25.7 jit_solution(12175438247514438759)
XLA Ops:
  0.6 2.0 %shard_map.113 = (f32[48,16,128]{2,1,0:T(8,128)S(1)}, bf16[48,16,128]{2,1,0:T(8,128)(2,1)S(1)}, bf16[48,16,128]{2,1,0:T(8,128)(2,1)S(1)}, bf16[48,16,128]{2,1,0:...) custom-call(f32[48,16,128]{2,1,0:T(8,128)} %args_0_.4, ...), custom_call_target="tpu_custom_call" | custom-call | tf_op jit(solution)/shard_map/pallas_call | solution.py:23
  2.6 3.0 %collective-permute-start = (f32[6,8,128]{2,1,0:T(8,128)S(1)}, f32[6,8,128]{2,1,0:T(8,128)S(1)}, u32[]{:S(2)}, u32[]{:S(2)}) collective-permute-start(f32[6,8,128]{2,1,0:T(8,128)S(1)} %get-tuple-element.58), channel_id=1, source_target_pairs={{0,16},{16,0},{1,17},{17,1},{2,18},{18,2},{3,19},{19,3},{4,20},{20... | collective-permute-start | bytes 73736 | tf_op jit(solution)/shard_map/ppermute | solution.py:890
  5.6 1.4 %shard_map.114 = (f32[20,16,128]{2,1,0:T(8,128)S(1)}, f32[49,8,128]{2,1,0:T(8,128)S(1)}) custom-call(f32[48,16,128]{2,1,0:T(8,128)S(1)} %get-tuple-element.47.s, bf16[48,16,128]{2,1,0:T(8,128)(2,1)S(1)} %get-tuple-element.48.es, bf16[48,16,128]{2,1,0:T(8,128)(2,1)S(1)} %get-tuple-element.49.ns, bf16[48,16,128]{2,1,0:T(8,128)(2,1)S(1)} %get-tuple-element.50.mix, ...), custom_call_target="tpu_custom_call" | custom-call | tf_op jit(solution)/shard_map/pallas_call | solution.py:23
  7.1 0.1 collective-permute-start.3
  7.2 0.3 %collective-permute-done.corners_n.corners_s = f32[6,8,128]{2,1,0:T(8,128)S(1)} collective-permute-done((f32[6,8,128]{2,1,0:T(8,128)S(1)}, f32[6,8,128]{2,1,0:T(8,128)S(1)}, u32[]{:S(2)}, u32[]{:S(2)}) %collective-permute-start) | collective-permute-done | bytes 24608 | tf_op jit(solution)/shard_map/ppermute | solution.py:890
  7.4 0.1 shard_map.115
  7.6 3.7 %collective-permute-start.2 = (f32[184,128]{1,0:T(8,128)S(1)}, f32[184,128]{1,0:T(8,128)S(1)}, u32[]{:S(2)}, u32[]{:S(2)}) collective-permute-start(f32[184,128]{1,0:T(8,128)S(1)} %get-tuple-element.67), channel_id=1, source_target_pairs={{0,15},{1,2},{2,1},{3,4},{4,3},{5,6},{6,5},{7,8},{8,7},{9,10},{10,... | collective-permute-start | bytes 282632 | tf_op jit(solution)/shard_map/ppermute | solution.py:898
  11.2 0.0 collective-permute-start.1
  11.3 0.9 %shard_map.116 = (f32[48,16,128]{2,1,0:T(8,128)S(1)}, f32[48,16,128]{2,1,0:T(8,128)S(1)}, f32[48,16,128]{2,1,0:T(8,128)S(1)}, f32[48,16,128]{2,1,0:T(8,128)S(1)}...) custom-call(f32[48,16,128]{2,1,0:T(8,128)S(1)} %get-tuple-element.47, ...), custom_call_target="tpu_custom_call" | custom-call | flops 1000000000 | tf_op jit(solution)/shard_map/pallas_call | solution.py:23
  12.1 2.2 %collective-permute-done.2.from_two = f32[184,128]{1,0:T(8,128)S(1)} collective-permute-done((f32[184,128]{1,0:T(8,128)S(1)}, f32[184,128]{1,0:T(8,128)S(1)}, u32[]{:S(2)}, u32[]{:S(2)}) %collective-permute-start.2) | collective-permute-done | bytes 94240 | tf_op jit(solution)/shard_map/ppermute | solution.py:898
  14.3 0.0 collective-permute-done.1.from_one
  14.3 0.0 collective-permute-done.3.rows_n.rows_s
  14.3 4.5 %shard_map.117 = (f32[48,32,128]{2,1,0:T(8,128)S(1)}, f32[48,32,128]{2,1,0:T(8,128)S(1)}, f32[48,32,128]{2,1,0:T(8,128)S(1)}, f32[48,32,128]{2,1,0:T(8,128)S(1)}...) custom-call(f32[48,16,128]{2,1,0:T(8,128)S(1)} %get-tuple-element.47, ...), custom_call_target="tpu_custom_call" | custom-call | tf_op jit(solution)/shard_map/pallas_call | solution.py:23
  18.9 2.0 %collective-permute-start.4 = (f32[25,8,128]{2,1,0:T(8,128)S(1)}, f32[25,8,128]{2,1,0:T(8,128)S(1)}, u32[]{:S(2)}, u32[]{:S(2)}) collective-permute-start(f32[25,8,128]{2,1,0:T(8,128)S(1)} %get-tuple-element.91), channel_id=1, source_target_pairs={{0,16},{16,0},{1,17},{17,1},{2,18},{18,2},{3,19},{19,3},{4,20},{20... | collective-permute-start | bytes 307208 | tf_op jit(solution)/shard_map/ppermute | solution.py:890
  20.9 1.4 %shard_map.118 = (f32[48,16,256]{2,1,0:T(8,128)S(1)}, f32[48,16,128]{2,1,0:T(8,128)S(1)}, f32[48,16,128]{2,1,0:T(8,128)S(1)}, f32[48,16,128]{2,1,0:T(8,128)S(1)}) custom-call(f32[48,16,128]{2,1,0:T(8,128)S(1)} %get-tuple-element.60.ep, f32[48,16,128]{2,1,0:T(8,128)S(1)} %get-tuple-element.61.em, f32[48,16,128]{2,1,0:T(8,128)S(1)} %get-tuple-element.62.np_, ...), custom_call_target="tpu_custom_call" | custom-call | bytes 8388608 | tf_op jit(solution)/shard_map/pallas_call | solution.py:23
  22.3 1.2 %collective-permute-done.4.rows_n.rows_s = f32[25,8,128]{2,1,0:T(8,128)S(1)} collective-permute-done((f32[25,8,128]{2,1,0:T(8,128)S(1)}, f32[25,8,128]{2,1,0:T(8,128)S(1)}, u32[]{:S(2)}, u32[]{:S(2)}) %collective-permute-start.4) | collective-permute-done | bytes 102432 | tf_op jit(solution)/shard_map/ppermute | solution.py:890
  23.5 2.2 %shard_map.119 = (f32[48,16,128]{2,1,0:T(8,128)}, f32[48,16,128]{2,1,0:T(8,128)}) custom-call(f32[48,16,128]{2,1,0:T(8,128)S(1)} %get-tuple-element.60.ep, f32[48,16,128]{2,1,0:T(8,128)S(1)} %get-tuple-element.61.em, f32[48,16,128]{2,1,0:T(8,128)S(1)} %get-tuple-element.62.np_, f32[48,16,128]{2,1,0:T(8,128)S(1)} %get-tuple-element.63.nm, ...), custom_call_target="tpu_custom_call" | custom-call | tf_op jit(solution)/shard_map/pallas_call | solution.py:23
Async XLA Ops:
  2.6 4.8 %collective-permute-start = (f32[6,8,128]{2,1,0:T(8,128)S(1)}, f32[6,8,128]{2,1,0:T(8,128)S(1)}, u32[]{:S(2)}, u32[]{:S(2)}) collective-permute-start(f32[6,8,128]{2,1,0:T(8,128)S(1)} %get-tuple-element.58), channel_id=1, source_target_pairs={{0,16},{16,0},{1,17},{17,1},{2,18},{18,2},{3,19},{19,3},{4,20},{20... | collective-permute-start | bytes 73736 | tf_op jit(solution)/shard_map/ppermute | solution.py:890
  7.1 7.3 %collective-permute-start.3 = (f32[49,8,128]{2,1,0:T(8,128)S(1)}, f32[49,8,128]{2,1,0:T(8,128)S(1)}, u32[]{:S(2)}, u32[]{:S(2)}) collective-permute-start(f32[49,8,128]{2,1,0:T(8,128)S(1)} %get-tuple-element.69), channel_id=1, source_target_pairs={{0,16},{16,0},{1,17},{17,1},{2,18},{18,2},{3,19},{19,3},{4,20},{20... | collective-permute-start | bytes 602120 | tf_op jit(solution)/shard_map/ppermute | solution.py:890
  7.6 6.8 %collective-permute-start.2 = (f32[184,128]{1,0:T(8,128)S(1)}, f32[184,128]{1,0:T(8,128)S(1)}, u32[]{:S(2)}, u32[]{:S(2)}) collective-permute-start(f32[184,128]{1,0:T(8,128)S(1)} %get-tuple-element.67), channel_id=1, source_target_pairs={{0,15},{1,2},{2,1},{3,4},{4,3},{5,6},{6,5},{7,8},{8,7},{9,10},{10,... | collective-permute-start | bytes 282632 | tf_op jit(solution)/shard_map/ppermute | solution.py:898
  11.2 3.1 %collective-permute-start.1 = (f32[184,128]{1,0:T(8,128)S(1)}, f32[184,128]{1,0:T(8,128)S(1)}, u32[]{:S(2)}, u32[]{:S(2)}) collective-permute-start(f32[184,128]{1,0:T(8,128)S(1)} %get-tuple-element.59.after), channel_id=1, source_target_pairs={{0,1},{1,0},{2,3},{3,2},{4,5},{5,4},{6,7},{7,6},{8,9},{9,8},{10,11... | collective-permute-start | bytes 282632 | tf_op jit(solution)/shard_map/ppermute | solution.py:898
  18.9 4.7 %collective-permute-start.4 = (f32[25,8,128]{2,1,0:T(8,128)S(1)}, f32[25,8,128]{2,1,0:T(8,128)S(1)}, u32[]{:S(2)}, u32[]{:S(2)}) collective-permute-start(f32[25,8,128]{2,1,0:T(8,128)S(1)} %get-tuple-element.91), channel_id=1, source_target_pairs={{0,16},{16,0},{1,17},{17,1},{2,18},{18,2},{3,19},{19,3},{4,20},{20... | collective-permute-start | bytes 307208 | tf_op jit(solution)/shard_map/ppermute | solution.py:890

commit v10 on v9

--- a/solution.py
+++ b/solution.py
@@ -329,7 +329,7 @@
     return lax.fori_loop(0, half, step, (zero, zero), unroll=UNROLL)
 
 
-def solve_outward(levels, ends, ratio, join, carries, use):
+def solve_outward(levels, ends, ratio, join, carries, use, unroll=2):
     half = levels // 2
     high, low = ends
     upper = (high + ratio(half - 1) * low) * join
@@ -346,7 +346,7 @@
             last = tuple(new)
         return last
 
-    lax.fori_loop(0, half // STEPS, block, (lower, upper), unroll=2)
+    lax.fori_loop(0, half // STEPS, block, (lower, upper), unroll=unroll)
 
 
 def merge_halos(odd, from_one, from_two, planes, start):
@@ -727,7 +727,7 @@
         moved = roll(pair[:, nx:], 2 * u + 1, 1)
         sides[m] = jnp.where(lane8 // 2 == u, moved, before)
 
-    solve_outward(levels, ends, ratio, join[:ny], main, to_send)
+    solve_outward(levels, ends, ratio, join[:ny], main, to_send, 3)
     both_sides = sides[0]
     for m in range(1, half // STEPS):
         place = m * 2 * STEPS

time: 25.9 us -> 25.8 us (level)
  no operation moved by 1% of the time
where the time goes in v10:
time: 25.8 us; the launch traced here: 25.6 us
  Pallas kernels  12.4 us (48%)
  starting transfers between devices  8.82 us (34%)
  waiting for transfers between devices  3.74 us (14%)
  between operations  0.68 us (3%)
    pallas_call x7, Pallas kernels, call(): pl.pallas_call(kernel, out_shape=[typed(x) for x in outs], in_specs=[spac...  12.4 us
    ppermute x3, starting transfers between devices, both_ways(): from_north = lax.ppermute(x, 'ty', ring('ty', -1))  5.14 us
    ppermute x2, starting transfers between devices, swap(): lax.ppermute(x, 'tx', [(i, (i + 1) % nx if i % 2 == phase else (i - 1) %...  3.68 us
    ppermute x2, waiting for transfers between devices, swap(): lax.ppermute(x, 'tx', [(i, (i + 1) % nx if i % 2 == phase else (i - 1) %...  2.2 us
    ppermute x3, waiting for transfers between devices, both_ways(): from_north = lax.ppermute(x, 'ty', ring('ty', -1))  1.54 us
  transfers between devices with their start and end apart: 5, of which 3 were waited for; matrix products, arithmetic and copies ran while one was open for 0% of the time, Pallas kernels for 15%

profile of v10, /device:TPU:0, one launch (start us, length us, event | category | flops | bytes accessed | tf_op | source)
XLA Modules:
  0.0 25.6 jit_solution(17548974138019167570)
XLA Ops:
  0.6 2.0 %shard_map.113 = (f32[48,16,128]{2,1,0:T(8,128)S(1)}, bf16[48,16,128]{2,1,0:T(8,128)(2,1)S(1)}, bf16[48,16,128]{2,1,0:T(8,128)(2,1)S(1)}, bf16[48,16,128]{2,1,0:...) custom-call(f32[48,16,128]{2,1,0:T(8,128)} %args_0_.4, ...), custom_call_target="tpu_custom_call" | custom-call | tf_op jit(solution)/shard_map/pallas_call | solution.py:23
  2.6 3.0 %collective-permute-start = (f32[6,8,128]{2,1,0:T(8,128)S(1)}, f32[6,8,128]{2,1,0:T(8,128)S(1)}, u32[]{:S(2)}, u32[]{:S(2)}) collective-permute-start(f32[6,8,128]{2,1,0:T(8,128)S(1)} %get-tuple-element.58), channel_id=1, source_target_pairs={{0,16},{16,0},{1,17},{17,1},{2,18},{18,2},{3,19},{19,3},{4,20},{20... | collective-permute-start | bytes 73736 | tf_op jit(solution)/shard_map/ppermute | solution.py:890
  5.6 1.4 %shard_map.114 = (f32[20,16,128]{2,1,0:T(8,128)S(1)}, f32[49,8,128]{2,1,0:T(8,128)S(1)}) custom-call(f32[48,16,128]{2,1,0:T(8,128)S(1)} %get-tuple-element.47.s, bf16[48,16,128]{2,1,0:T(8,128)(2,1)S(1)} %get-tuple-element.48.es, bf16[48,16,128]{2,1,0:T(8,128)(2,1)S(1)} %get-tuple-element.49.ns, bf16[48,16,128]{2,1,0:T(8,128)(2,1)S(1)} %get-tuple-element.50.mix, ...), custom_call_target="tpu_custom_call" | custom-call | tf_op jit(solution)/shard_map/pallas_call | solution.py:23
  7.1 0.1 collective-permute-start.3
  7.2 0.3 %collective-permute-done.corners_n.corners_s = f32[6,8,128]{2,1,0:T(8,128)S(1)} collective-permute-done((f32[6,8,128]{2,1,0:T(8,128)S(1)}, f32[6,8,128]{2,1,0:T(8,128)S(1)}, u32[]{:S(2)}, u32[]{:S(2)}) %collective-permute-start) | collective-permute-done | bytes 24608 | tf_op jit(solution)/shard_map/ppermute | solution.py:890
  7.4 0.1 shard_map.115
  7.6 3.7 %collective-permute-start.2 = (f32[184,128]{1,0:T(8,128)S(1)}, f32[184,128]{1,0:T(8,128)S(1)}, u32[]{:S(2)}, u32[]{:S(2)}) collective-permute-start(f32[184,128]{1,0:T(8,128)S(1)} %get-tuple-element.67), channel_id=1, source_target_pairs={{0,15},{1,2},{2,1},{3,4},{4,3},{5,6},{6,5},{7,8},{8,7},{9,10},{10,... | collective-permute-start | bytes 282632 | tf_op jit(solution)/shard_map/ppermute | solution.py:898
  11.2 0.0 collective-permute-start.1
  11.3 0.9 %shard_map.116 = (f32[48,16,128]{2,1,0:T(8,128)S(1)}, f32[48,16,128]{2,1,0:T(8,128)S(1)}, f32[48,16,128]{2,1,0:T(8,128)S(1)}, f32[48,16,128]{2,1,0:T(8,128)S(1)}...) custom-call(f32[48,16,128]{2,1,0:T(8,128)S(1)} %get-tuple-element.47, ...), custom_call_target="tpu_custom_call" | custom-call | flops 1000000000 | tf_op jit(solution)/shard_map/pallas_call | solution.py:23
  12.1 2.2 %collective-permute-done.2.from_two = f32[184,128]{1,0:T(8,128)S(1)} collective-permute-done((f32[184,128]{1,0:T(8,128)S(1)}, f32[184,128]{1,0:T(8,128)S(1)}, u32[]{:S(2)}, u32[]{:S(2)}) %collective-permute-start.2) | collective-permute-done | bytes 94240 | tf_op jit(solution)/shard_map/ppermute | solution.py:898
  14.3 0.0 collective-permute-done.1.from_one
  14.3 0.0 collective-permute-done.3.rows_n.rows_s
  14.3 4.4 %shard_map.117 = (f32[48,32,128]{2,1,0:T(8,128)S(1)}, f32[48,32,128]{2,1,0:T(8,128)S(1)}, f32[48,32,128]{2,1,0:T(8,128)S(1)}, f32[48,32,128]{2,1,0:T(8,128)S(1)}...) custom-call(f32[48,16,128]{2,1,0:T(8,128)S(1)} %get-tuple-element.47, ...), custom_call_target="tpu_custom_call" | custom-call | tf_op jit(solution)/shard_map/pallas_call | solution.py:23
  18.8 2.0 %collective-permute-start.4 = (f32[25,8,128]{2,1,0:T(8,128)S(1)}, f32[25,8,128]{2,1,0:T(8,128)S(1)}, u32[]{:S(2)}, u32[]{:S(2)}) collective-permute-start(f32[25,8,128]{2,1,0:T(8,128)S(1)} %get-tuple-element.91), channel_id=1, source_target_pairs={{0,16},{16,0},{1,17},{17,1},{2,18},{18,2},{3,19},{19,3},{4,20},{20... | collective-permute-start | bytes 307208 | tf_op jit(solution)/shard_map/ppermute | solution.py:890
  20.8 1.4 %shard_map.118 = (f32[48,16,256]{2,1,0:T(8,128)S(1)}, f32[48,16,128]{2,1,0:T(8,128)S(1)}, f32[48,16,128]{2,1,0:T(8,128)S(1)}, f32[48,16,128]{2,1,0:T(8,128)S(1)}) custom-call(f32[48,16,128]{2,1,0:T(8,128)S(1)} %get-tuple-element.60.ep, f32[48,16,128]{2,1,0:T(8,128)S(1)} %get-tuple-element.61.em, f32[48,16,128]{2,1,0:T(8,128)S(1)} %get-tuple-element.62.np_, ...), custom_call_target="tpu_custom_call" | custom-call | bytes 8388608 | tf_op jit(solution)/shard_map/pallas_call | solution.py:23
  22.2 1.2 %collective-permute-done.4.rows_n.rows_s = f32[25,8,128]{2,1,0:T(8,128)S(1)} collective-permute-done((f32[25,8,128]{2,1,0:T(8,128)S(1)}, f32[25,8,128]{2,1,0:T(8,128)S(1)}, u32[]{:S(2)}, u32[]{:S(2)}) %collective-permute-start.4) | collective-permute-done | bytes 102432 | tf_op jit(solution)/shard_map/ppermute | solution.py:890
  23.4 2.2 %shard_map.119 = (f32[48,16,128]{2,1,0:T(8,128)}, f32[48,16,128]{2,1,0:T(8,128)}) custom-call(f32[48,16,128]{2,1,0:T(8,128)S(1)} %get-tuple-element.60.ep, f32[48,16,128]{2,1,0:T(8,128)S(1)} %get-tuple-element.61.em, f32[48,16,128]{2,1,0:T(8,128)S(1)} %get-tuple-element.62.np_, f32[48,16,128]{2,1,0:T(8,128)S(1)} %get-tuple-element.63.nm, ...), custom_call_target="tpu_custom_call" | custom-call | tf_op jit(solution)/shard_map/pallas_call | solution.py:23
Async XLA Ops:
  2.6 4.8 %collective-permute-start = (f32[6,8,128]{2,1,0:T(8,128)S(1)}, f32[6,8,128]{2,1,0:T(8,128)S(1)}, u32[]{:S(2)}, u32[]{:S(2)}) collective-permute-start(f32[6,8,128]{2,1,0:T(8,128)S(1)} %get-tuple-element.58), channel_id=1, source_target_pairs={{0,16},{16,0},{1,17},{17,1},{2,18},{18,2},{3,19},{19,3},{4,20},{20... | collective-permute-start | bytes 73736 | tf_op jit(solution)/shard_map/ppermute | solution.py:890
  7.1 7.3 %collective-permute-start.3 = (f32[49,8,128]{2,1,0:T(8,128)S(1)}, f32[49,8,128]{2,1,0:T(8,128)S(1)}, u32[]{:S(2)}, u32[]{:S(2)}) collective-permute-start(f32[49,8,128]{2,1,0:T(8,128)S(1)} %get-tuple-element.69), channel_id=1, source_target_pairs={{0,16},{16,0},{1,17},{17,1},{2,18},{18,2},{3,19},{19,3},{4,20},{20... | collective-permute-start | bytes 602120 | tf_op jit(solution)/shard_map/ppermute | solution.py:890
  7.6 6.8 %collective-permute-start.2 = (f32[184,128]{1,0:T(8,128)S(1)}, f32[184,128]{1,0:T(8,128)S(1)}, u32[]{:S(2)}, u32[]{:S(2)}) collective-permute-start(f32[184,128]{1,0:T(8,128)S(1)} %get-tuple-element.67), channel_id=1, source_target_pairs={{0,15},{1,2},{2,1},{3,4},{4,3},{5,6},{6,5},{7,8},{8,7},{9,10},{10,... | collective-permute-start | bytes 282632 | tf_op jit(solution)/shard_map/ppermute | solution.py:898
  11.2 3.1 %collective-permute-start.1 = (f32[184,128]{1,0:T(8,128)S(1)}, f32[184,128]{1,0:T(8,128)S(1)}, u32[]{:S(2)}, u32[]{:S(2)}) collective-permute-start(f32[184,128]{1,0:T(8,128)S(1)} %get-tuple-element.59.after), channel_id=1, source_target_pairs={{0,1},{1,0},{2,3},{3,2},{4,5},{5,4},{6,7},{7,6},{8,9},{9,8},{10,11... | collective-permute-start | bytes 282632 | tf_op jit(solution)/shard_map/ppermute | solution.py:898
  18.8 4.7 %collective-permute-start.4 = (f32[25,8,128]{2,1,0:T(8,128)S(1)}, f32[25,8,128]{2,1,0:T(8,128)S(1)}, u32[]{:S(2)}, u32[]{:S(2)}) collective-permute-start(f32[25,8,128]{2,1,0:T(8,128)S(1)} %get-tuple-element.91), channel_id=1, source_target_pairs={{0,16},{16,0},{1,17},{17,1},{2,18},{18,2},{3,19},{19,3},{4,20},{20... | collective-permute-start | bytes 307208 | tf_op jit(solution)/shard_map/ppermute | solution.py:890

commit v11 on v10

--- a/solution.py
+++ b/solution.py
@@ -829,7 +829,7 @@
         return carry
 
     zero = jnp.zeros(carries.shape[1:], F32)
-    ends = lax.fori_loop(0, half // STEPS, late_steps, (zero, zero), unroll=2)
+    ends = lax.fori_loop(0, half // STEPS, late_steps, (zero, zero), unroll=3)
 
     def early(k, x):
         main, side = halves(x[:ny])

time: 25.8 us -> 25.8 us (level)
  no operation moved by 1% of the time
where the time goes in v11:
time: 25.8 us; the launch traced here: 25.6 us
  Pallas kernels  12.4 us (48%)
  starting transfers between devices  8.82 us (34%)
  waiting for transfers between devices  3.74 us (14%)
  between operations  0.68 us (3%)
    pallas_call x7, Pallas kernels, call(): pl.pallas_call(kernel, out_shape=[typed(x) for x in outs], in_specs=[spac...  12.4 us
    ppermute x3, starting transfers between devices, both_ways(): from_north = lax.ppermute(x, 'ty', ring('ty', -1))  5.14 us
    ppermute x2, starting transfers between devices, swap(): lax.ppermute(x, 'tx', [(i, (i + 1) % nx if i % 2 == phase else (i - 1) %...  3.68 us
    ppermute x2, waiting for transfers between devices, swap(): lax.ppermute(x, 'tx', [(i, (i + 1) % nx if i % 2 == phase else (i - 1) %...  2.2 us
    ppermute x3, waiting for transfers between devices, both_ways(): from_north = lax.ppermute(x, 'ty', ring('ty', -1))  1.54 us
  transfers between devices with their start and end apart: 5, of which 3 were waited for; matrix products, arithmetic and copies ran while one was open for 0% of the time, Pallas kernels for 15%

profile of v11, /device:TPU:0, one launch (start us, length us, event | category | flops | bytes accessed | tf_op | source)
XLA Modules:
  0.0 25.6 jit_solution(14536655874034991243)
XLA Ops:
  0.6 2.0 %shard_map.113 = (f32[48,16,128]{2,1,0:T(8,128)S(1)}, bf16[48,16,128]{2,1,0:T(8,128)(2,1)S(1)}, bf16[48,16,128]{2,1,0:T(8,128)(2,1)S(1)}, bf16[48,16,128]{2,1,0:...) custom-call(f32[48,16,128]{2,1,0:T(8,128)} %args_0_.4, ...), custom_call_target="tpu_custom_call" | custom-call | tf_op jit(solution)/shard_map/pallas_call | solution.py:23
  2.6 3.0 %collective-permute-start = (f32[6,8,128]{2,1,0:T(8,128)S(1)}, f32[6,8,128]{2,1,0:T(8,128)S(1)}, u32[]{:S(2)}, u32[]{:S(2)}) collective-permute-start(f32[6,8,128]{2,1,0:T(8,128)S(1)} %get-tuple-element.58), channel_id=1, source_target_pairs={{0,16},{16,0},{1,17},{17,1},{2,18},{18,2},{3,19},{19,3},{4,20},{20... | collective-permute-start | bytes 73736 | tf_op jit(solution)/shard_map/ppermute | solution.py:890
  5.6 1.4 %shard_map.114 = (f32[20,16,128]{2,1,0:T(8,128)S(1)}, f32[49,8,128]{2,1,0:T(8,128)S(1)}) custom-call(f32[48,16,128]{2,1,0:T(8,128)S(1)} %get-tuple-element.47.s, bf16[48,16,128]{2,1,0:T(8,128)(2,1)S(1)} %get-tuple-element.48.es, bf16[48,16,128]{2,1,0:T(8,128)(2,1)S(1)} %get-tuple-element.49.ns, bf16[48,16,128]{2,1,0:T(8,128)(2,1)S(1)} %get-tuple-element.50.mix, ...), custom_call_target="tpu_custom_call" | custom-call | tf_op jit(solution)/shard_map/pallas_call | solution.py:23
  7.1 0.1 collective-permute-start.3
  7.2 0.3 %collective-permute-done.corners_n.corners_s = f32[6,8,128]{2,1,0:T(8,128)S(1)} collective-permute-done((f32[6,8,128]{2,1,0:T(8,128)S(1)}, f32[6,8,128]{2,1,0:T(8,128)S(1)}, u32[]{:S(2)}, u32[]{:S(2)}) %collective-permute-start) | collective-permute-done | bytes 24608 | tf_op jit(solution)/shard_map/ppermute | solution.py:890
  7.4 0.1 shard_map.115
  7.6 3.7 %collective-permute-start.2 = (f32[184,128]{1,0:T(8,128)S(1)}, f32[184,128]{1,0:T(8,128)S(1)}, u32[]{:S(2)}, u32[]{:S(2)}) collective-permute-start(f32[184,128]{1,0:T(8,128)S(1)} %get-tuple-element.67), channel_id=1, source_target_pairs={{0,15},{1,2},{2,1},{3,4},{4,3},{5,6},{6,5},{7,8},{8,7},{9,10},{10,... | collective-permute-start | bytes 282632 | tf_op jit(solution)/shard_map/ppermute | solution.py:898
  11.2 0.0 collective-permute-start.1
  11.3 0.9 %shard_map.116 = (f32[48,16,128]{2,1,0:T(8,128)S(1)}, f32[48,16,128]{2,1,0:T(8,128)S(1)}, f32[48,16,128]{2,1,0:T(8,128)S(1)}, f32[48,16,128]{2,1,0:T(8,128)S(1)}...) custom-call(f32[48,16,128]{2,1,0:T(8,128)S(1)} %get-tuple-element.47, ...), custom_call_target="tpu_custom_call" | custom-call | flops 1000000000 | tf_op jit(solution)/shard_map/pallas_call | solution.py:23
  12.1 2.2 %collective-permute-done.2.from_two = f32[184,128]{1,0:T(8,128)S(1)} collective-permute-done((f32[184,128]{1,0:T(8,128)S(1)}, f32[184,128]{1,0:T(8,128)S(1)}, u32[]{:S(2)}, u32[]{:S(2)}) %collective-permute-start.2) | collective-permute-done | bytes 94240 | tf_op jit(solution)/shard_map/ppermute | solution.py:898
  14.3 0.0 collective-permute-done.1.from_one
  14.3 0.0 collective-permute-done.3.rows_n.rows_s
  14.3 4.4 %shard_map.117 = (f32[48,32,128]{2,1,0:T(8,128)S(1)}, f32[48,32,128]{2,1,0:T(8,128)S(1)}, f32[48,32,128]{2,1,0:T(8,128)S(1)}, f32[48,32,128]{2,1,0:T(8,128)S(1)}...) custom-call(f32[48,16,128]{2,1,0:T(8,128)S(1)} %get-tuple-element.47, ...), custom_call_target="tpu_custom_call" | custom-call | tf_op jit(solution)/shard_map/pallas_call | solution.py:23
  18.8 2.0 %collective-permute-start.4 = (f32[25,8,128]{2,1,0:T(8,128)S(1)}, f32[25,8,128]{2,1,0:T(8,128)S(1)}, u32[]{:S(2)}, u32[]{:S(2)}) collective-permute-start(f32[25,8,128]{2,1,0:T(8,128)S(1)} %get-tuple-element.91), channel_id=1, source_target_pairs={{0,16},{16,0},{1,17},{17,1},{2,18},{18,2},{3,19},{19,3},{4,20},{20... | collective-permute-start | bytes 307208 | tf_op jit(solution)/shard_map/ppermute | solution.py:890
  20.8 1.4 %shard_map.118 = (f32[48,16,256]{2,1,0:T(8,128)S(1)}, f32[48,16,128]{2,1,0:T(8,128)S(1)}, f32[48,16,128]{2,1,0:T(8,128)S(1)}, f32[48,16,128]{2,1,0:T(8,128)S(1)}) custom-call(f32[48,16,128]{2,1,0:T(8,128)S(1)} %get-tuple-element.60.ep, f32[48,16,128]{2,1,0:T(8,128)S(1)} %get-tuple-element.61.em, f32[48,16,128]{2,1,0:T(8,128)S(1)} %get-tuple-element.62.np_, ...), custom_call_target="tpu_custom_call" | custom-call | bytes 8388608 | tf_op jit(solution)/shard_map/pallas_call | solution.py:23
  22.2 1.2 %collective-permute-done.4.rows_n.rows_s = f32[25,8,128]{2,1,0:T(8,128)S(1)} collective-permute-done((f32[25,8,128]{2,1,0:T(8,128)S(1)}, f32[25,8,128]{2,1,0:T(8,128)S(1)}, u32[]{:S(2)}, u32[]{:S(2)}) %collective-permute-start.4) | collective-permute-done | bytes 102432 | tf_op jit(solution)/shard_map/ppermute | solution.py:890
  23.4 2.2 %shard_map.119 = (f32[48,16,128]{2,1,0:T(8,128)}, f32[48,16,128]{2,1,0:T(8,128)}) custom-call(f32[48,16,128]{2,1,0:T(8,128)S(1)} %get-tuple-element.60.ep, f32[48,16,128]{2,1,0:T(8,128)S(1)} %get-tuple-element.61.em, f32[48,16,128]{2,1,0:T(8,128)S(1)} %get-tuple-element.62.np_, f32[48,16,128]{2,1,0:T(8,128)S(1)} %get-tuple-element.63.nm, ...), custom_call_target="tpu_custom_call" | custom-call | tf_op jit(solution)/shard_map/pallas_call | solution.py:23
Async XLA Ops:
  2.6 4.8 %collective-permute-start = (f32[6,8,128]{2,1,0:T(8,128)S(1)}, f32[6,8,128]{2,1,0:T(8,128)S(1)}, u32[]{:S(2)}, u32[]{:S(2)}) collective-permute-start(f32[6,8,128]{2,1,0:T(8,128)S(1)} %get-tuple-element.58), channel_id=1, source_target_pairs={{0,16},{16,0},{1,17},{17,1},{2,18},{18,2},{3,19},{19,3},{4,20},{20... | collective-permute-start | bytes 73736 | tf_op jit(solution)/shard_map/ppermute | solution.py:890
  7.1 7.3 %collective-permute-start.3 = (f32[49,8,128]{2,1,0:T(8,128)S(1)}, f32[49,8,128]{2,1,0:T(8,128)S(1)}, u32[]{:S(2)}, u32[]{:S(2)}) collective-permute-start(f32[49,8,128]{2,1,0:T(8,128)S(1)} %get-tuple-element.69), channel_id=1, source_target_pairs={{0,16},{16,0},{1,17},{17,1},{2,18},{18,2},{3,19},{19,3},{4,20},{20... | collective-permute-start | bytes 602120 | tf_op jit(solution)/shard_map/ppermute | solution.py:890
  7.6 6.8 %collective-permute-start.2 = (f32[184,128]{1,0:T(8,128)S(1)}, f32[184,128]{1,0:T(8,128)S(1)}, u32[]{:S(2)}, u32[]{:S(2)}) collective-permute-start(f32[184,128]{1,0:T(8,128)S(1)} %get-tuple-element.67), channel_id=1, source_target_pairs={{0,15},{1,2},{2,1},{3,4},{4,3},{5,6},{6,5},{7,8},{8,7},{9,10},{10,... | collective-permute-start | bytes 282632 | tf_op jit(solution)/shard_map/ppermute | solution.py:898
  11.2 3.1 %collective-permute-start.1 = (f32[184,128]{1,0:T(8,128)S(1)}, f32[184,128]{1,0:T(8,128)S(1)}, u32[]{:S(2)}, u32[]{:S(2)}) collective-permute-start(f32[184,128]{1,0:T(8,128)S(1)} %get-tuple-element.59.after), channel_id=1, source_target_pairs={{0,1},{1,0},{2,3},{3,2},{4,5},{5,4},{6,7},{7,6},{8,9},{9,8},{10,11... | collective-permute-start | bytes 282632 | tf_op jit(solution)/shard_map/ppermute | solution.py:898
  18.8 4.7 %collective-permute-start.4 = (f32[25,8,128]{2,1,0:T(8,128)S(1)}, f32[25,8,128]{2,1,0:T(8,128)S(1)}, u32[]{:S(2)}, u32[]{:S(2)}) collective-permute-start(f32[25,8,128]{2,1,0:T(8,128)S(1)} %get-tuple-element.91), channel_id=1, source_target_pairs={{0,16},{16,0},{1,17},{17,1},{2,18},{18,2},{3,19},{19,3},{4,20},{20... | collective-permute-start | bytes 307208 | tf_op jit(solution)/shard_map/ppermute | solution.py:890
